TPU v7x, 32 devices: a whole 2x2x4 slice. The times are simulated.
32 devices in a mesh: dp: 8 (over z, y), mp: 4 (over x, core).
Axes of the slice: x: 2, y: 2, z: 4, core: 2. Of those that a mesh axis runs over, the one named last changes fastest.
Arguments:
- block_input: float32 [25088, 768], P(('dp', 'mp')), may hold values from -6 to 6
- cotangent: float32 [25088, 768], P(('dp', 'mp')), may hold values from -6 to 6
- image_size: int32 [128, 2], P('dp'), may hold values from 7 to 14, as said below
- attention_weights: float32 [4, 768, 768], P(None, 'dp', 'mp')
- attention_first: float32 [4, 768, 768], P(None, 'dp', 'mp'), may hold values from -112 to 112
- attention_second: float32 [4, 768, 768], P(None, 'dp', 'mp'), may hold values from 12.544 to 200.704
- mlp_weights: float32 [2, 768, 3072], P(None, 'dp', 'mp')
- mlp_first: float32 [2, 768, 3072], P(None, 'dp', 'mp'), may hold values from -112 to 112
- mlp_second: float32 [2, 768, 3072], P(None, 'dp', 'mp'), may hold values from 12.544 to 200.704
- head_params: float32 [12, 857], P('mp')
- head_first: float32 [12, 857], P('mp'), may hold values from -112 to 112
- head_second: float32 [12, 857], P('mp'), may hold values from 12.544 to 200.704
- norm_params: float32 [12, 768], replicated, as said below
- norm_first: float32 [12, 768], replicated, may hold values from -112 to 112
- norm_second: float32 [12, 768], replicated, may hold values from 12.544 to 200.704
Outputs:
- block_output: float32 [25088, 768], P(('dp', 'mp'))
- input_grad: float32 [25088, 768], P(('dp', 'mp'))
- attention_grad: float32 [4, 768, 768], P(None, 'dp', 'mp')
- attention_second_new: float32 [4, 768, 768], P(None, 'dp', 'mp')
- attention_new: float32 [4, 768, 768], P(None, 'dp', 'mp')
- mlp_grad: float32 [2, 768, 3072], P(None, 'dp', 'mp')
- mlp_second_new: float32 [2, 768, 3072], P(None, 'dp', 'mp')
- mlp_new: float32 [2, 768, 3072], P(None, 'dp', 'mp')
- head_grad: float32 [12, 857], P('mp')
- head_second_new: float32 [12, 857], P('mp')
- head_new: float32 [12, 857], P('mp')
- norm_grad: float32 [12, 768], replicated
- norm_second_new: float32 [12, 768], replicated
- norm_new: float32 [12, 768], replicated
Inputs may be any that keep to these rules, and one draw needn't show every extreme that they name: `image_size`: column 0 holds heights, column 1 widths, in patches of a 14 x 14 grid; the first image fills the grid and the second is the smallest. `norm_params`: rows 0, 2, 5 and 7 are positive.
All inputs are finite; a program needn't handle non-finite values.
Results may differ from a plain program's by a relative error of at most 0.017.
Values may be sent and summed in bfloat16 or wider, within the bound.
No kernel may reach another device: no remote copies, remote signals or barrier semaphores. Data moves between devices by JAX's collectives and lax.ppermute only.
A program may use at most 256 MiB of HBM per device.

v0:
```python
import jax
import jax.numpy as jnp
from jax import lax
from jax.sharding import PartitionSpec as P

HD = 64
GRID = 14
STEP = 10
PATCHES = 196


EPSILON = 1e-06
NEGATIVE = -1e30
BETA_ONE = 0.9
BETA_TWO = 0.999
ADAM_EPSILON = 1e-08
RATE_MATRIX = 0.05
RATE_VECTOR = 0.4
DECAY_MATRIX = 0.05
HIGHEST = lax.Precision.HIGHEST


def layer_norm(values, norm_gain, norm_shift):
    row_mean = jnp.mean(values, axis=-1, keepdims=True)
    centre = values - row_mean
    variance = jnp.mean(centre * centre, axis=-1, keepdims=True)
    inverse = lax.rsqrt(variance + EPSILON)
    scaled = centre * inverse
    return (scaled * norm_gain + norm_shift, scaled, inverse)


def norm_back(incoming, norm_gain, scaled, inverse):
    weighted = incoming * norm_gain
    centred = weighted - jnp.mean(weighted, axis=-1, keepdims=True)
    return inverse * (centred - scaled * jnp.mean(weighted * scaled, axis=-1, keepdims=True))


def offsets_table(grid):
    span_size = 2 * grid - 1
    row_from = jnp.arange(grid, dtype=jnp.int32)[:, None, None]
    row_to = jnp.arange(grid, dtype=jnp.int32)[None, :, None]
    offset_slot = jnp.arange(span_size, dtype=jnp.int32)[None, None, :]
    return (row_from - row_to + grid - 1 == offset_slot).astype(jnp.float32)


def table_bias(table, grid):
    heads_count = table.shape[0]
    span_size = 2 * grid - 1
    onehot = offsets_table(grid)
    table_cube = table.reshape(heads_count, span_size, span_size)
    spread = jnp.einsum("hrs,abr,cds->hacbd", table_cube, onehot, onehot, precision=HIGHEST)
    return spread.reshape(heads_count, grid * grid, grid * grid)


def table_grad(pair_grads, grid):
    heads_count = pair_grads.shape[0]
    onehot = offsets_table(grid)
    table_cube = pair_grads.reshape(heads_count, grid, grid, grid, grid)
    return jnp.einsum("hacbd,abr,cds->hrs", table_cube, onehot, onehot, precision=HIGHEST).reshape(
        heads_count, -1
    )


def valid_keys(image_dims, grid):
    position = jnp.arange(grid * grid, dtype=jnp.int32)
    return ((position // grid)[None, :] < image_dims[:, 0:1]) & (
        (position % grid)[None, :] < image_dims[:, 1:2]
    )


def group_size(images, patches):
    upper_bound = max(1, 1024 // patches)
    return max(
        [
            divisor
            for divisor in range(1, images + 1)
            if images % divisor == 0 and divisor <= upper_bound
        ]
    )


def masked_scores(queries, key_rows, key_mask, pair_bias):
    scores = (
        jnp.einsum("iqhd,ikhd->ihqk", queries, key_rows, preferred_element_type=jnp.float32)
        + pair_bias[None]
    )
    return jnp.where(key_mask[:, None, None, :], scores, NEGATIVE)


def attend_block(block_item, pair_bias):
    queries, key_rows, values, key_mask = block_item
    scores = masked_scores(queries, key_rows, key_mask, pair_bias)
    row_max = jnp.max(scores, axis=-1, keepdims=True)
    exponent = jnp.exp(scores - row_max)
    row_total = jnp.sum(exponent, axis=-1, keepdims=True)
    softmax = (exponent / row_total).astype(jnp.bfloat16)
    context = jnp.einsum("ihqk,ikhd->iqhd", softmax, values, preferred_element_type=jnp.float32)
    return (context.astype(jnp.bfloat16), (row_max + jnp.log(row_total))[..., 0])


def attend_back(block_item, pair_bias):
    queries, key_rows, values, key_mask, logsum, grad_context = block_item
    scores = masked_scores(queries, key_rows, key_mask, pair_bias)
    softmax = jnp.exp(scores - logsum[..., None])
    grad_probs = jnp.einsum(
        "iqhd,ikhd->ihqk", grad_context, values, preferred_element_type=jnp.float32
    )
    dot_rows = jnp.sum(grad_probs * softmax, axis=-1, keepdims=True)
    grad_scores = (softmax * (grad_probs - dot_rows)).astype(jnp.bfloat16)
    grad_queries = jnp.einsum(
        "ihqk,ikhd->iqhd", grad_scores, key_rows, preferred_element_type=jnp.float32
    )
    grad_keys = jnp.einsum(
        "ihqk,iqhd->ikhd", grad_scores, queries, preferred_element_type=jnp.float32
    )
    grad_values = jnp.einsum(
        "ihqk,iqhd->ikhd",
        softmax.astype(jnp.bfloat16),
        grad_context,
        preferred_element_type=jnp.float32,
    )
    return (grad_queries, grad_keys, grad_values, jnp.sum(grad_scores.astype(jnp.float32), axis=0))


def adam(weight, moment_one, moment_two, incoming, step_rate, decay_rate):
    first_new = BETA_ONE * moment_one + (1.0 - BETA_ONE) * incoming
    second_new = BETA_TWO * moment_two + (1.0 - BETA_TWO) * incoming * incoming
    update = (
        first_new
        / (1.0 - BETA_ONE**STEP)
        / (jnp.sqrt(second_new / (1.0 - BETA_TWO**STEP)) + ADAM_EPSILON)
    )
    return (second_new, weight * (1.0 - step_rate * decay_rate) - step_rate * update)


def contract_rows(former, latter):
    return lax.dot_general(
        former, latter, (((0,), (0,)), ((), ())), preferred_element_type=jnp.float32
    )


def contract_cols(former, latter):
    return lax.dot_general(
        former, latter, (((1,), (1,)), ((), ())), preferred_element_type=jnp.float32
    )


def shards(
    block_input,
    cotangent,
    image_size,
    attention_weights,
    attention_first,
    attention_second,
    mlp_weights,
    mlp_first,
    mlp_second,
    head_params,
    head_first,
    head_second,
    norm_params,
    norm_first,
    norm_second,
):
    low_type = jnp.bfloat16
    full_type = jnp.float32
    lane_count = lax.axis_size("mp")
    lane_index = lax.axis_index("mp")
    local_rows, width = block_input.shape
    attention, mlp = (
        lax.all_gather(attention_weights.astype(low_type), "dp", axis=1, tiled=True),
        lax.all_gather(mlp_weights.astype(low_type), "dp", axis=1, tiled=True),
    )
    unit_bias_all = norm_params[8:].reshape(-1)
    attention, mlp = (
        lax.all_gather(attention, "mp", axis=2, tiled=True),
        lax.all_gather(mlp, "mp", axis=2, tiled=True),
    )
    head_table = lax.all_gather(head_params, "mp", axis=0, tiled=True)
    per_lane = image_size.shape[0] // lane_count
    image_dims = lax.dynamic_slice_in_dim(image_size, lane_index * per_lane, per_lane, 0)

    def unchanged(values):
        return values

    def entire(terms):
        return terms(0, local_rows)

    share_attention = share_mlp = share_down_grad = share_attended_grad = unchanged
    sum_attention = sum_mlp = sum_mlp_grad = sum_attention_grad = entire
    place_units = place_heads = unchanged
    heads_count = head_table.shape[0]
    columns = heads_count * HD
    query_scale = HD ** (-0.5)
    normed_one, scaled_one, inverse_one = layer_norm(block_input, norm_params[0], norm_params[1])
    rows_one = share_attention(normed_one.astype(low_type))
    total_rows = rows_one.shape[0]
    images = total_rows // PATCHES
    projected = jnp.einsum("td,kdc->ktc", rows_one, attention[:3], preferred_element_type=full_type)
    queries = ((projected[0] + head_table[:, :HD].reshape(columns)) * query_scale).astype(low_type)
    key_rows = projected[1].astype(low_type)
    values = (projected[2] + head_table[:, HD : 2 * HD].reshape(columns)).astype(low_type)
    pair_bias = table_bias(head_table[:, 2 * HD :], GRID)
    key_mask = valid_keys(image_dims, GRID)
    per_group = group_size(images, PATCHES)
    groups = images // per_group
    block_shape = (groups, per_group, PATCHES, heads_count, HD)
    pieces = (
        queries.reshape(block_shape),
        key_rows.reshape(block_shape),
        values.reshape(block_shape),
        key_mask.reshape(groups, per_group, PATCHES),
    )
    context, logsum = lax.map(lambda block_item: attend_block(block_item, pair_bias), pieces)
    context = context.reshape(total_rows, columns)
    out_weight = attention[3]

    def attention_terms(row_start, row_count):
        return contract_cols(context, out_weight)

    attended = sum_attention(attention_terms) + norm_params[4]
    middle = block_input + norm_params[5] * attended
    normed_two, scaled_two, inverse_two = layer_norm(middle, norm_params[2], norm_params[3])
    rows_two = share_mlp(normed_two.astype(low_type))
    up_weight = mlp[0]
    down_weight = mlp[1]
    hidden = jnp.dot(rows_two, up_weight, preferred_element_type=full_type) + unit_bias_all
    active, gelu_back = jax.vjp(lambda inputs: jax.nn.gelu(inputs, approximate=False), hidden)
    active_low = active.astype(low_type)

    def mlp_terms(row_start, row_count):
        return contract_cols(active_low, down_weight)

    down_out = sum_mlp(mlp_terms) + norm_params[6]
    output = middle + norm_params[7] * down_out
    grad_down = (cotangent * norm_params[7]).astype(low_type)
    rows_down = share_down_grad(grad_down)
    grad_down_weight = contract_rows(rows_down, active_low)
    grad_active = jnp.dot(rows_down, down_weight, preferred_element_type=full_type)
    grad_hidden = gelu_back(grad_active)[0].astype(low_type)
    grad_up_weight = contract_rows(rows_two, grad_hidden)

    def mlp_back_terms(row_start, row_count):
        return contract_cols(grad_hidden, up_weight)

    grad_normed_two = sum_mlp_grad(mlp_back_terms)
    grad_middle = cotangent + norm_back(grad_normed_two, norm_params[2], scaled_two, inverse_two)
    grad_attended = (grad_middle * norm_params[5]).astype(low_type)
    rows_attended = share_attended_grad(grad_attended)
    grad_out_weight = contract_rows(rows_attended, context)
    grad_context = jnp.dot(rows_attended, out_weight, preferred_element_type=full_type).astype(
        low_type
    )
    back_pieces = pieces + (logsum, grad_context.reshape(block_shape))
    grad_queries, grad_keys, grad_values, pair_grads = lax.map(
        lambda block_item: attend_back(block_item, pair_bias), back_pieces
    )
    grad_qkv = jnp.stack(
        [
            (grad_queries * query_scale).reshape(total_rows, columns),
            grad_keys.reshape(total_rows, columns),
            grad_values.reshape(total_rows, columns),
        ]
    ).astype(low_type)
    grad_projection = jnp.einsum(
        "td,ktc->kdc", rows_one, grad_qkv, preferred_element_type=full_type
    )

    def attention_back_terms(row_start, row_count):
        return jnp.einsum("ktc,kdc->td", grad_qkv, attention[:3], preferred_element_type=full_type)

    grad_normed_one = sum_attention_grad(attention_back_terms)
    grad_input = grad_middle + norm_back(grad_normed_one, norm_params[0], scaled_one, inverse_one)
    grad_heads = jnp.concatenate(
        [
            jnp.sum(grad_qkv[0].astype(full_type), axis=0).reshape(heads_count, HD),
            jnp.sum(grad_qkv[2].astype(full_type), axis=0).reshape(heads_count, HD),
            table_grad(jnp.sum(pair_grads, axis=0), GRID),
        ],
        axis=1,
    )
    grad_units = jnp.sum(grad_hidden.astype(full_type), axis=0)
    vector_rows = jnp.stack(
        [
            jnp.sum(grad_normed_one * scaled_one, axis=0),
            jnp.sum(grad_normed_one, axis=0),
            jnp.sum(grad_normed_two * scaled_two, axis=0),
            jnp.sum(grad_normed_two, axis=0),
            jnp.sum(grad_middle, axis=0) * norm_params[5],
            jnp.sum(grad_middle * attended, axis=0),
            jnp.sum(cotangent, axis=0) * norm_params[7],
            jnp.sum(cotangent * down_out, axis=0),
        ]
    )
    grad_norms = jnp.concatenate([vector_rows, place_units(grad_units).reshape(-1, width)], axis=0)
    reduced_norms, reduced_heads_all = lax.psum((grad_norms, place_heads(grad_heads)), ("dp", "mp"))
    local_heads = head_params.shape[0]
    reduced_heads = lax.dynamic_slice_in_dim(
        reduced_heads_all, lane_index * local_heads, local_heads, 0
    )
    grad_attention = jnp.concatenate([grad_projection, grad_out_weight[None]], axis=0)
    grad_mlp = jnp.stack([grad_up_weight, grad_down_weight])
    grad_attention, grad_mlp = (
        lax.psum_scatter(
            grad_attention.astype(jnp.bfloat16), "mp", scatter_dimension=2, tiled=True
        ).astype(jnp.float32),
        lax.psum_scatter(
            grad_mlp.astype(jnp.bfloat16), "mp", scatter_dimension=2, tiled=True
        ).astype(jnp.float32),
    )
    reduced_attention, reduced_mlp = (
        lax.psum_scatter(grad_attention, "dp", scatter_dimension=1, tiled=True),
        lax.psum_scatter(grad_mlp, "dp", scatter_dimension=1, tiled=True),
    )
    attention_second_new, attention_new = adam(
        attention_weights,
        attention_first,
        attention_second,
        reduced_attention,
        RATE_MATRIX,
        DECAY_MATRIX,
    )
    mlp_second_new, mlp_new = adam(
        mlp_weights, mlp_first, mlp_second, reduced_mlp, RATE_MATRIX, DECAY_MATRIX
    )
    head_second_new, head_new = adam(
        head_params, head_first, head_second, reduced_heads, RATE_VECTOR, 0.0
    )
    norm_second_new, norm_new = adam(
        norm_params, norm_first, norm_second, reduced_norms, RATE_VECTOR, 0.0
    )
    return (
        output,
        grad_input,
        reduced_attention,
        attention_second_new,
        attention_new,
        reduced_mlp,
        mlp_second_new,
        mlp_new,
        reduced_heads,
        head_second_new,
        head_new,
        reduced_norms,
        norm_second_new,
        norm_new,
    )


def solution(mesh):
    placed = (
        P(("dp", "mp"), None),
        P(("dp", "mp"), None),
        P("dp", None),
        P(None, "dp", "mp"),
        P(None, "dp", "mp"),
        P(None, "dp", "mp"),
        P(None, "dp", "mp"),
        P(None, "dp", "mp"),
        P(None, "dp", "mp"),
        P("mp", None),
        P("mp", None),
        P("mp", None),
        P(),
        P(),
        P(),
    )
    return jax.shard_map(
        shards,
        mesh=mesh,
        in_specs=placed,
        out_specs=(
            P(("dp", "mp"), None),
            P(("dp", "mp"), None),
            P(None, "dp", "mp"),
            P(None, "dp", "mp"),
            P(None, "dp", "mp"),
            P(None, "dp", "mp"),
            P(None, "dp", "mp"),
            P(None, "dp", "mp"),
            P("mp", None),
            P("mp", None),
            P("mp", None),
            P(),
            P(),
            P(),
        ),
        check_vma=False,
    )
```

profile of v0, /device:TPU:0, one launch (start us, length us, event | category | flops | bytes accessed | tf_op | source)
XLA Modules:
  0.0 830.3 jit_solution(1015885214162530447)
XLA Ops:
  11.1 46.6 %all-gather.6.cloned.1.call-done = bf16[4,768,192]{2,0,1:T(4,128)(2,1)} async-done(((bf16[4,96,192]{2,0,1:T(4,128)(2,1)}), bf16[4,768,192]{2,0,1:T(4,128)(2,1)}) %all-gather.6.cloned.1.call-update) | async-done | bytes 1179664 | tf_op jit(solution)/shard_map/all_gather | solution.py:171
  61.9 49.5 %all-gather.10.cloned.1.call-done = bf16[2,768,768]{2,1,0:T(8,128)(2,1)} async-done(((bf16[2,96,768]{2,1,0:T(8,128)(2,1)}), bf16[2,768,768]{2,1,0:T(8,128)(2,1)}) %all-gather.10.cloned.1.call-update) | async-done | bytes 2359312 | tf_op jit(solution)/shard_map/all_gather | solution.py:172
  117.7 10.9 %convolution_bitcast_fusion = f32[12,14,14,14,14]{4,3,2,0,1:T(8,128)} fusion(f32[14,14,12,27,1]{3,1,4,2,0:T(8,128)S(1)} %convolution_bitcast_fusion.3, s32[14,14]{1,0:T(8,128)S(1)} %subtract_add_fusion), kind=kOutput, calls=%fused_computation.27 | convolution fusion | flops 149366704 | bytes 2098768 | tf_op jit(solution)/shard_map/hrs,abr,cds->hacbd/dot_general | solution.py:51
  128.7 27.3 %copy.196 = f32[12,14,14,14,14]{2,1,4,3,0:T(8,128)} copy(f32[12,14,14,14,14]{4,3,2,0,1:T(8,128)} %convolution_bitcast_fusion) | data formatting | bytes 3687936 | tf_op jit(solution)/shard_map/while/body/eval_jaxpr/add | solution.py:84
  156.0 14.2 %reshape.203 = f32[12,196,196]{1,2,0:T(8,128)} reshape(f32[12,14,14,14,14]{2,1,4,3,0:T(8,128)} %copy.196) | data formatting | bytes 3687936 | tf_op jit(solution)/shard_map/while/body/eval_jaxpr/add | solution.py:84
  171.8 8.1 copy.207
  247.7 6.4 copy.208
  260.5 28.5 %multiply_convert_fusion.1 = (bf16[784,3072]{1,0:T(8,128)(2,1)}, f32[784,3072]{1,0:T(8,128)}, f32[784,3072]{1,0:T(8,128)}) fusion(f32[3072]{0:T(1024)S(1)} %add.246, bf16[2,768,3072]{2,1,0:T(8,128)(2,1)} %all-gather.12.cloned.1.call-done, f32[784,768]{1,0:T(8,128)} %copy-done.12, f32[768]{0:T(1024)S(1)} %get-tuple-element.157, ...), kind=kOutput, calls=%fused_computation.11 | convolution fusion | flops 3861344256 | bytes 31236224 | tf_op jit(solution)/shard_map/dot_general | solution.py:227
  289.0 12.8 %convert_reduce_fusion.1 = (f32[3072]{0:T(1024)S(1)}, bf16[784,3072]{1,0:T(8,128)(2,1)}) fusion(f32[784,3072]{1,0:T(8,128)} %get-tuple-element.177, bf16[2,768,3072]{2,1,0:T(8,128)(2,1)S(1)} %copy-done.48, f32[784,768]{1,0:T(8,128)S(1)} %copy-done.49, f32[768]{0:T(1024)S(1)} %get-tuple-element.156, f32[784,3072]{1,0:T(8,128)} %get-tuple-element.197, ...), kind=kOutput, calls=%fused_computation.9 | convolution fusion | flops 3741520896 | bytes 31240192 | tf_op jit(solution)/shard_map/dot_general | solution.py:239
  301.8 8.3 %multiply_reduce_fusion.3 = (f32[768]{0:T(1024)S(1)}, f32[784]{0:T(1024)S(1)}, f32[784]{0:T(1024)S(1)}, f32[768]{0:T(1024)S(1)}, f32[784,768]{1,0:T(8,128)}) fusion(f32[784,768]{1,0:T(8,128)S(1)} %copy-done.13, f32[784]{0:T(1024)S(1)} %add_rsqrt_fusion, f32[784]{0:T(1024)S(1)} %broadcast_multiply_fusion.4, f32[768]{0:T(1024)S(1)} %get-tuple-element.158, ...), kind=kOutput, calls=%fused_computation.58 | convolution fusion | flops 3704792064 | bytes 14377088 | tf_op jit(solution)/shard_map/dot_general | solution.py:143
  310.2 10.2 %multiply_reduce_fusion.1 = (f32[768]{0:T(1024)S(1)}, f32[768]{0:T(1024)S(1)}, f32[784,768]{1,0:T(8,128)}, f32[768]{0:T(1024)S(1)}, f32[768]{0:T(1024)S(1)}, /*index=5*/f32[784,768]{1,0:T(8,128)S(1)}) fusion(f32[784,768]{1,0:T(8,128)} %param.16, f32[768]{0:T(1024)S(1)} %copy-done.47, f32[784,768]{1,0:T(8,128)S(1)} %copy-done.13, ...), kind=kOutput, calls=%fused_computation.56 | convolution fusion | flops 3710211072 | bytes 24031232 | tf_op jit(solution)/shard_map/dot_general | solution.py:143
  331.5 6.8 fusion.24
  338.4 6.9 multiply_reduce_fusion
  390.1 9.6 %fusion.13 = bf16[1,768,3072]{2,1,0:T(8,128)(2,1)} fusion(bf16[784,3072]{1,0:T(8,128)(2,1)} %get-tuple-element.176, f32[784,768]{1,0:T(8,128)} %param.16, f32[768]{0:T(1024)S(1)} %get-tuple-element.156), kind=kOutput, calls=%fused_computation.38 | convolution fusion | flops 3702939648 | bytes 11947008 | tf_op jit(solution)/shard_map/dot_general | solution.py:137
  399.7 9.6 %fusion.12 = bf16[1,768,3072]{2,1,0:T(8,128)(2,1)} fusion(bf16[784,3072]{1,0:T(8,128)(2,1)} %get-tuple-element.203, f32[784,768]{1,0:T(8,128)S(1)} %copy-done.14, f32[768]{0:T(1024)S(1)} %get-tuple-element.157, f32[768]{0:T(1024)S(1)} %get-tuple-element.158, f32[784]{0:T(1024)S(1)} %add_rsqrt_fusion, f32[784]{0:T(1024)S(1)} %broadcast_multiply_fusion.4), kind=kOutput, calls=%fused_computation.37 | convolution fusion | flops 3704745984 | bytes 11956352 | tf_op jit(solution)/shard_map/dot_general | solution.py:137
  409.3 8.2 pad_maximum_fusion
  417.6 12.9 %reshape.189 = f32[12,14,14,14,14]{2,1,4,3,0:T(8,128)} reshape(f32[12,196,196]{1,2,0:T(8,128)} %get-tuple-element.172) | data formatting | bytes 3687936 | tf_op jit(solution)/shard_map/reshape | solution.py:58
  430.4 30.4 %copy.182 = f32[12,14,14,14,14]{3,4,1,2,0:T(8,128)} copy(f32[12,14,14,14,14]{2,1,4,3,0:T(8,128)} %reshape.189) | data formatting | bytes 3687936 | tf_op jit(solution)/shard_map/reshape | solution.py:58
  460.8 16.7 %convolution_bitcast_fusion.2 = f32[27,12,14,14]{0,3,2,1:T(8,128)S(1)} fusion(f32[12,14,14,14,14]{3,4,1,2,0:T(8,128)} %copy.182, s32[14,14]{1,0:T(8,128)S(1)} %copy-done.29), kind=kOutput, calls=%fused_computation.85 | convolution fusion | flops 149366704 | bytes 2098768 | tf_op jit(solution)/shard_map/hacbd,abr,cds->hrs/dot_general | solution.py:59
  482.4 7.9 fusion.18
  501.3 16.6 %reduce-scatter.9.cloned.1.call-done = bf16[2,768,768]{2,1,0:T(8,128)(2,1)} async-done(((bf16[2,768,3072]{2,1,0:T(8,128)(2,1)}), bf16[2,768,768]{2,1,0:T(8,128)(2,1)}) %reduce-scatter.9.cloned.1.call-update) | async-done | bytes 2359312 | tf_op jit(solution)/shard_map/reduce_scatter | solution.py:307
  530.4 116.3 %all-reduce.3.cloned.1.call-done = (f32[12,857]{1,0:T(8,128)}, f32[12,768]{1,0:T(8,128)}) async-done(((f32[12,857]{1,0:T(8,128)}, f32[12,768]{1,0:T(8,128)}), (f32[12,857]{1,0:T(8,128)}, f32[12,768]{1,0:T(8,128)})) %all-reduce.3.cloned.1.call-update) | async-done | bytes 78016 | tf_op jit(solution)/shard_map/psum | solution.py:296
  649.6 71.2 %reduce-scatter.13.cloned.1.call-done = f32[96,768]{1,0:T(8,128)} async-done(((f32[768,768]{1,0:T(8,128)}), f32[96,768]{1,0:T(8,128)}) %reduce-scatter.13.cloned.1.call-update) | async-done | bytes 294928
  725.3 94.5 %reduce-scatter.11.cloned.1.call-done = f32[2,96,768]{2,1,0:T(8,128)} async-done(((f32[2,768,768]{2,1,0:T(8,128)}), f32[2,96,768]{2,1,0:T(8,128)}) %reduce-scatter.11.cloned.1.call-update) | async-done | bytes 589840 | tf_op jit(solution)/shard_map/reduce_scatter | solution.py:313
  (225 shorter events, 184.8 us)
Async XLA Ops:
  7.2 163.3 %copy-start = (s32[16,2]{0,1:T(2,128)S(1)}, s32[16,2]{0,1:T(2,128)}, u32[]{:S(2)}) copy-start(s32[16,2]{0,1:T(2,128)} %param.17) | copy-start | bytes 388
  7.2 50.5 %all-gather.6.cloned.1.call-start = ((), (), s32[]{:S(2)}) async-start(), calls=%async_computation.4 | async-start | bytes 1769472 | tf_op jit(solution)/shard_map/all_gather | solution.py:171
  9.2 102.2 %all-gather.10.cloned.1.call-start = ((), (), s32[]{:S(2)}) async-start(), calls=%async_computation.6 | async-start | bytes 2654208 | tf_op jit(solution)/shard_map/all_gather | solution.py:172
  11.1 100.4 %copy-start.33 = (f32[3,857]{1,0:T(4,128)S(1)}, f32[3,857]{1,0:T(4,128)}, u32[]{:S(2)}) copy-start(f32[3,857]{1,0:T(4,128)} %param.24) | copy-start | bytes 30856
  11.1 160.7 %all-gather.8.cloned.1.call-start = ((), (), s32[]{:S(2)}) async-start(), calls=%async_computation.5 | async-start | bytes 5898240 | tf_op jit(solution)/shard_map/all_gather | solution.py:176
  61.8 198.6 %all-gather.12.cloned.1.call-start = ((), (), s32[]{:S(2)}) async-start(), calls=%async_computation.7 | async-start | bytes 11796480 | tf_op jit(solution)/shard_map/all_gather | solution.py:177
  111.4 381.1 %reduce-scatter.7.cloned.1.call-start = ((), (), s32[]{:S(2)}) async-start(), calls=%async_computation.8 | async-start | bytes 5898240 | tf_op jit(solution)/shard_map/reduce_scatter | solution.py:304
  156.0 14.5 %copy-start.31 = (f32[12,768]{1,0:T(8,128)S(1)}, f32[12,768]{1,0:T(8,128)}, u32[]{:S(2)}) copy-start(f32[12,768]{1,0:T(8,128)} %param.27) | copy-start | bytes 110596
  260.5 28.6 %copy-start.48 = (bf16[2,768,3072]{2,1,0:T(8,128)(2,1)S(1)}, bf16[2,768,3072]{2,1,0:T(8,128)(2,1)}, u32[]{:S(2)}) copy-start(bf16[2,768,3072]{2,1,0:T(8,128)(2,1)} %all-gather.12.cloned.1.call-done) | copy-start | bytes 28311556
  260.5 28.5 %copy-start.49 = (f32[784,768]{1,0:T(8,128)S(1)}, f32[784,768]{1,0:T(8,128)}, u32[]{:S(2)}) copy-start(f32[784,768]{1,0:T(8,128)} %param.16) | copy-start | bytes 7225348
  390.1 127.8 %reduce-scatter.9.cloned.1.call-start = ((), (), s32[]{:S(2)}) async-start(), calls=%async_computation.9 | async-start | bytes 11796480 | tf_op jit(solution)/shard_map/reduce_scatter | solution.py:307
  417.5 229.1 %all-reduce.3.cloned.1.call-start = ((), (), s32[]{:S(2)}) async-start(), calls=%async_computation.12 | async-start | bytes 212992 | tf_op jit(solution)/shard_map/psum | solution.py:296
  430.4 30.4 %copy-start.29 = (s32[14,14]{1,0:T(8,128)S(1)}, s32[14,14]{1,0:T(8,128)}, u32[]{:S(2)}) copy-start(s32[14,14]{1,0:T(8,128)} %copy-done.28) | copy-start | bytes 2356
  492.4 228.4 %reduce-scatter.13.cloned.1.call-start = ((), (), s32[]{:S(2)}) async-start(), calls=%async_computation.11 | async-start | bytes 2654208
  501.2 318.6 %reduce-scatter.11.cloned.1.call-start = ((), (), s32[]{:S(2)}) async-start(), calls=%async_computation.10 | async-start | bytes 5308416 | tf_op jit(solution)/shard_map/reduce_scatter | solution.py:313
  526.5 120.2 %copy-start.34 = (f32[3,857]{1,0:T(4,128)S(1)}, f32[3,857]{1,0:T(4,128)}, u32[]{:S(2)}) copy-start(f32[3,857]{1,0:T(4,128)} %param.24) | copy-start | bytes 30856
  526.5 120.2 %copy-start.43 = (f32[3,857]{1,0:T(4,128)S(1)}, f32[3,857]{1,0:T(4,128)}, u32[]{:S(2)}) copy-start(f32[3,857]{1,0:T(4,128)} %param.25) | copy-start | bytes 30856
  526.5 120.2 %copy-start.44 = (f32[3,857]{1,0:T(4,128)S(1)}, f32[3,857]{1,0:T(4,128)}, u32[]{:S(2)}) copy-start(f32[3,857]{1,0:T(4,128)} %param.26) | copy-start | bytes 30856
  526.5 121.6 %copy-start.35 = (f32[12,768]{1,0:T(8,128)S(1)}, f32[12,768]{1,0:T(8,128)}, u32[]{:S(2)}) copy-start(f32[12,768]{1,0:T(8,128)} %param.28) | copy-start | bytes 110596
  526.5 121.6 %copy-start.36 = (f32[12,768]{1,0:T(8,128)S(1)}, f32[12,768]{1,0:T(8,128)}, u32[]{:S(2)}) copy-start(f32[12,768]{1,0:T(8,128)} %param.29) | copy-start | bytes 110596
  530.4 192.7 %copy-start.26 = (f32[4,96,192]{1,2,0:T(8,128)S(1)}, f32[4,96,192]{1,2,0:T(8,128)}, u32[]{:S(2)}) copy-start(f32[4,96,192]{1,2,0:T(8,128)} %copy.179) | copy-start | bytes 884740
  722.1 97.8 %copy-start.24 = (f32[2,96,768]{2,1,0:T(8,128)S(1)}, f32[2,96,768]{2,1,0:T(8,128)}, u32[]{:S(2)}) copy-start(f32[2,96,768]{2,1,0:T(8,128)} %param.21) | copy-start | bytes 1769476
  723.1 100.2 %copy-start.1 = (s32[16,2]{0,1:T(2,128)S(1)}, s32[16,2]{0,1:T(2,128)}, u32[]{:S(2)}) copy-start(s32[16,2]{0,1:T(2,128)} %param.17) | copy-start | bytes 388
  723.4 99.3 %copy-start.30 = (f32[12,768]{1,0:T(8,128)S(1)}, f32[12,768]{1,0:T(8,128)}, u32[]{:S(2)}) copy-start(f32[12,768]{1,0:T(8,128)} %get-tuple-element.219) | copy-start | bytes 110596
  (39 other events, 259.1 us)
Sparse Core Ops, SparseCore 0:
  10.8 46.8 all-gather.5
  60.5 50.8 all-gather.9
  113.5 35.9 all-gather.7
  151.0 64.2 all-gather.11
  390.2 46.5 reduce-scatter.6
  439.4 78.4 reduce-scatter.8
  525.6 120.9 all-reduce.2
  650.5 70.2 reduce-scatter.12
  725.5 94.2 reduce-scatter.10
where the time goes:
time: 843 us; the launch traced here: 830 us
  waiting for transfers between devices  395 us (47%)
  local copies, waits for them, and re-layouts  211 us (25%)
  matrix products  160 us (19%)
  other arithmetic  43.7 us (5%)
  between operations  15 us (2%)
    psum x1, waiting for transfers between devices, shards(): lax.psum((grad_norms, place_heads(grad_heads)), ('dp', 'mp'))  116 us
    reduce_scatter x1, waiting for transfers between devices, shards(): lax.psum_scatter(grad_mlp, 'dp', scatter_dimension=1, tiled=True)  94.5 us
    unnamed x10, waiting for transfers between devices  71.4 us
    all_gather x1, waiting for transfers between devices, shards(): lax.all_gather(mlp_weights.astype(low_type), 'dp', axis=1, tiled=True)  49.5 us
    all_gather x1, waiting for transfers between devices, shards(): lax.all_gather(attention_weights.astype(low_type), 'dp', axis=1, tiled=True)  46.6 us
    unnamed x121, local copies, waits for them, and re-layouts  44 us
    reshape x2, local copies, waits for them, and re-layouts, table_grad(): table_cube = pair_grads.reshape(heads_count, grid, grid, grid, grid)  43.2 us
    add x2, local copies, waits for them, and re-layouts, masked_scores(): jnp.einsum('iqhd,ikhd->ihqk', queries, key_rows, preferred_element_type=j...  41.5 us
  transfers between devices with their start and end apart: 9, of which 6 were waited for; matrix products, arithmetic and copies ran while one was open for 33% of the time, Pallas kernels for 0%

commit v1 on v0

v1 whole, which is shorter than its diff:
```python
import functools

import jax
import jax.numpy as jnp
from jax import lax
from jax.experimental import pallas as pl
from jax.experimental.pallas import tpu as pltpu
from jax.sharding import PartitionSpec as P

HD = 64
GRID = 14
SPAN = 2 * GRID - 1
STEP = 10
PATCHES = 196
PADDED = 208
PACK = 640
OUT_PACK = 256
CHUNKS = 8
LANES = 4
HEADS_LANE = 3

EPSILON = 1e-06
NEGATIVE = -1e30
BETA_ONE = 0.9
BETA_TWO = 0.999
ADAM_EPSILON = 1e-08
RATE_MATRIX = 0.05
RATE_VECTOR = 0.4
DECAY_MATRIX = 0.05

LOW = jnp.bfloat16
FULL = jnp.float32
INV_SQRT2 = 0.7071067811865476
INV_SQRT2PI = 0.3989422804014327
VMEM_LIMIT = 60 << 20


def dot(former, latter, former_dim=1, latter_dim=0):
    return lax.dot_general(
        former,
        latter,
        (((former_dim,), (latter_dim,)), ((), ())),
        preferred_element_type=FULL,
    )


def normalise(values):
    row_mean = jnp.mean(values, axis=-1, keepdims=True)
    centre = values - row_mean
    variance = jnp.mean(centre * centre, axis=-1, keepdims=True)
    inverse = lax.rsqrt(variance + EPSILON)
    return centre * inverse, inverse


def norm_back(incoming, norm_gain, scaled, inverse):
    weighted = incoming * norm_gain
    centred = weighted - jnp.mean(weighted, axis=-1, keepdims=True)
    return inverse * (centred - scaled * jnp.mean(weighted * scaled, axis=-1, keepdims=True))


def fold(values):
    rows, cols = values.shape
    return jnp.sum(values.reshape(rows // 8, 8, cols), axis=0)


def reversed_bits(index):
    return (index & 1) * 4 + (index & 2) + (index & 4) // 4


def whole(shape):
    zeros = (0,) * len(shape)
    return pl.BlockSpec(tuple(shape), lambda *_: zeros)


def params():
    return pltpu.CompilerParams(vmem_limit_bytes=VMEM_LIMIT)


def cost(flops, moved):
    return pl.CostEstimate(flops=int(flops), bytes_accessed=int(moved), transcendentals=0)


def place_rows(target, source, mine, at=None):
    rows = source.shape[1]
    for chunk in range(CHUNKS):
        value = source[reversed_bits(chunk) ^ mine]
        if at is None:
            target[chunk * rows : (chunk + 1) * rows, :] = value
        else:
            target[at, chunk * rows : (chunk + 1) * rows, :] = value


def load_image(pad, source, step):
    for image in range(source.shape[0] // PATCHES):

        @pl.when(step == image)
        def _(image=image):
            pad[0:PATCHES, :] = source[image * PATCHES : (image + 1) * PATCHES, :]

    return pad[...]


def store_image(target, pad, value, step):
    pad[...] = value
    for image in range(target.shape[0] // PATCHES):

        @pl.when(step == image)
        def _(image=image):
            target[image * PATCHES : (image + 1) * PATCHES, :] = pad[0:PATCHES, :]


def prepare_body(images, x_ref, vec_ref, spread_ref, normed_ref, bias_ref, pad_s):
    pad_s[...] = jnp.zeros_like(pad_s)
    for image in range(images):
        scaled, _ = normalise(x_ref[image * PATCHES : (image + 1) * PATCHES, :])
        pad_s[0:PATCHES, :] = scaled * vec_ref[0:1, :] + vec_ref[1:2, :]
        normed_ref[image * PADDED : (image + 1) * PADDED, :] = pad_s[...].astype(LOW)

    def head(index, carry):
        bias_ref[index] = jnp.zeros(bias_ref.shape[1:], FULL)
        for row in range(GRID):
            start = GRID * (GRID - 1 - row)
            bias_ref[index, row * GRID : (row + 1) * GRID, 0:PATCHES] = spread_ref[
                index, :, start : start + PATCHES
            ]
        return carry

    lax.fori_loop(0, bias_ref.shape[0], head, 0)


def prepare(x, vectors, spread, images):
    rows, width = x.shape
    heads = spread.shape[0]
    return pl.pallas_call(
        functools.partial(prepare_body, images),
        out_shape=[
            jax.ShapeDtypeStruct((images * PADDED, width), LOW),
            jax.ShapeDtypeStruct((heads, PADDED, PADDED), FULL),
        ],
        scratch_shapes=[pltpu.VMEM((PADDED, width), FULL)],
        compiler_params=params(),
        cost_estimate=cost(1e6, 8e6),
    )(x, vectors, spread)


Q_TILE = (0, 0, 1)
K_TILE = (3, 3, 4)
V_TILE = (2, 2, 1)
QK_ODD = (False, True, False)
V_ODD = (False, True, True)


def halves():
    lane = lax.broadcasted_iota(jnp.int32, (PADDED, 128), 1)
    return lane


def half_of(value, lane, odd):
    keep = lane >= HD if odd else lane < HD
    return jnp.where(keep, value, jnp.zeros_like(value))


def attend_body(
    me_ref, n_ref, bias_ref, add_ref, scale_ref, mask_ref, w0, w1, w2, w3, qkv_ref, prob_ref, ctx_ref, full_ref
):
    mine = me_ref[0]

    @pl.when(pl.program_id(0) == 0)
    def _():
        for group, piece in enumerate((w0, w1, w2, w3)):
            place_rows(full_ref, piece, mine, group)

    lane = halves()
    mask = mask_ref[0]
    zero = jnp.zeros_like(mask)
    one = jnp.ones_like(mask)
    for group in range(LANES):
        acc = dot(n_ref[...], full_ref[group])
        qkv = ((acc + add_ref[group]) * scale_ref[...]).astype(LOW)
        qkv_ref[group] = qkv
        tiles = [qkv[:, 128 * t : 128 * (t + 1)] for t in range(5)]
        outs = []
        for head in range(HEADS_LANE):
            odd = QK_ODD[head]
            mark = 0 if odd else HD
            keep = lane >= HD if odd else lane < HD
            key = jnp.where(keep, tiles[K_TILE[head]], jnp.where(lane == mark, mask, zero))
            query = jnp.where(lane == mark, one, tiles[Q_TILE[head]])
            scores = dot(key, query, 1, 1) + bias_ref[group * HEADS_LANE + head]
            top = jnp.max(scores, axis=0, keepdims=True)
            exponent = jnp.exp(scores - top)
            total = jnp.sum(exponent, axis=0, keepdims=True)
            prob = (exponent * (1.0 / total)).astype(LOW)
            prob_ref[0, group * HEADS_LANE + head] = prob
            value = half_of(tiles[V_TILE[head]], lane, V_ODD[head])
            outs.append(dot(prob, value, 0, 0))
        ctx_ref[:, group * OUT_PACK : group * OUT_PACK + 128] = (outs[0] + outs[1]).astype(LOW)
        ctx_ref[:, group * OUT_PACK + 128 : (group + 1) * OUT_PACK] = outs[2].astype(LOW)


def attend(mine, normed, bias, add, scale, mask, pieces, images):
    rows, width = normed.shape
    heads = bias.shape[0]
    return pl.pallas_call(
        attend_body,
        grid=(images,),
        in_specs=[
            pl.BlockSpec(memory_space=pltpu.SMEM),
            pl.BlockSpec((PADDED, width), lambda i: (i, 0)),
            whole(bias.shape),
            whole(add.shape),
            whole(scale.shape),
            pl.BlockSpec((1, PADDED, 128), lambda i: (i, 0, 0)),
        ]
        + [whole(piece.shape) for piece in pieces],
        out_specs=[
            pl.BlockSpec((LANES, PADDED, PACK), lambda i: (0, i, 0)),
            pl.BlockSpec((1, heads, PADDED, PADDED), lambda i: (i, 0, 0, 0)),
            pl.BlockSpec((PADDED, LANES * OUT_PACK), lambda i: (i, 0)),
            whole((LANES, width, PACK)),
        ],
        out_shape=[
            jax.ShapeDtypeStruct((LANES, rows, PACK), LOW),
            jax.ShapeDtypeStruct((images, heads, PADDED, PADDED), LOW),
            jax.ShapeDtypeStruct((rows, LANES * OUT_PACK), LOW),
            jax.ShapeDtypeStruct((LANES, width, PACK), LOW),
        ],
        compiler_params=params(),
        cost_estimate=cost(8e9, 2e7),
    )(mine, normed, bias, add, scale, mask, *pieces)


def middle_body(
    me_ref, ctx_ref, x_ref, cot_ref, vec_ref, w0, w1, w2, w3, att_ref, mid_ref, n_ref, gd_ref, cs_ref, full_ref, pad_s
):
    mine = me_ref[0]
    step = pl.program_id(0)

    @pl.when(step == 0)
    def _():
        for group, piece in enumerate((w0, w1, w2, w3)):
            place_rows(full_ref, piece, mine, group)
        pad_s[...] = jnp.zeros_like(pad_s)
        cs_ref[...] = jnp.zeros_like(cs_ref)

    total = vec_ref[4:5, :]
    for group in range(LANES):
        total = total + dot(
            ctx_ref[:, group * OUT_PACK : (group + 1) * OUT_PACK], full_ref[group], 1, 1
        )
    att_ref[...] = total
    mid = load_image(pad_s, x_ref, step) + vec_ref[5:6, :] * total
    mid_ref[...] = mid
    scaled, _ = normalise(mid)
    n_ref[...] = (scaled * vec_ref[2:3, :] + vec_ref[3:4, :]).astype(LOW)
    cot = load_image(pad_s, cot_ref, step)
    gd_ref[...] = (cot * vec_ref[7:8, :]).astype(LOW)
    cs_ref[...] += fold(cot)


def middle(mine, ctx, x, cot, vectors, pieces, images):
    rows = images * PADDED
    width = x.shape[1]
    block = lambda: pl.BlockSpec((PADDED, width), lambda i: (i, 0))
    return pl.pallas_call(
        middle_body,
        grid=(images,),
        in_specs=[
            pl.BlockSpec(memory_space=pltpu.SMEM),
            pl.BlockSpec((PADDED, LANES * OUT_PACK), lambda i: (i, 0)),
            whole(x.shape),
            whole(cot.shape),
            whole(vectors.shape),
        ]
        + [whole(piece.shape) for piece in pieces],
        out_specs=[block(), block(), block(), block(), whole((8, width)), whole((LANES, width, OUT_PACK))],
        out_shape=[
            jax.ShapeDtypeStruct((rows, width), FULL),
            jax.ShapeDtypeStruct((rows, width), FULL),
            jax.ShapeDtypeStruct((rows, width), LOW),
            jax.ShapeDtypeStruct((rows, width), LOW),
            jax.ShapeDtypeStruct((8, width), FULL),
            jax.ShapeDtypeStruct((LANES, width, OUT_PACK), LOW),
        ],
        scratch_shapes=[pltpu.VMEM((PADDED, width), FULL)],
        compiler_params=params(),
        cost_estimate=cost(1.3e9, 1.5e7),
    )(mine, ctx, x, cot, vectors, *pieces)


def gelu_pair(values):
    density = jnp.exp(values * values * -0.5) * INV_SQRT2PI
    below = 0.5 * lax.erf(values * INV_SQRT2) + 0.5
    return values * below, below + values * density


def feed_body(steps, blocks, me_ref, n_ref, gd_ref, ub_ref, *refs):
    up = refs[:LANES]
    down = refs[LANES : 2 * LANES]
    out_ref, gn_ref, keep1, send1, keep2, send2, gub_ref, nt_s, gdt_s, up_s, down_s, act_s, gh_s = refs[
        2 * LANES :
    ]
    step = pl.program_id(0)
    mine = me_ref[0]
    rows = n_ref.shape[0]
    per = rows // blocks
    chunk_rows = up[0].shape[1]

    @pl.when(step == 0)
    def _():
        nt_s[...] = n_ref[...].T
        gdt_s[...] = gd_ref[...].T
        out_ref[...] = jnp.zeros_like(out_ref)
        gn_ref[...] = jnp.zeros_like(gn_ref)

    for piece in range(LANES):

        @pl.when(step // steps == piece)
        def _(piece=piece):
            place_rows(up_s, up[piece], mine)
            place_rows(down_s, down[piece], mine)

    up_weight = up_s[...]
    down_weight = down_s[...]
    unit_sums = jnp.zeros((8, up_weight.shape[1]), FULL)
    for block in range(blocks):
        part = slice(block * per, (block + 1) * per)
        hidden = dot(n_ref[part, :], up_weight) + ub_ref[0]
        active, slope = gelu_pair(hidden)
        active = active.astype(LOW)
        act_s[part, :] = active
        grad = (dot(gd_ref[part, :], down_weight) * slope).astype(LOW)
        gh_s[part, :] = grad
        unit_sums = unit_sums + fold(grad.astype(FULL))
        out_ref[part, :] += dot(active, down_weight, 1, 1)
        gn_ref[part, :] += dot(grad, up_weight, 1, 1)
    gub_ref[0] = unit_sums
    grad_up = dot(nt_s[...], gh_s[...]).astype(LOW)
    grad_down = dot(gdt_s[...], act_s[...]).astype(LOW)
    for piece in range(LANES):

        @pl.when(step // steps == piece)
        def _(piece=piece):
            one, two = (keep1, keep2) if piece % 2 == 0 else (send1, send2)
            for chunk in range(CHUNKS):
                slot = reversed_bits(chunk) ^ mine
                one[0, slot] = grad_up[chunk * chunk_rows : (chunk + 1) * chunk_rows]
                two[0, slot] = grad_down[chunk * chunk_rows : (chunk + 1) * chunk_rows]


def feed(mine, normed, grad_down, unit_bias, up, down, images):
    rows, width = normed.shape
    _, chunk_rows, units = up[0].shape
    sub = units if images <= 4 else units // 2
    blocks = 2 if images <= 4 else 4
    steps = units // sub

    def piece_map(piece):
        return lambda j: (0, 0, jnp.clip(j - piece * steps, 0, steps - 1))

    def keep_map(j):
        slot = jnp.where(j >= 2 * steps, 1, 0)
        return (slot, 0, 0, jnp.clip(j - 2 * steps * slot, 0, steps - 1))

    def send_map(j):
        slot = jnp.where(j >= 3 * steps, 1, 0)
        return (slot, 0, 0, jnp.clip(j - steps - 2 * steps * slot, 0, steps - 1))

    grad_block = (1, CHUNKS, chunk_rows, sub)
    grads = jax.ShapeDtypeStruct((2, CHUNKS, chunk_rows, units), LOW)
    total = LANES * steps
    return pl.pallas_call(
        functools.partial(feed_body, steps, blocks),
        grid=(total,),
        in_specs=[
            pl.BlockSpec(memory_space=pltpu.SMEM),
            whole((rows, width)),
            whole((rows, width)),
            pl.BlockSpec((1, 1, sub), lambda j: (j, 0, 0)),
        ]
        + [pl.BlockSpec((CHUNKS, chunk_rows, sub), piece_map(p)) for p in range(LANES)] * 2,
        out_specs=[
            whole((rows, width)),
            whole((rows, width)),
            pl.BlockSpec(grad_block, keep_map),
            pl.BlockSpec(grad_block, send_map),
            pl.BlockSpec(grad_block, keep_map),
            pl.BlockSpec(grad_block, send_map),
            pl.BlockSpec((1, 8, sub), lambda j: (j, 0, 0)),
        ],
        out_shape=[jax.ShapeDtypeStruct((rows, width), FULL)] * 2
        + [grads] * 4
        + [jax.ShapeDtypeStruct((total, 8, sub), FULL)],
        scratch_shapes=[
            pltpu.VMEM((width, rows), LOW),
            pltpu.VMEM((width, rows), LOW),
            pltpu.VMEM((width, sub), LOW),
            pltpu.VMEM((width, sub), LOW),
            pltpu.VMEM((rows, sub), LOW),
            pltpu.VMEM((rows, sub), LOW),
        ],
        compiler_params=params(),
        cost_estimate=cost(12 * rows * width * units * LANES, 4e7),
    )(mine, normed, grad_down, unit_bias.reshape(total, 1, sub), *up, *down)


def back_body(
    me_ref,
    down_ref,
    gn_ref,
    mid_ref,
    att_ref,
    ctx_ref,
    cot_ref,
    vec_ref,
    wo_ref,
    qkv_ref,
    prob_ref,
    out_ref,
    gm_ref,
    dqkv_ref,
    keep_ref,
    send_ref,
    spread_ref,
    sums_ref,
    cols_ref,
    pad_s,
    out_s,
    ga_s,
    pair_s,
):
    mine = me_ref[0]
    step = pl.program_id(0)
    heads = pair_s.shape[0]

    @pl.when(step == 0)
    def _():
        pad_s[...] = jnp.zeros_like(pad_s)
        pair_s[...] = jnp.zeros_like(pair_s)
        sums_ref[...] = jnp.zeros_like(sums_ref)
        cols_ref[...] = jnp.zeros_like(cols_ref)

    cot = load_image(pad_s, cot_ref, step)
    down = down_ref[...] + vec_ref[6:7, :]
    mid = mid_ref[...]
    store_image(out_ref, out_s, mid + vec_ref[7:8, :] * down, step)
    scaled, inverse = normalise(mid)
    grad_normed = gn_ref[...]
    grad_mid = cot + norm_back(grad_normed, vec_ref[2:3, :], scaled, inverse)
    gm_ref[...] = grad_mid
    sums_ref[0] += fold(grad_normed * scaled)
    sums_ref[1] += fold(grad_normed)
    sums_ref[2] += fold(grad_mid)
    sums_ref[3] += fold(grad_mid * att_ref[...])
    sums_ref[4] += fold(cot * down)
    grad_att = (grad_mid * vec_ref[5:6, :]).astype(LOW)
    ga_s[pl.ds(pl.multiple_of(step * PADDED, PADDED), PADDED), :] = grad_att

    lane = halves()
    for group in range(LANES):
        grad_ctx = dot(grad_att, wo_ref[group]).astype(LOW)
        qkv = qkv_ref[group]
        tiles = [qkv[:, 128 * t : 128 * (t + 1)] for t in range(5)]
        grads = []
        for head in range(HEADS_LANE):
            odd, value_odd = QK_ODD[head], V_ODD[head]
            query = half_of(tiles[Q_TILE[head]], lane, odd)
            key = half_of(tiles[K_TILE[head]], lane, odd)
            value = tiles[V_TILE[head]]
            half = 128 if head == 2 else 0
            upstream = half_of(grad_ctx[:, half : half + 128], lane, value_odd)
            prob = prob_ref[0, group * HEADS_LANE + head]
            grad_prob = dot(value, upstream, 1, 1)
            soft = prob.astype(FULL)
            weighted = soft * grad_prob
            inner = jnp.sum(weighted, axis=0, keepdims=True)
            grad_score = weighted - soft * inner
            pair_s[group * HEADS_LANE + head] += grad_score
            low_score = grad_score.astype(LOW)
            grads.append(
                (
                    dot(low_score, key, 0, 0) * HD**-0.5,
                    dot(low_score, query),
                    dot(prob, upstream),
                )
            )
        packed = (
            grads[0][0] + grads[1][0],
            grads[2][0] + grads[2][2],
            grads[0][2] + grads[1][2],
            grads[0][1] + grads[1][1],
            grads[2][1],
        )
        for tile, value in enumerate(packed):
            low_value = value.astype(LOW)
            dqkv_ref[group, :, 128 * tile : 128 * (tile + 1)] = low_value
            cols_ref[group, :, 128 * tile : 128 * (tile + 1)] += fold(low_value.astype(FULL))

    @pl.when(step == pl.num_programs(0) - 1)
    def _():
        grad_out = dot(ga_s[...], ctx_ref[...], 0, 0).astype(LOW)
        rows = keep_ref.shape[2]
        for group in range(LANES):
            target = (keep_ref, send_ref)[group % 2]
            for chunk in range(CHUNKS):
                target[group // 2, reversed_bits(chunk) ^ mine] = grad_out[
                    chunk * rows : (chunk + 1) * rows, group * OUT_PACK : (group + 1) * OUT_PACK
                ]
        spread_ref[...] = jnp.zeros_like(spread_ref)

        def head_sum(index, carry):
            for row in range(GRID):
                at = GRID * (GRID - 1 - row)
                spread_ref[index, :, at : at + PATCHES] += pair_s[
                    index, row * GRID : (row + 1) * GRID, 0:PATCHES
                ]
            return carry

        lax.fori_loop(0, heads, head_sum, 0)


def back(mine, down, grad_normed, mid, att, ctx, cot, vectors, wo, qkv, prob, images, chunk_rows):
    rows, width = mid.shape
    heads = prob.shape[1]
    block = lambda: pl.BlockSpec((PADDED, width), lambda i: (i, 0))
    grads = (2, CHUNKS, chunk_rows, OUT_PACK)
    return pl.pallas_call(
        back_body,
        grid=(images,),
        in_specs=[
            pl.BlockSpec(memory_space=pltpu.SMEM),
            block(),
            block(),
            block(),
            block(),
            whole(ctx.shape),
            whole(cot.shape),
            whole(vectors.shape),
            whole(wo.shape),
            pl.BlockSpec((LANES, PADDED, PACK), lambda i: (0, i, 0)),
            pl.BlockSpec((1, heads, PADDED, PADDED), lambda i: (i, 0, 0, 0)),
        ],
        out_specs=[
            whole(cot.shape),
            block(),
            pl.BlockSpec((LANES, PADDED, PACK), lambda i: (0, i, 0)),
            whole(grads),
            whole(grads),
            whole((heads, GRID, 384)),
            whole((5, 8, width)),
            whole((LANES, 8, PACK)),
        ],
        out_shape=[
            jax.ShapeDtypeStruct(cot.shape, FULL),
            jax.ShapeDtypeStruct((rows, width), FULL),
            jax.ShapeDtypeStruct((LANES, rows, PACK), LOW),
            jax.ShapeDtypeStruct(grads, LOW),
            jax.ShapeDtypeStruct(grads, LOW),
            jax.ShapeDtypeStruct((heads, GRID, 384), FULL),
            jax.ShapeDtypeStruct((5, 8, width), FULL),
            jax.ShapeDtypeStruct((LANES, 8, PACK), FULL),
        ],
        scratch_shapes=[
            pltpu.VMEM((PADDED, width), FULL),
            pltpu.VMEM((PADDED, width), FULL),
            pltpu.VMEM((rows, width), LOW),
            pltpu.VMEM((heads, PADDED, PADDED), FULL),
        ],
        compiler_params=params(),
        cost_estimate=cost(1.2e10, 4e7),
    )(mine, down, grad_normed, mid, att, ctx, cot, vectors, wo, qkv, prob)


def project_body(me_ref, n_ref, dqkv_ref, keep_ref, send_ref, nt_s):
    mine = me_ref[0]
    nt_s[...] = n_ref[...].T
    rows = keep_ref.shape[2]
    for group in range(LANES):
        grad = dot(nt_s[...], dqkv_ref[group]).astype(LOW)
        target = (keep_ref, send_ref)[group % 2]
        for chunk in range(CHUNKS):
            target[group // 2, reversed_bits(chunk) ^ mine] = grad[chunk * rows : (chunk + 1) * rows]


def project(mine, normed, dqkv, chunk_rows):
    rows, width = normed.shape
    grads = jax.ShapeDtypeStruct((2, CHUNKS, chunk_rows, PACK), LOW)
    return pl.pallas_call(
        project_body,
        in_specs=[pl.BlockSpec(memory_space=pltpu.SMEM)] + [pl.BlockSpec(memory_space=pltpu.VMEM)] * 2,
        out_shape=[grads, grads],
        scratch_shapes=[pltpu.VMEM((width, rows), LOW)],
        compiler_params=params(),
        cost_estimate=cost(2 * rows * width * PACK * LANES, 1e7),
    )(mine, normed, dqkv)


def input_body(dqkv_ref, full_ref, gm_ref, x_ref, vec_ref, out_ref, sums_ref, pad_s, out_s):
    step = pl.program_id(0)

    @pl.when(step == 0)
    def _():
        pad_s[...] = jnp.zeros_like(pad_s)
        sums_ref[...] = jnp.zeros_like(sums_ref)

    scaled, inverse = normalise(load_image(pad_s, x_ref, step))
    grad = dot(dqkv_ref[0], full_ref[0], 1, 1)
    for group in range(1, LANES):
        grad = grad + dot(dqkv_ref[group], full_ref[group], 1, 1)
    sums_ref[0] += fold(grad * scaled)
    sums_ref[1] += fold(grad)
    result = gm_ref[...] + norm_back(grad, vec_ref[0:1, :], scaled, inverse)
    store_image(out_ref, out_s, result, step)


def input_back(dqkv, full, grad_mid, x, vectors, images):
    width = x.shape[1]
    return pl.pallas_call(
        input_body,
        grid=(images,),
        in_specs=[
            pl.BlockSpec((LANES, PADDED, PACK), lambda i: (0, i, 0)),
            whole(full.shape),
            pl.BlockSpec((PADDED, width), lambda i: (i, 0)),
            whole(x.shape),
            whole(vectors.shape),
        ],
        out_specs=[whole(x.shape), whole((2, 8, width))],
        out_shape=[jax.ShapeDtypeStruct(x.shape, FULL), jax.ShapeDtypeStruct((2, 8, width), FULL)],
        scratch_shapes=[pltpu.VMEM((PADDED, width), FULL)] * 2,
        compiler_params=params(),
        cost_estimate=cost(4e9, 1.5e7),
    )(dqkv, full, grad_mid, x, vectors)


def swap(values, axis, bit):
    count = lax.axis_size(axis)
    return lax.ppermute(values, axis, [(index, index ^ bit) for index in range(count)])


def gather_near(piece):
    held = piece[None]
    for bit in (4, 2, 1):
        held = jnp.concatenate([held, swap(held, "dp", bit)], axis=0)
    far = swap(held, "mp", 2)
    return (held, swap(held, "mp", 1), far, swap(far, "mp", 1))


def scatter_near(keep, send):
    got = swap(send, "mp", 1)
    near = keep[0].astype(FULL) + got[0].astype(FULL)
    away = (keep[1].astype(FULL) + got[1].astype(FULL)).astype(LOW)
    near = near + swap(away, "mp", 2).astype(FULL)
    for bit, half in ((1, 4), (2, 2), (4, 1)):
        near = near[:half] + swap(near[half:].astype(LOW), "dp", bit).astype(FULL)
    return near[0]


def adam(weight, moment_one, moment_two, incoming, step_rate, decay_rate):
    first_new = BETA_ONE * moment_one + (1.0 - BETA_ONE) * incoming
    second_new = BETA_TWO * moment_two + (1.0 - BETA_TWO) * incoming * incoming
    update = (
        first_new
        / (1.0 - BETA_ONE**STEP)
        / (jnp.sqrt(second_new / (1.0 - BETA_TWO**STEP)) + ADAM_EPSILON)
    )
    return (second_new, weight * (1.0 - step_rate * decay_rate) - step_rate * update)


def pack_attention(weights):
    query, key, value, out = (weights[index] for index in range(4))
    rows = query.shape[0]
    blank = jnp.zeros((rows, HD), weights.dtype)
    first = jnp.concatenate([query, value[:, 128:], value[:, :128], key, blank], axis=1)
    last = jnp.concatenate([out[:, :128], blank, out[:, 128:]], axis=1)
    return first, last


def unpack_attention(first, last):
    query = first[:, :192]
    value = jnp.concatenate([first[:, 256:384], first[:, 192:256]], axis=1)
    key = first[:, 384:576]
    out = jnp.concatenate([last[:, :128], last[:, 192:]], axis=1)
    return jnp.stack([query, key, value, out])


def spread_table(table):
    heads = table.shape[0]
    cube = table.reshape(heads, SPAN, SPAN)
    parts = [cube[:, :, GRID - 1 - col : SPAN - col] for col in range(GRID)]
    flat = jnp.stack(parts, axis=1).reshape(heads, GRID, SPAN * GRID)
    return jnp.pad(flat, ((0, 0), (0, 0), (0, 384 - SPAN * GRID)))


def gather_table(spread):
    heads = spread.shape[0]
    cube = spread[:, :, : SPAN * GRID].reshape(heads, GRID, SPAN, GRID)
    total = 0.0
    for col in range(GRID):
        total = total + jnp.pad(cube[:, col], ((0, 0), (0, 0), (GRID - 1 - col, col)))
    return total.reshape(heads, SPAN * SPAN)


def shards(
    block_input,
    cotangent,
    image_size,
    attention_weights,
    attention_first,
    attention_second,
    mlp_weights,
    mlp_first,
    mlp_second,
    head_params,
    head_first,
    head_second,
    norm_params,
    norm_first,
    norm_second,
):
    near = lax.axis_size("dp") == CHUNKS
    lane_index = lax.axis_index("mp")
    local_rows, width = block_input.shape
    images = local_rows // PATCHES
    local_heads = head_params.shape[0]
    chunk_rows = width // CHUNKS

    first, last = pack_attention(attention_weights.astype(LOW))
    mlp_low = mlp_weights.astype(LOW)
    if near:
        mine = reversed_bits(lax.axis_index("dp")).astype(jnp.int32)[None]
        other = swap(head_params, "mp", 2)
        both = jnp.stack([head_params, other])
        cross = swap(both, "mp", 1)
        tables = jnp.stack([both[0], cross[0], both[1], cross[1]])
        unit_bias = norm_params[8:]
        qkv_pieces = gather_near(first)
        out_pieces = gather_near(last)
        up_pieces = gather_near(mlp_low[0])
        down_pieces = gather_near(mlp_low[1])
        lanes = [lane_index ^ index for index in range(LANES)]
        unit_bias = jnp.stack([lax.dynamic_index_in_dim(unit_bias, lane, 0, False) for lane in lanes])
    else:
        mine = jnp.zeros((1,), jnp.int32)

        def gather_far(piece):
            full = lax.all_gather(piece, "dp", axis=0, tiled=True)
            full = lax.all_gather(full, "mp", axis=0, tiled=False)
            full = full.reshape(LANES, CHUNKS, chunk_rows, piece.shape[1])
            order = [reversed_bits(index) for index in range(CHUNKS)]
            full = jnp.stack([full[:, index] for index in order], axis=1)
            return tuple(full[index] for index in range(LANES))

        tables = lax.all_gather(head_params, "mp", axis=0, tiled=False)
        qkv_pieces = gather_far(first)
        out_pieces = gather_far(last)
        up_pieces = gather_far(mlp_low[0])
        down_pieces = gather_far(mlp_low[1])
        unit_bias = norm_params[8:]

    per_lane = image_size.shape[0] // LANES
    image_dims = lax.dynamic_slice_in_dim(image_size, lane_index * per_lane, per_lane, 0)
    position = jnp.arange(PADDED, dtype=jnp.int32)
    valid = (
        ((position // GRID)[None, :] < image_dims[:, 0:1])
        & ((position % GRID)[None, :] < image_dims[:, 1:2])
        & (position < PATCHES)[None, :]
    )
    mask = jnp.where(valid, 0.0, NEGATIVE).astype(LOW)
    mask = jnp.broadcast_to(mask[:, :, None], (images, PADDED, 128))

    query_bias = tables[:, :, :HD].reshape(LANES, -1)
    value_bias = tables[:, :, HD : 2 * HD].reshape(LANES, -1)
    blank = jnp.zeros((LANES, PACK - 384), FULL)
    add = jnp.concatenate(
        [query_bias, value_bias[:, 128:], value_bias[:, :128], blank], axis=1
    ).reshape(LANES, 1, PACK)
    scale = jnp.where(jnp.arange(PACK) < 192, HD**-0.5, 1.0).astype(FULL)[None]
    spread = spread_table(tables[:, :, 2 * HD :].reshape(LANES * local_heads, -1))

    normed_one, bias = prepare(block_input, norm_params, spread, images)
    qkv, prob, ctx, full = attend(mine, normed_one, bias, add, scale, mask, qkv_pieces, images)
    att, mid, normed_two, grad_down, cot_sum, wo = middle(
        mine, ctx, block_input, cotangent, norm_params, out_pieces, images
    )
    down, grad_normed, keep1, send1, keep2, send2, unit_sums = feed(
        mine, normed_two, grad_down, unit_bias, up_pieces, down_pieces, images
    )
    output, grad_mid, dqkv, keep_out, send_out, grad_spread, sums, cols = back(
        mine, down, grad_normed, mid, att, ctx, cotangent, norm_params, wo, qkv, prob, images, chunk_rows
    )
    keep_qkv, send_qkv = project(mine, normed_one, dqkv, chunk_rows)
    grad_input, first_sums = input_back(dqkv, full, grad_mid, block_input, norm_params, images)

    sums = jnp.sum(sums, axis=1)
    first_sums = jnp.sum(first_sums, axis=1)
    cot_sum = jnp.sum(cot_sum, axis=0)
    vector_rows = jnp.stack(
        [
            first_sums[0],
            first_sums[1],
            sums[0],
            sums[1],
            sums[2] * norm_params[5],
            sums[3],
            cot_sum * norm_params[7],
            sums[4],
        ]
    )
    unit_sums = jnp.sum(unit_sums, axis=1).reshape(LANES, width)
    cols = jnp.sum(cols, axis=1)
    grad_heads = jnp.concatenate(
        [
            cols[:, :192].reshape(LANES, local_heads, HD),
            jnp.concatenate([cols[:, 256:384], cols[:, 192:256]], axis=1).reshape(
                LANES, local_heads, HD
            ),
            gather_table(grad_spread).reshape(LANES, local_heads, -1),
        ],
        axis=2,
    )
    if near:
        placed = jnp.stack(
            [lax.dynamic_index_in_dim(unit_sums, lane, 0, False) for lane in lanes]
        )
        heads_width = grad_heads.shape[2]
        wide = lambda rows: jnp.pad(rows, ((0, 0), (0, heads_width - width)))
        norms = wide(jnp.concatenate([vector_rows, placed], axis=0))
        keep = jnp.concatenate([norms, grad_heads[0], grad_heads[2]], axis=0)
        send = jnp.concatenate([norms, grad_heads[1], grad_heads[3]], axis=0)
        small = keep + swap(send, "mp", 1)
        rest = 12 + local_heads
        keep = small[:rest]
        send = jnp.concatenate([small[:12], small[rest:]], axis=0)
        small = keep + swap(send, "mp", 2)
        for bit in (1, 2, 4):
            small = small + swap(small, "dp", bit)
        reduced_norms = small[:12, :width]
        reduced_heads = small[12:]
        grad_up = scatter_near(keep1, send1)
        grad_dn = scatter_near(keep2, send2)
        grad_out = scatter_near(keep_out, send_out)
        grad_qkv = scatter_near(keep_qkv, send_qkv)
    else:
        norms = jnp.concatenate([vector_rows, unit_sums], axis=0)
        reduced_norms = lax.psum(norms, ("dp", "mp"))
        reduced_heads = lax.psum_scatter(
            lax.psum(grad_heads, "dp"), "mp", scatter_dimension=0, tiled=False
        )

        def scatter_far(keep, send):
            terms = jnp.stack([keep[0], send[0], keep[1], send[1]])
            order = [reversed_bits(index) for index in range(CHUNKS)]
            terms = jnp.stack([terms[:, index] for index in order], axis=1)
            terms = terms.reshape(LANES, width, terms.shape[-1])
            mine_only = lax.psum_scatter(terms, "mp", scatter_dimension=0, tiled=False)
            return lax.psum_scatter(
                mine_only.astype(FULL), "dp", scatter_dimension=0, tiled=True
            )

        grad_up = scatter_far(keep1, send1)
        grad_dn = scatter_far(keep2, send2)
        grad_out = scatter_far(keep_out, send_out)
        grad_qkv = scatter_far(keep_qkv, send_qkv)

    reduced_attention = unpack_attention(grad_qkv, grad_out)
    reduced_mlp = jnp.stack([grad_up, grad_dn])
    attention_second_new, attention_new = adam(
        attention_weights,
        attention_first,
        attention_second,
        reduced_attention,
        RATE_MATRIX,
        DECAY_MATRIX,
    )
    mlp_second_new, mlp_new = adam(
        mlp_weights, mlp_first, mlp_second, reduced_mlp, RATE_MATRIX, DECAY_MATRIX
    )
    head_second_new, head_new = adam(
        head_params, head_first, head_second, reduced_heads, RATE_VECTOR, 0.0
    )
    norm_second_new, norm_new = adam(
        norm_params, norm_first, norm_second, reduced_norms, RATE_VECTOR, 0.0
    )
    return (
        output,
        grad_input,
        reduced_attention,
        attention_second_new,
        attention_new,
        reduced_mlp,
        mlp_second_new,
        mlp_new,
        reduced_heads,
        head_second_new,
        head_new,
        reduced_norms,
        norm_second_new,
        norm_new,
    )


def solution(mesh):
    rows = P(("dp", "mp"), None)
    matrix = P(None, "dp", "mp")
    head = P("mp", None)
    placed = (rows, rows, P("dp", None)) + (matrix,) * 6 + (head,) * 3 + (P(),) * 3
    given = (rows, rows) + (matrix,) * 6 + (head,) * 3 + (P(),) * 3
    return jax.shard_map(shards, mesh=mesh, in_specs=placed, out_specs=given, check_vma=False)
```

time: 843 us -> 420 us (0.50)
  waiting for transfers between devices: 395 us -> 194 us
  local copies, waits for them, and re-layouts: 211 us -> 21.2 us
  matrix products: 160 us -> 0 us
  Pallas kernels: 0 us -> 128 us
  starting transfers between devices: 0.37 us -> 48.2 us
  other arithmetic: 43.7 us -> 20.3 us
  between operations: 15 us -> 1.86 us
    ppermute x0 -> x51, waiting for transfers between devices: none -> 194 us  [swap(): lax.ppermute(values, axis, [(index, index ^ bit) for index in range(count)])]
    dot_general x22 -> x0, matrix products: 160 us -> none  [the longest x1 28.5 us: shards(): jnp.dot(rows_two, up_weight, preferred_element_type=full_type)]
    pallas_call x0 -> x7, Pallas kernels: none -> 128 us  [the longest x1 38.5 us: feed(): pl.pallas_call(functools.partial(feed_body, steps, blocks), grid=(total,)...]
    psum x1 -> x0, waiting for transfers between devices: 116 us -> none  [shards(): lax.psum((grad_norms, place_heads(grad_heads)), ('dp', 'mp'))]
    reduce_scatter x3 -> x0, waiting for transfers between devices: 111 us -> none  [the longest x1 94.5 us: shards(): lax.psum_scatter(grad_mlp, 'dp', scatter_dimension=1, tiled=True)]
    all_gather x4 -> x0, waiting for transfers between devices: 96.1 us -> none  [the longest x1 49.5 us: shards(): lax.all_gather(mlp_weights.astype(low_type), 'dp', axis=1, tiled=True)]
    unnamed x10 -> x0, waiting for transfers between devices: 71.4 us -> none
    ppermute x0 -> x51, starting transfers between devices: none -> 48.2 us  [swap(): lax.ppermute(values, axis, [(index, index ^ bit) for index in range(count)])]
  transfers between devices with their start and end apart: 9 -> 51, of which waited for: 6 -> 25; matrix products, arithmetic and copies ran while one was open for 33% -> 9% of each run, Pallas kernels for 0% -> 14%
where the time goes in v1:
time: 420 us; the launch traced here: 413 us
  waiting for transfers between devices  194 us (46%)
  Pallas kernels  128 us (30%)
  starting transfers between devices  48.2 us (11%)
  local copies, waits for them, and re-layouts  21.2 us (5%)
  other arithmetic  20.3 us (5%)
    ppermute x51, waiting for transfers between devices, swap(): lax.ppermute(values, axis, [(index, index ^ bit) for index in range(count)])  194 us
    ppermute x51, starting transfers between devices, swap(): lax.ppermute(values, axis, [(index, index ^ bit) for index in range(count)])  48.2 us
    pallas_call x1, Pallas kernels, feed(): pl.pallas_call(functools.partial(feed_body, steps, blocks), grid=(total,)...  38.5 us
    pallas_call x1, Pallas kernels, back(): pl.pallas_call(back_body, grid=(images,), in_specs=[pl.BlockSpec(memory_s...  33.3 us
    pallas_call x1, Pallas kernels, attend(): pl.pallas_call(attend_body, grid=(images,), in_specs=[pl.BlockSpec(memory...  19.2 us
    pallas_call x1, Pallas kernels, input_back(): pl.pallas_call(input_body, grid=(images,), in_specs=[pl.BlockSpec((LANES,...  12 us
    another operation x15, local copies, waits for them, and re-layouts, spread_table(): flat = jnp.stack(parts, axis=1).reshape(heads, GRID, SPAN * GRID)  9.92 us
    pallas_call x1, Pallas kernels, middle(): pl.pallas_call(middle_body, grid=(images,), in_specs=[pl.BlockSpec(memory...  9.5 us
  transfers between devices with their start and end apart: 51, of which 25 were waited for; matrix products, arithmetic and copies ran while one was open for 9% of the time, Pallas kernels for 14%

profile of v1, /device:TPU:0, one launch (start us, length us, event | category | flops | bytes accessed | tf_op | source)
XLA Modules:
  0.0 413.1 jit_solution(12255788951074117737)
XLA Ops:
  0.7 3.0 collective-permute-start
  11.1 12.1 %collective-permute-done.2 = bf16[1,96,640]{2,1,0:T(8,128)(2,1)S(1)} collective-permute-done((bf16[1,96,640]{2,1,0:T(8,128)(2,1)S(1)}, bf16[1,96,640]{2,1,0:T(8,128)(2,1)S(1)}, u32[]{:S(2)}, u32[]{:S(2)}) %collective-permute-start.2) | collective-permute-done | bytes 122912 | tf_op jit(solution)/shard_map/ppermute | solution.py:638
  23.3 3.1 collective-permute-done.20
  29.0 5.1 %collective-permute-done.3 = bf16[2,96,640]{2,1,0:T(8,128)(2,1)S(1)} collective-permute-done((bf16[2,96,640]{2,1,0:T(8,128)(2,1)S(1)}, bf16[2,96,640]{2,1,0:T(8,128)(2,1)S(1)}, u32[]{:S(2)}, u32[]{:S(2)}) %collective-permute-start.3) | collective-permute-done | bytes 245792 | tf_op jit(solution)/shard_map/ppermute | solution.py:638
  35.8 10.8 %collective-permute-done.15 = bf16[2,96,768]{2,1,0:T(8,128)(2,1)S(1)} collective-permute-done((bf16[2,96,768]{2,1,0:T(8,128)(2,1)S(1)}, bf16[2,96,768]{2,1,0:T(8,128)(2,1)S(1)}, u32[]{:S(2)}, u32[]{:S(2)}) %collective-permute-start.15) | collective-permute-done | bytes 294944 | tf_op jit(solution)/shard_map/ppermute | solution.py:638
  55.3 7.7 %collective-permute-done.16 = bf16[4,96,768]{2,1,0:T(8,128)(2,1)S(1)} collective-permute-done((bf16[4,96,768]{2,1,0:T(8,128)(2,1)S(1)}, bf16[4,96,768]{2,1,0:T(8,128)(2,1)S(1)}, u32[]{:S(2)}, u32[]{:S(2)}) %collective-permute-start.16) | collective-permute-done | bytes 589856 | tf_op jit(solution)/shard_map/ppermute | solution.py:638
  63.7 11.9 %collective-permute-done.22 = bf16[4,96,768]{2,1,0:T(8,128)(2,1)S(1)} collective-permute-done((bf16[4,96,768]{2,1,0:T(8,128)(2,1)S(1)}, bf16[4,96,768]{2,1,0:T(8,128)(2,1)S(1)}, u32[]{:S(2)}, u32[]{:S(2)}) %collective-permute-start.22) | collective-permute-done | bytes 589856 | tf_op jit(solution)/shard_map/ppermute | solution.py:638
  81.4 51.0 %collective-permute-done.12.w2 = bf16[8,96,256]{2,1,0:T(8,128)(2,1)S(1)} collective-permute-done((bf16[8,96,256]{2,1,0:T(8,128)(2,1)S(1)}, bf16[8,96,256]{2,1,0:T(8,128)(2,1)S(1)}, u32[]{:S(2)}, u32[]{:S(2)}) %collective-permute-start.12) | collective-permute-done | bytes 393248 | tf_op jit(solution)/shard_map/ppermute | solution.py:638
  148.7 6.6 %shard_map.254 = (bf16[832,768]{1,0:T(8,128)(2,1)}, f32[12,208,208]{2,1,0:T(8,128)}) custom-call(f32[784,768]{1,0:T(8,128)} %x_ref.5, f32[12,768]{1,0:T(8,128)} %vec_ref.7, f32[12,14,384]{2,1,0:T(8,128)} %pad.64.spread_ref), custom_call_target="tpu_custom_call" | custom-call | flops 1000000 | bytes 8000000 | tf_op jit(solution)/shard_map/pallas_call | solution.py:134
  156.3 19.2 %shard_map.255 = (bf16[4,832,640]{2,1,0:T(8,128)(2,1)}, bf16[4,12,208,208]{3,2,1,0:T(8,128)(2,1)}, bf16[832,1024]{1,0:T(8,128)(2,1)}, bf16[4,768,640]{2,1,0:T(8,128)(2,1)}) custom-call(s32[1]{0:T(128)} %bitcast.me_ref, bf16[832,768]{1,0:T(8,128)(2,1)} %get-tuple-element.45.n_ref, f32[12,208,208]{2,1,0:T(8,128)} %get-tuple-element.46.bias_ref, ...), custom_call_target="tpu_custom_call" | custom-call | flops 8000000000 | bytes 20000000 | tf_op jit(solution)/shard_map/pallas_call | solution.py:204
  176.2 9.5 %shard_map.256 = (f32[832,768]{1,0:T(8,128)}, f32[832,768]{1,0:T(8,128)}, bf16[832,768]{1,0:T(8,128)(2,1)}, bf16[832,768]{1,0:T(8,128)(2,1)}, f32[8,768]{1,0:T(8,128)}, /*index=5*/bf16[4,768,256]{2,1,0:T(8,128)(2,1)}) custom-call(s32[1]{0:T(128)} %bitcast.me_ref, bf16[832,1024]{1,0:T(8,128)(2,1)} %get-tuple-element.47.ctx_ref, f32[784,768]{1,0:T(8,128)} %x_ref.5, ...), custom_call_target="tpu_custom_call" | custom-call | flops 1300000000 | bytes 15000000 | tf_op jit(solution)/shard_map/pallas_call | solution.py:265
  186.5 38.5 %shard_map.257 = (f32[832,768]{1,0:T(8,128)}, f32[832,768]{1,0:T(8,128)}, bf16[2,8,96,768]{3,2,1,0:T(8,128)(2,1)}, bf16[2,8,96,768]{3,2,1,0:T(8,128)(2,1)}, bf16...) custom-call(s32[1]{0:T(128)} %bitcast.me_ref, ...), custom_call_target="tpu_custom_call" | custom-call | flops 23555211264 | bytes 40000000 | tf_op jit(solution)/shard_map/pallas_call | solution.py:372
  225.0 33.3 %shard_map.258 = (f32[784,768]{1,0:T(8,128)}, f32[832,768]{1,0:T(8,128)}, bf16[4,832,640]{2,1,0:T(8,128)(2,1)}, bf16[2,8,96,256]{3,2,1,0:T(8,128)(2,1)}, bf16[2,...) custom-call(s32[1]{0:T(128)} %bitcast.me_ref, ...), custom_call_target="tpu_custom_call" | custom-call | flops 12000000000 | bytes 40000000 | tf_op jit(solution)/shard_map/pallas_call | solution.py:527
  260.9 8.9 %shard_map.260 = (bf16[2,8,96,640]{3,2,1,0:T(8,128)(2,1)}, bf16[2,8,96,640]{3,2,1,0:T(8,128)(2,1)}) custom-call(s32[1]{0:T(128)} %bitcast.me_ref, bf16[832,768]{1,0:T(8,128)(2,1)} %get-tuple-element.45.n_ref, bf16[4,832,640]{2,1,0:T(8,128)(2,1)} %get-tuple-element.58.dqkv_ref), custom_call_target="tpu_custom_call" | custom-call | flops 3271557120 | bytes 10000000 | tf_op jit(solution)/shard_map/pallas_call | solution.py:588
  269.9 3.8 reshape.220
  274.9 12.0 %shard_map.259 = (f32[784,768]{1,0:T(8,128)}, f32[2,8,768]{2,1,0:T(8,128)}) custom-call(bf16[4,832,640]{2,1,0:T(8,128)(2,1)} %get-tuple-element.58.dqkv_ref, bf16[4,768,640]{2,1,0:T(8,128)(2,1)} %get-tuple-element.59.full_ref, f32[832,768]{1,0:T(8,128)} %get-tuple-element.60.gm_ref, f32[784,768]{1,0:T(8,128)} %x_ref.5, f32[12,768]{1,0:T(8,128)} %vec_ref.7), custom_call_target="tpu_custom_call" | custom-call | flops 4000000000 | bytes 15000000 | tf_op jit(solution)/shard_map/pallas_call | solution.py:618
  302.3 3.2 collective-permute-start.50
  323.8 13.6 %collective-permute-done.27 = bf16[8,96,640]{2,1,0:T(8,128)(2,1)S(1)} collective-permute-done((bf16[8,96,640]{2,1,0:T(8,128)(2,1)S(1)}, bf16[8,96,640]{2,1,0:T(8,128)(2,1)S(1)}, u32[]{:S(2)}, u32[]{:S(2)}) %collective-permute-start.27) | collective-permute-done | bytes 983072 | tf_op jit(solution)/shard_map/ppermute | solution.py:638
  340.8 7.3 %collective-permute-done.28 = bf16[4,96,640]{2,1,0:T(8,128)(2,1)S(1)} collective-permute-done((bf16[4,96,640]{2,1,0:T(8,128)(2,1)S(1)}, bf16[4,96,640]{2,1,0:T(8,128)(2,1)S(1)}, u32[]{:S(2)}, u32[]{:S(2)}) %collective-permute-start.28) | collective-permute-done | bytes 491552 | tf_op jit(solution)/shard_map/ppermute | solution.py:638
  349.8 12.9 %collective-permute-done.37 = bf16[8,96,768]{2,1,0:T(8,128)(2,1)S(1)} collective-permute-done((bf16[8,96,768]{2,1,0:T(8,128)(2,1)S(1)}, bf16[8,96,768]{2,1,0:T(8,128)(2,1)S(1)}, u32[]{:S(2)}, u32[]{:S(2)}) %collective-permute-start.37) | collective-permute-done | bytes 1179680 | tf_op jit(solution)/shard_map/ppermute | solution.py:638
  366.8 16.3 %collective-permute-done.42 = bf16[8,96,768]{2,1,0:T(8,128)(2,1)S(1)} collective-permute-done((bf16[8,96,768]{2,1,0:T(8,128)(2,1)S(1)}, bf16[8,96,768]{2,1,0:T(8,128)(2,1)S(1)}, u32[]{:S(2)}, u32[]{:S(2)}) %collective-permute-start.42) | collective-permute-done | bytes 1179680 | tf_op jit(solution)/shard_map/ppermute | solution.py:638
  386.2 8.0 %collective-permute-done.43 = bf16[4,96,768]{2,1,0:T(8,128)(2,1)S(1)} collective-permute-done((bf16[4,96,768]{2,1,0:T(8,128)(2,1)S(1)}, bf16[4,96,768]{2,1,0:T(8,128)(2,1)S(1)}, u32[]{:S(2)}, u32[]{:S(2)}) %collective-permute-start.43) | collective-permute-done | bytes 589856 | tf_op jit(solution)/shard_map/ppermute | solution.py:638
  398.5 5.7 %collective-permute-done.44 = bf16[2,96,768]{2,1,0:T(8,128)(2,1)S(1)} collective-permute-done((bf16[2,96,768]{2,1,0:T(8,128)(2,1)S(1)}, bf16[2,96,768]{2,1,0:T(8,128)(2,1)S(1)}, u32[]{:S(2)}, u32[]{:S(2)}) %collective-permute-start.44) | collective-permute-done | bytes 294944 | tf_op jit(solution)/shard_map/ppermute | solution.py:638
  404.8 6.6 %collective-permute-done.45 = bf16[1,96,768]{2,1,0:T(8,128)(2,1)S(1)} collective-permute-done((bf16[1,96,768]{2,1,0:T(8,128)(2,1)S(1)}, bf16[1,96,768]{2,1,0:T(8,128)(2,1)S(1)}, u32[]{:S(2)}, u32[]{:S(2)}) %collective-permute-start.45) | collective-permute-done | bytes 147488 | tf_op jit(solution)/shard_map/ppermute | solution.py:638
  (276 shorter events, 101.1 us)
Async XLA Ops:
  0.7 76.6 %collective-permute-start = (f32[3,857]{1,0:T(4,128)}, f32[3,857]{1,0:T(4,128)S(1)}, u32[]{:S(2)}, u32[]{:S(2)}) collective-permute-start(f32[3,857]{1,0:T(4,128)} %param.24), channel_id=1, source_target_pairs={{0,2},{1,3},{2,0},{3,1},{4,6},{5,7},{6,4},{7,5},{8,10},{9,11},{10,... | collective-permute-start | bytes 30860 | tf_op jit(solution)/shard_map/ppermute | solution.py:638
  4.8 44.1 %collective-permute-start.8 = (bf16[1,96,256]{2,1,0:T(8,128)(2,1)S(1)}, bf16[1,96,256]{2,1,0:T(8,128)(2,1)S(1)}, u32[]{:S(2)}, u32[]{:S(2)}) collective-permute-start(bf16[1,96,256]{2,1,0:T(8,128)(2,1)S(1)} %maximum_bitcast_fusion.2), channel_id=1, source_target_pairs={{0,16},{4,20},{8,24},{12,28},{16,0},{20,4},{24,8},{28,12},{1,17},{... | collective-permute-start | bytes 147464 | tf_op jit(solution)/shard_map/ppermute | solution.py:638
  26.5 21.9 %collective-permute-start.21 = (bf16[2,96,768]{2,1,0:T(8,128)(2,1)S(1)}, bf16[2,96,768]{2,1,0:T(8,128)(2,1)S(1)}, u32[]{:S(2)}, u32[]{:S(2)}) collective-permute-start(bf16[2,96,768]{2,1,0:T(8,128)(2,1)S(1)} %pad_maximum_fusion.10), channel_id=1, source_target_pairs={{0,8},{4,12},{8,0},{12,4},{16,24},{20,28},{24,16},{28,20},{1,9},{5... | collective-permute-start | bytes 884744 | tf_op jit(solution)/shard_map/ppermute | solution.py:638
  48.4 27.2 %collective-permute-start.22 = (bf16[4,96,768]{2,1,0:T(8,128)(2,1)S(1)}, bf16[4,96,768]{2,1,0:T(8,128)(2,1)S(1)}, u32[]{:S(2)}, u32[]{:S(2)}) collective-permute-start(bf16[4,96,768]{2,1,0:T(8,128)(2,1)S(1)} %pad_maximum_fusion.4), channel_id=1, source_target_pairs={{0,4},{4,0},{8,12},{12,8},{16,20},{20,16},{24,28},{28,24},{1,5},{5... | collective-permute-start | bytes 1769480 | tf_op jit(solution)/shard_map/ppermute | solution.py:638
  50.2 29.5 %collective-permute-start.6 = (bf16[8,96,640]{2,1,0:T(8,128)(2,1)}, bf16[8,96,640]{2,1,0:T(8,128)(2,1)}, u32[]{:S(2)}, u32[]{:S(2)}) collective-permute-start(bf16[8,96,640]{2,1,0:T(8,128)(2,1)} %pad_maximum_fusion.2.w0), channel_id=1, source_target_pairs={{0,2},{1,3},{2,0},{3,1},{4,6},{5,7},{6,4},{7,5},{8,10},{9,11},{10,... | collective-permute-start | bytes 2949128 | tf_op jit(solution)/shard_map/ppermute | solution.py:638
  53.7 25.2 %collective-permute-start.10 = (bf16[4,96,256]{2,1,0:T(8,128)(2,1)S(1)}, bf16[4,96,256]{2,1,0:T(8,128)(2,1)S(1)}, u32[]{:S(2)}, u32[]{:S(2)}) collective-permute-start(bf16[4,96,256]{2,1,0:T(8,128)(2,1)S(1)} %pad_maximum_fusion.12), channel_id=1, source_target_pairs={{0,4},{4,0},{8,12},{12,8},{16,20},{20,16},{24,28},{28,24},{1,5},{5... | collective-permute-start | bytes 589832 | tf_op jit(solution)/shard_map/ppermute | solution.py:638
  63.1 71.6 %collective-permute-start.18 = (bf16[8,96,768]{2,1,0:T(8,128)(2,1)S(1)}, bf16[8,96,768]{2,1,0:T(8,128)(2,1)}, u32[]{:S(2)}, u32[]{:S(2)}) collective-permute-start(bf16[8,96,768]{2,1,0:T(8,128)(2,1)S(1)} %pad_maximum_fusion.refs_0_), channel_id=1, source_target_pairs={{0,2},{1,3},{2,0},{3,1},{4,6},{5,7},{6,4},{7,5},{8,10},{9,11},{10,... | collective-permute-start | bytes 3538952 | tf_op jit(solution)/shard_map/ppermute | solution.py:638
  76.8 58.1 %collective-permute-start.24 = (bf16[8,96,768]{2,1,0:T(8,128)(2,1)}, bf16[8,96,768]{2,1,0:T(8,128)(2,1)}, u32[]{:S(2)}, u32[]{:S(2)}) collective-permute-start(bf16[8,96,768]{2,1,0:T(8,128)(2,1)} %pad_maximum_fusion.1.refs_4_), channel_id=1, source_target_pairs={{0,2},{1,3},{2,0},{3,1},{4,6},{5,7},{6,4},{7,5},{8,10},{9,11},{10,... | collective-permute-start | bytes 3538952 | tf_op jit(solution)/shard_map/ppermute | solution.py:638
  79.0 53.5 %collective-permute-start.12 = (bf16[8,96,256]{2,1,0:T(8,128)(2,1)S(1)}, bf16[8,96,256]{2,1,0:T(8,128)(2,1)S(1)}, u32[]{:S(2)}, u32[]{:S(2)}) collective-permute-start(bf16[8,96,256]{2,1,0:T(8,128)(2,1)S(1)} %pad_maximum_fusion.7.w0), channel_id=1, source_target_pairs={{0,2},{1,3},{2,0},{3,1},{4,6},{5,7},{6,4},{7,5},{8,10},{9,11},{10,... | collective-permute-start | bytes 1179656 | tf_op jit(solution)/shard_map/ppermute | solution.py:638
  79.6 54.8 %collective-permute-start.5 = (bf16[8,96,640]{2,1,0:T(8,128)(2,1)}, bf16[8,96,640]{2,1,0:T(8,128)(2,1)}, u32[]{:S(2)}, u32[]{:S(2)}) collective-permute-start(bf16[8,96,640]{2,1,0:T(8,128)(2,1)} %pad_maximum_fusion.2.w0), channel_id=1, source_target_pairs={{0,1},{1,0},{2,3},{3,2},{4,5},{5,4},{6,7},{7,6},{8,9},{9,8},{10,11... | collective-permute-start | bytes 2949128 | tf_op jit(solution)/shard_map/ppermute | solution.py:638
  79.7 75.6 %collective-permute-start.7 = (bf16[8,96,640]{2,1,0:T(8,128)(2,1)}, bf16[8,96,640]{2,1,0:T(8,128)(2,1)}, u32[]{:S(2)}, u32[]{:S(2)}) collective-permute-start(bf16[8,96,640]{2,1,0:T(8,128)(2,1)} %collective-permute-done.6.w2), channel_id=1, source_target_pairs={{0,1},{1,0},{2,3},{3,2},{4,5},{5,4},{6,7},{7,6},{8,9},{9,8},{10,11... | collective-permute-start | bytes 2949128 | tf_op jit(solution)/shard_map/ppermute | solution.py:638
  134.2 52.3 %collective-permute-start.17 = (bf16[8,96,768]{2,1,0:T(8,128)(2,1)S(1)}, bf16[8,96,768]{2,1,0:T(8,128)(2,1)}, u32[]{:S(2)}, u32[]{:S(2)}) collective-permute-start(bf16[8,96,768]{2,1,0:T(8,128)(2,1)S(1)} %pad_maximum_fusion.refs_0_), channel_id=1, source_target_pairs={{0,1},{1,0},{2,3},{3,2},{4,5},{5,4},{6,7},{7,6},{8,9},{9,8},{10,11... | collective-permute-start | bytes 3538952 | tf_op jit(solution)/shard_map/ppermute | solution.py:638
  134.3 52.1 %collective-permute-start.23 = (bf16[8,96,768]{2,1,0:T(8,128)(2,1)}, bf16[8,96,768]{2,1,0:T(8,128)(2,1)}, u32[]{:S(2)}, u32[]{:S(2)}) collective-permute-start(bf16[8,96,768]{2,1,0:T(8,128)(2,1)} %pad_maximum_fusion.1.refs_4_), channel_id=1, source_target_pairs={{0,1},{1,0},{2,3},{3,2},{4,5},{5,4},{6,7},{7,6},{8,9},{9,8},{10,11... | collective-permute-start | bytes 3538952 | tf_op jit(solution)/shard_map/ppermute | solution.py:638
  134.7 51.8 %collective-permute-start.19 = (bf16[8,96,768]{2,1,0:T(8,128)(2,1)}, bf16[8,96,768]{2,1,0:T(8,128)(2,1)}, u32[]{:S(2)}, u32[]{:S(2)}) collective-permute-start(bf16[8,96,768]{2,1,0:T(8,128)(2,1)} %collective-permute-done.18.refs_2_), channel_id=1, source_target_pairs={{0,1},{1,0},{2,3},{3,2},{4,5},{5,4},{6,7},{7,6},{8,9},{9,8},{10,11... | collective-permute-start | bytes 3538952 | tf_op jit(solution)/shard_map/ppermute | solution.py:638
  134.9 51.6 %collective-permute-start.25 = (bf16[8,96,768]{2,1,0:T(8,128)(2,1)}, bf16[8,96,768]{2,1,0:T(8,128)(2,1)}, u32[]{:S(2)}, u32[]{:S(2)}) collective-permute-start(bf16[8,96,768]{2,1,0:T(8,128)(2,1)} %collective-permute-done.24.refs_6_), channel_id=1, source_target_pairs={{0,1},{1,0},{2,3},{3,2},{4,5},{5,4},{6,7},{7,6},{8,9},{9,8},{10,11... | collective-permute-start | bytes 3538952 | tf_op jit(solution)/shard_map/ppermute | solution.py:638
  260.5 29.6 %collective-permute-start.31 = (bf16[2,8,96,256]{3,2,1,0:T(8,128)(2,1)}, bf16[2,8,96,256]{3,2,1,0:T(8,128)(2,1)}, u32[]{:S(2)}, u32[]{:S(2)}) collective-permute-start(bf16[2,8,96,256]{3,2,1,0:T(8,128)(2,1)} %get-tuple-element.65), channel_id=1, source_target_pairs={{0,1},{1,0},{2,3},{3,2},{4,5},{5,4},{6,7},{7,6},{8,9},{9,8},{10,11... | collective-permute-start | bytes 2359304 | tf_op jit(solution)/shard_map/ppermute | solution.py:638
  269.8 41.2 %collective-permute-start.26 = (bf16[2,8,96,640]{3,2,1,0:T(8,128)(2,1)}, bf16[2,8,96,640]{3,2,1,0:T(8,128)(2,1)}, u32[]{:S(2)}, u32[]{:S(2)}) collective-permute-start(bf16[2,8,96,640]{3,2,1,0:T(8,128)(2,1)} %get-tuple-element.63), channel_id=1, source_target_pairs={{0,1},{1,0},{2,3},{3,2},{4,5},{5,4},{6,7},{7,6},{8,9},{9,8},{10,11... | collective-permute-start | bytes 5898248 | tf_op jit(solution)/shard_map/ppermute | solution.py:638
  288.5 34.5 %collective-permute-start.36 = (bf16[2,8,96,768]{3,2,1,0:T(8,128)(2,1)}, bf16[2,8,96,768]{3,2,1,0:T(8,128)(2,1)S(1)}, u32[]{:S(2)}, u32[]{:S(2)}) collective-permute-start(bf16[2,8,96,768]{3,2,1,0:T(8,128)(2,1)} %get-tuple-element.67), channel_id=1, source_target_pairs={{0,1},{1,0},{2,3},{3,2},{4,5},{5,4},{6,7},{7,6},{8,9},{9,8},{10,11... | collective-permute-start | bytes 7077896 | tf_op jit(solution)/shard_map/ppermute | solution.py:638
  288.6 51.1 %collective-permute-start.41 = (bf16[2,8,96,768]{3,2,1,0:T(8,128)(2,1)}, bf16[2,8,96,768]{3,2,1,0:T(8,128)(2,1)S(1)}, u32[]{:S(2)}, u32[]{:S(2)}) collective-permute-start(bf16[2,8,96,768]{3,2,1,0:T(8,128)(2,1)} %get-tuple-element.69), channel_id=1, source_target_pairs={{0,1},{1,0},{2,3},{3,2},{4,5},{5,4},{6,7},{7,6},{8,9},{9,8},{10,11... | collective-permute-start | bytes 7077896 | tf_op jit(solution)/shard_map/ppermute | solution.py:638
  312.7 24.8 %collective-permute-start.27 = (bf16[8,96,640]{2,1,0:T(8,128)(2,1)S(1)}, bf16[8,96,640]{2,1,0:T(8,128)(2,1)S(1)}, u32[]{:S(2)}, u32[]{:S(2)}) collective-permute-start(bf16[8,96,640]{2,1,0:T(8,128)(2,1)S(1)} %fusion.2), channel_id=1, source_target_pairs={{0,2},{1,3},{2,0},{3,1},{4,6},{5,7},{6,4},{7,5},{8,10},{9,11},{10,... | collective-permute-start | bytes 2949128 | tf_op jit(solution)/shard_map/ppermute | solution.py:638
  320.0 20.7 %collective-permute-start.35 = (bf16[1,96,256]{2,1,0:T(8,128)(2,1)S(1)}, bf16[1,96,256]{2,1,0:T(8,128)(2,1)S(1)}, u32[]{:S(2)}, u32[]{:S(2)}) collective-permute-start(bf16[1,96,256]{2,1,0:T(8,128)(2,1)S(1)} %slice.657), channel_id=1, source_target_pairs={{0,16},{4,20},{8,24},{12,28},{16,0},{20,4},{24,8},{28,12},{1,17},{... | collective-permute-start | bytes 147464 | tf_op jit(solution)/shard_map/ppermute | solution.py:638
  323.3 39.5 %collective-permute-start.37 = (bf16[8,96,768]{2,1,0:T(8,128)(2,1)S(1)}, bf16[8,96,768]{2,1,0:T(8,128)(2,1)S(1)}, u32[]{:S(2)}, u32[]{:S(2)}) collective-permute-start(bf16[8,96,768]{2,1,0:T(8,128)(2,1)S(1)} %fusion), channel_id=1, source_target_pairs={{0,2},{1,3},{2,0},{3,1},{4,6},{5,7},{6,4},{7,5},{8,10},{9,11},{10,... | collective-permute-start | bytes 3538952 | tf_op jit(solution)/shard_map/ppermute | solution.py:638
  340.1 43.1 %collective-permute-start.42 = (bf16[8,96,768]{2,1,0:T(8,128)(2,1)S(1)}, bf16[8,96,768]{2,1,0:T(8,128)(2,1)S(1)}, u32[]{:S(2)}, u32[]{:S(2)}) collective-permute-start(bf16[8,96,768]{2,1,0:T(8,128)(2,1)S(1)} %fusion.1), channel_id=1, source_target_pairs={{0,2},{1,3},{2,0},{3,1},{4,6},{5,7},{6,4},{7,5},{8,10},{9,11},{10,... | collective-permute-start | bytes 3538952 | tf_op jit(solution)/shard_map/ppermute | solution.py:638
  363.2 21.2 %collective-permute-start.38 = (bf16[4,96,768]{2,1,0:T(8,128)(2,1)S(1)}, bf16[4,96,768]{2,1,0:T(8,128)(2,1)S(1)}, u32[]{:S(2)}, u32[]{:S(2)}) collective-permute-start(bf16[4,96,768]{2,1,0:T(8,128)(2,1)S(1)} %slice.647), channel_id=1, source_target_pairs={{0,4},{4,0},{8,12},{12,8},{16,20},{20,16},{24,28},{28,24},{1,5},{5... | collective-permute-start | bytes 1769480 | tf_op jit(solution)/shard_map/ppermute | solution.py:638
  (54 other events, 728.7 us)

commit v2 on v1

--- a/solution.py
+++ b/solution.py
@@ -80,14 +80,25 @@
     return pl.CostEstimate(flops=int(flops), bytes_accessed=int(moved), transcendentals=0)
 
 
-def place_rows(target, source, mine, at=None):
-    rows = source.shape[1]
-    for chunk in range(CHUNKS):
-        value = source[reversed_bits(chunk) ^ mine]
-        if at is None:
-            target[chunk * rows : (chunk + 1) * rows, :] = value
-        else:
-            target[at, chunk * rows : (chunk + 1) * rows, :] = value
+def fetch(group, table, refs, columns, target, sem, place):
+    for rows, part in table[group]:
+        for slot, (source, lead) in enumerate(part):
+            height = refs[source].shape[1]
+            chunk = target.shape[0] // CHUNKS
+            start = (reversed_bits(slot) ^ place) * chunk + rows
+            pltpu.make_async_copy(
+                refs[source].at[lead, :, columns[0] : columns[1]],
+                target.at[pl.ds(pl.multiple_of(start, 16), height), :],
+                sem,
+            ).start()
+
+
+def fetched(target, sem):
+    pltpu.make_async_copy(target, target, sem).wait()
+
+
+def anywhere():
+    return pl.BlockSpec(memory_space=pl.ANY)
 
 
 def load_image(pad, source, step):
@@ -160,15 +171,16 @@
     return jnp.where(keep, value, jnp.zeros_like(value))
 
 
-def attend_body(
-    me_ref, n_ref, bias_ref, add_ref, scale_ref, mask_ref, w0, w1, w2, w3, qkv_ref, prob_ref, ctx_ref, full_ref
-):
-    mine = me_ref[0]
+def attend_body(table, me_ref, n_ref, bias_ref, add_ref, scale_ref, mask_ref, *refs):
+    pieces = refs[:-5]
+    qkv_ref, prob_ref, ctx_ref, full_ref, sems = refs[-5:]
 
     @pl.when(pl.program_id(0) == 0)
     def _():
-        for group, piece in enumerate((w0, w1, w2, w3)):
-            place_rows(full_ref, piece, mine, group)
+        for group in range(LANES):
+            fetch(group, table, pieces, (0, PACK), full_ref.at[group], sems.at[group], me_ref[0])
+        for group in range(LANES):
+            fetched(full_ref.at[group], sems.at[group])
 
     lane = halves()
     mask = mask_ref[0]
@@ -198,11 +210,12 @@
         ctx_ref[:, group * OUT_PACK + 128 : (group + 1) * OUT_PACK] = outs[2].astype(LOW)
 
 
-def attend(mine, normed, bias, add, scale, mask, pieces, images):
+def attend(mine, normed, bias, add, scale, mask, gathered, images):
     rows, width = normed.shape
     heads = bias.shape[0]
+    pieces, table = gathered
     return pl.pallas_call(
-        attend_body,
+        functools.partial(attend_body, table),
         grid=(images,),
         in_specs=[
             pl.BlockSpec(memory_space=pltpu.SMEM),
@@ -212,7 +225,7 @@
             whole(scale.shape),
             pl.BlockSpec((1, PADDED, 128), lambda i: (i, 0, 0)),
         ]
-        + [whole(piece.shape) for piece in pieces],
+        + [anywhere()] * len(pieces),
         out_specs=[
             pl.BlockSpec((LANES, PADDED, PACK), lambda i: (0, i, 0)),
             pl.BlockSpec((1, heads, PADDED, PADDED), lambda i: (i, 0, 0, 0)),
@@ -225,21 +238,23 @@
             jax.ShapeDtypeStruct((rows, LANES * OUT_PACK), LOW),
             jax.ShapeDtypeStruct((LANES, width, PACK), LOW),
         ],
+        scratch_shapes=[pltpu.SemaphoreType.DMA((LANES,))],
         compiler_params=params(),
-        cost_estimate=cost(8e9, 2e7),
+        cost_estimate=cost(1.5e10, 2e7),
     )(mine, normed, bias, add, scale, mask, *pieces)
 
 
-def middle_body(
-    me_ref, ctx_ref, x_ref, cot_ref, vec_ref, w0, w1, w2, w3, att_ref, mid_ref, n_ref, gd_ref, cs_ref, full_ref, pad_s
-):
-    mine = me_ref[0]
+def middle_body(table, columns, me_ref, ctx_ref, x_ref, cot_ref, vec_ref, *refs):
+    pieces = refs[:-8]
+    att_ref, mid_ref, n_ref, gd_ref, cs_ref, full_ref, pad_s, sems = refs[-8:]
     step = pl.program_id(0)
 
     @pl.when(step == 0)
     def _():
-        for group, piece in enumerate((w0, w1, w2, w3)):
-            place_rows(full_ref, piece, mine, group)
+        for group in range(LANES):
+            fetch(group, table, pieces, columns, full_ref.at[group], sems.at[group], me_ref[0])
+        for group in range(LANES):
+            fetched(full_ref.at[group], sems.at[group])
         pad_s[...] = jnp.zeros_like(pad_s)
         cs_ref[...] = jnp.zeros_like(cs_ref)
 
@@ -258,12 +273,13 @@
     cs_ref[...] += fold(cot)
 
 
-def middle(mine, ctx, x, cot, vectors, pieces, images):
+def middle(mine, ctx, x, cot, vectors, gathered, columns, images):
     rows = images * PADDED
     width = x.shape[1]
+    pieces, table = gathered
     block = lambda: pl.BlockSpec((PADDED, width), lambda i: (i, 0))
     return pl.pallas_call(
-        middle_body,
+        functools.partial(middle_body, table, columns),
         grid=(images,),
         in_specs=[
             pl.BlockSpec(memory_space=pltpu.SMEM),
@@ -272,7 +288,7 @@
             whole(cot.shape),
             whole(vectors.shape),
         ]
-        + [whole(piece.shape) for piece in pieces],
+        + [anywhere()] * len(pieces),
         out_specs=[block(), block(), block(), block(), whole((8, width)), whole((LANES, width, OUT_PACK))],
         out_shape=[
             jax.ShapeDtypeStruct((rows, width), FULL),
@@ -282,9 +298,9 @@
             jax.ShapeDtypeStruct((8, width), FULL),
             jax.ShapeDtypeStruct((LANES, width, OUT_PACK), LOW),
         ],
-        scratch_shapes=[pltpu.VMEM((PADDED, width), FULL)],
+        scratch_shapes=[pltpu.VMEM((PADDED, width), FULL), pltpu.SemaphoreType.DMA((LANES,))],
         compiler_params=params(),
-        cost_estimate=cost(1.3e9, 1.5e7),
+        cost_estimate=cost(8e9, 1.5e7),
     )(mine, ctx, x, cot, vectors, *pieces)
 
 
@@ -294,34 +310,57 @@
     return values * below, below + values * density
 
 
-def feed_body(steps, blocks, me_ref, n_ref, gd_ref, ub_ref, *refs):
-    up = refs[:LANES]
-    down = refs[LANES : 2 * LANES]
-    out_ref, gn_ref, keep1, send1, keep2, send2, gub_ref, nt_s, gdt_s, up_s, down_s, act_s, gh_s = refs[
-        2 * LANES :
-    ]
+def feed_body(blocks, layout, me_ref, n_ref, gd_ref, ub_ref, *refs):
+    count = sum(part[3] for part in layout)
+    pieces = refs[:count]
+    out_ref, gn_ref, keep_ref, send_ref, gub_ref, nt_s, gdt_s, up_s, down_s, act_s, gh_s, sems = refs[count:]
     step = pl.program_id(0)
-    mine = me_ref[0]
+    place = me_ref[0]
     rows = n_ref.shape[0]
+    units = up_s.shape[3]
     per = rows // blocks
-    chunk_rows = up[0].shape[1]
+
+    def begin(group):
+        slot = group % 2
+        for index, (_, table, first, number, up_at, down_at) in enumerate(layout):
+            held = pieces[first : first + number]
+            for target, at, kind in ((up_s, up_at, 0), (down_s, down_at, 1)):
+                fetch(
+                    group,
+                    table,
+                    held,
+                    (at, at + units),
+                    target.at[slot, index],
+                    sems.at[slot, kind, index],
+                    place,
+                )
 
     @pl.when(step == 0)
     def _():
+        begin(0)
         nt_s[...] = n_ref[...].T
         gdt_s[...] = gd_ref[...].T
         out_ref[...] = jnp.zeros_like(out_ref)
         gn_ref[...] = jnp.zeros_like(gn_ref)
 
-    for piece in range(LANES):
-
-        @pl.when(step // steps == piece)
-        def _(piece=piece):
-            place_rows(up_s, up[piece], mine)
-            place_rows(down_s, down[piece], mine)
-
-    up_weight = up_s[...]
-    down_weight = down_s[...]
+    for group in range(LANES):
+
+        @pl.when(step == group)
+        def _(group=group):
+            if group + 1 < LANES:
+                begin(group + 1)
+
+    now = step % 2
+    parts = len(layout)
+    for index in range(parts):
+        for kind, target in enumerate((up_s, down_s)):
+            fetched(target.at[now, index], sems.at[now, kind, index])
+    up_weight = [up_s[now, index] for index in range(parts)]
+    down_weight = [down_s[now, index] for index in range(parts)]
+    if parts > 1:
+        up_weight = [jnp.concatenate(up_weight, axis=1)]
+        down_weight = [jnp.concatenate(down_weight, axis=1)]
+    up_weight, down_weight = up_weight[0], down_weight[0]
     unit_sums = jnp.zeros((8, up_weight.shape[1]), FULL)
     for block in range(blocks):
         part = slice(block * per, (block + 1) * per)
@@ -337,80 +376,70 @@
     gub_ref[0] = unit_sums
     grad_up = dot(nt_s[...], gh_s[...]).astype(LOW)
     grad_down = dot(gdt_s[...], act_s[...]).astype(LOW)
-    for piece in range(LANES):
-
-        @pl.when(step // steps == piece)
-        def _(piece=piece):
-            one, two = (keep1, keep2) if piece % 2 == 0 else (send1, send2)
+    chunk_rows = keep_ref.shape[2]
+    wide = grad_up.shape[1]
+    for odd, target in enumerate((keep_ref, send_ref)):
+
+        @pl.when(step % 2 == odd)
+        def _(target=target):
             for chunk in range(CHUNKS):
-                slot = reversed_bits(chunk) ^ mine
-                one[0, slot] = grad_up[chunk * chunk_rows : (chunk + 1) * chunk_rows]
-                two[0, slot] = grad_down[chunk * chunk_rows : (chunk + 1) * chunk_rows]
-
-
-def feed(mine, normed, grad_down, unit_bias, up, down, images):
+                slot = reversed_bits(chunk) ^ reversed_bits(place)
+                at = slice(chunk * chunk_rows, (chunk + 1) * chunk_rows)
+                target[0, slot, :, :wide] = grad_up[at]
+                target[0, slot, :, wide:] = grad_down[at]
+
+
+def feed(mine, normed, grad_down, unit_bias, groups, units, images):
     rows, width = normed.shape
-    _, chunk_rows, units = up[0].shape
-    sub = units if images <= 4 else units // 2
     blocks = 2 if images <= 4 else 4
-    steps = units // sub
-
-    def piece_map(piece):
-        return lambda j: (0, 0, jnp.clip(j - piece * steps, 0, steps - 1))
-
-    def keep_map(j):
-        slot = jnp.where(j >= 2 * steps, 1, 0)
-        return (slot, 0, 0, jnp.clip(j - 2 * steps * slot, 0, steps - 1))
-
-    def send_map(j):
-        slot = jnp.where(j >= 3 * steps, 1, 0)
-        return (slot, 0, 0, jnp.clip(j - steps - 2 * steps * slot, 0, steps - 1))
-
-    grad_block = (1, CHUNKS, chunk_rows, sub)
-    grads = jax.ShapeDtypeStruct((2, CHUNKS, chunk_rows, units), LOW)
-    total = LANES * steps
+    parts = len(groups)
+    sub = units // parts
+    pieces, layout = [], []
+    for (arrays, table), up_at, down_at in groups:
+        layout.append((None, table, len(pieces), len(arrays), up_at, down_at))
+        pieces.extend(arrays)
+    chunk_rows = width // CHUNKS
+    grad_block = (1, CHUNKS, chunk_rows, 2 * units)
+    grads = jax.ShapeDtypeStruct((2,) + grad_block[1:], LOW)
     return pl.pallas_call(
-        functools.partial(feed_body, steps, blocks),
-        grid=(total,),
+        functools.partial(feed_body, blocks, layout),
+        grid=(LANES,),
         in_specs=[
             pl.BlockSpec(memory_space=pltpu.SMEM),
             whole((rows, width)),
             whole((rows, width)),
-            pl.BlockSpec((1, 1, sub), lambda j: (j, 0, 0)),
+            pl.BlockSpec((1, 1, units), lambda j: (j, 0, 0)),
         ]
-        + [pl.BlockSpec((CHUNKS, chunk_rows, sub), piece_map(p)) for p in range(LANES)] * 2,
+        + [anywhere()] * len(pieces),
         out_specs=[
             whole((rows, width)),
             whole((rows, width)),
-            pl.BlockSpec(grad_block, keep_map),
-            pl.BlockSpec(grad_block, send_map),
-            pl.BlockSpec(grad_block, keep_map),
-            pl.BlockSpec(grad_block, send_map),
-            pl.BlockSpec((1, 8, sub), lambda j: (j, 0, 0)),
+            pl.BlockSpec(grad_block, lambda j: (j // 2, 0, 0, 0)),
+            pl.BlockSpec(grad_block, lambda j: (jnp.maximum(j - 1, 0) // 2, 0, 0, 0)),
+            pl.BlockSpec((1, 8, units), lambda j: (j, 0, 0)),
         ],
         out_shape=[jax.ShapeDtypeStruct((rows, width), FULL)] * 2
-        + [grads] * 4
-        + [jax.ShapeDtypeStruct((total, 8, sub), FULL)],
+        + [grads] * 2
+        + [jax.ShapeDtypeStruct((LANES, 8, units), FULL)],
         scratch_shapes=[
             pltpu.VMEM((width, rows), LOW),
             pltpu.VMEM((width, rows), LOW),
-            pltpu.VMEM((width, sub), LOW),
-            pltpu.VMEM((width, sub), LOW),
-            pltpu.VMEM((rows, sub), LOW),
-            pltpu.VMEM((rows, sub), LOW),
+            pltpu.VMEM((2, parts, width, sub), LOW),
+            pltpu.VMEM((2, parts, width, sub), LOW),
+            pltpu.VMEM((rows, units), LOW),
+            pltpu.VMEM((rows, units), LOW),
+            pltpu.SemaphoreType.DMA((2, 2, parts)),
         ],
         compiler_params=params(),
-        cost_estimate=cost(12 * rows * width * units * LANES, 4e7),
-    )(mine, normed, grad_down, unit_bias.reshape(total, 1, sub), *up, *down)
+        cost_estimate=cost(3.5e10, 4e7),
+    )(mine, normed, grad_down, unit_bias.reshape(LANES, 1, units), *pieces)
 
 
 def back_body(
-    me_ref,
     down_ref,
     gn_ref,
     mid_ref,
     att_ref,
-    ctx_ref,
     cot_ref,
     vec_ref,
     wo_ref,
@@ -419,17 +448,14 @@
     out_ref,
     gm_ref,
     dqkv_ref,
-    keep_ref,
-    send_ref,
+    ga_ref,
     spread_ref,
     sums_ref,
     cols_ref,
     pad_s,
     out_s,
-    ga_s,
     pair_s,
 ):
-    mine = me_ref[0]
     step = pl.program_id(0)
     heads = pair_s.shape[0]
 
@@ -454,7 +480,7 @@
     sums_ref[3] += fold(grad_mid * att_ref[...])
     sums_ref[4] += fold(cot * down)
     grad_att = (grad_mid * vec_ref[5:6, :]).astype(LOW)
-    ga_s[pl.ds(pl.multiple_of(step * PADDED, PADDED), PADDED), :] = grad_att
+    ga_ref[...] = grad_att
 
     lane = halves()
     for group in range(LANES):
@@ -498,14 +524,6 @@
 
     @pl.when(step == pl.num_programs(0) - 1)
     def _():
-        grad_out = dot(ga_s[...], ctx_ref[...], 0, 0).astype(LOW)
-        rows = keep_ref.shape[2]
-        for group in range(LANES):
-            target = (keep_ref, send_ref)[group % 2]
-            for chunk in range(CHUNKS):
-                target[group // 2, reversed_bits(chunk) ^ mine] = grad_out[
-                    chunk * rows : (chunk + 1) * rows, group * OUT_PACK : (group + 1) * OUT_PACK
-                ]
         spread_ref[...] = jnp.zeros_like(spread_ref)
 
         def head_sum(index, carry):
@@ -519,21 +537,18 @@
         lax.fori_loop(0, heads, head_sum, 0)
 
 
-def back(mine, down, grad_normed, mid, att, ctx, cot, vectors, wo, qkv, prob, images, chunk_rows):
+def back(down, grad_normed, mid, att, cot, vectors, wo, qkv, prob, images):
     rows, width = mid.shape
     heads = prob.shape[1]
     block = lambda: pl.BlockSpec((PADDED, width), lambda i: (i, 0))
-    grads = (2, CHUNKS, chunk_rows, OUT_PACK)
     return pl.pallas_call(
         back_body,
         grid=(images,),
         in_specs=[
-            pl.BlockSpec(memory_space=pltpu.SMEM),
             block(),
             block(),
             block(),
             block(),
-            whole(ctx.shape),
             whole(cot.shape),
             whole(vectors.shape),
             whole(wo.shape),
@@ -544,8 +559,7 @@
             whole(cot.shape),
             block(),
             pl.BlockSpec((LANES, PADDED, PACK), lambda i: (0, i, 0)),
-            whole(grads),
-            whole(grads),
+            block(),
             whole((heads, GRID, 384)),
             whole((5, 8, width)),
             whole((LANES, 8, PACK)),
@@ -554,8 +568,7 @@
             jax.ShapeDtypeStruct(cot.shape, FULL),
             jax.ShapeDtypeStruct((rows, width), FULL),
             jax.ShapeDtypeStruct((LANES, rows, PACK), LOW),
-            jax.ShapeDtypeStruct(grads, LOW),
-            jax.ShapeDtypeStruct(grads, LOW),
+            jax.ShapeDtypeStruct((rows, width), LOW),
             jax.ShapeDtypeStruct((heads, GRID, 384), FULL),
             jax.ShapeDtypeStruct((5, 8, width), FULL),
             jax.ShapeDtypeStruct((LANES, 8, PACK), FULL),
@@ -563,36 +576,44 @@
         scratch_shapes=[
             pltpu.VMEM((PADDED, width), FULL),
             pltpu.VMEM((PADDED, width), FULL),
-            pltpu.VMEM((rows, width), LOW),
             pltpu.VMEM((heads, PADDED, PADDED), FULL),
         ],
         compiler_params=params(),
-        cost_estimate=cost(1.2e10, 4e7),
-    )(mine, down, grad_normed, mid, att, ctx, cot, vectors, wo, qkv, prob)
-
-
-def project_body(me_ref, n_ref, dqkv_ref, keep_ref, send_ref, nt_s):
-    mine = me_ref[0]
-    nt_s[...] = n_ref[...].T
+        cost_estimate=cost(3e10, 4e7),
+    )(down, grad_normed, mid, att, cot, vectors, wo, qkv, prob)
+
+
+def project_body(me_ref, n_ref, dqkv_ref, ga_ref, ctx_ref, keep_ref, send_ref, t_s):
     rows = keep_ref.shape[2]
-    for group in range(LANES):
-        grad = dot(nt_s[...], dqkv_ref[group]).astype(LOW)
+    mine = reversed_bits(me_ref[0])
+
+    def give(group, grad, first):
         target = (keep_ref, send_ref)[group % 2]
         for chunk in range(CHUNKS):
-            target[group // 2, reversed_bits(chunk) ^ mine] = grad[chunk * rows : (chunk + 1) * rows]
-
-
-def project(mine, normed, dqkv, chunk_rows):
+            target[group // 2, reversed_bits(chunk) ^ mine, :, first : first + grad.shape[1]] = grad[
+                chunk * rows : (chunk + 1) * rows
+            ]
+
+    t_s[...] = ga_ref[...].T
+    for group in range(LANES):
+        at = slice(group * OUT_PACK, (group + 1) * OUT_PACK)
+        give(group, dot(t_s[...], ctx_ref[:, at]).astype(LOW), PACK)
+    t_s[...] = n_ref[...].T
+    for group in range(LANES):
+        give(group, dot(t_s[...], dqkv_ref[group]).astype(LOW), 0)
+
+
+def project(mine, normed, dqkv, grad_att, ctx):
     rows, width = normed.shape
-    grads = jax.ShapeDtypeStruct((2, CHUNKS, chunk_rows, PACK), LOW)
+    grads = jax.ShapeDtypeStruct((2, CHUNKS, width // CHUNKS, PACK + OUT_PACK), LOW)
     return pl.pallas_call(
         project_body,
-        in_specs=[pl.BlockSpec(memory_space=pltpu.SMEM)] + [pl.BlockSpec(memory_space=pltpu.VMEM)] * 2,
+        in_specs=[pl.BlockSpec(memory_space=pltpu.SMEM)] + [pl.BlockSpec(memory_space=pltpu.VMEM)] * 4,
         out_shape=[grads, grads],
         scratch_shapes=[pltpu.VMEM((width, rows), LOW)],
         compiler_params=params(),
-        cost_estimate=cost(2 * rows * width * PACK * LANES, 1e7),
-    )(mine, normed, dqkv)
+        cost_estimate=cost(8e9, 1e7),
+    )(mine, normed, dqkv, grad_att, ctx)
 
 
 def input_body(dqkv_ref, full_ref, gm_ref, x_ref, vec_ref, out_ref, sums_ref, pad_s, out_s):
@@ -638,22 +659,89 @@
     return lax.ppermute(values, axis, [(index, index ^ bit) for index in range(count)])
 
 
-def gather_near(piece):
-    held = piece[None]
-    for bit in (4, 2, 1):
+def after(values, *others):
+    return lax.optimization_barrier((values,) + others)[0]
+
+
+def z_gather(piece, *others):
+    held = after(piece, *others)[None]
+    for bit in (4, 2):
         held = jnp.concatenate([held, swap(held, "dp", bit)], axis=0)
-    far = swap(held, "mp", 2)
-    return (held, swap(held, "mp", 1), far, swap(far, "mp", 1))
-
-
-def scatter_near(keep, send):
+    return held
+
+
+def plane_one(held):
+    half = held.shape[1] // 2
+    upper, lower = held[:, :half], held[:, half:]
+    return upper, swap(upper, "dp", 1), lower, swap(lower, "mp", 2)
+
+
+def plane_two(upper, upper_y, lower, lower_x):
+    upper = jnp.concatenate([upper, upper_y], axis=0)
+    lower = jnp.concatenate([lower, lower_x], axis=0)
+    return upper, swap(upper, "mp", 2), lower, swap(lower, "dp", 1)
+
+
+def plane_core(upper, upper_x, lower, lower_y):
+    arrays = [upper, upper_x, lower, lower_y]
+    arrays = arrays + [swap(array, "mp", 1) for array in arrays]
+    half = upper.shape[1]
+
+    def part(first, far):
+        top = [(first + far, slot) for slot in range(8)]
+        low = [(first + 2 + slot // 4, 4 * far + slot % 4) for slot in range(8)]
+        return ((0, top), (half, low))
+
+    return arrays, (part(0, 0), part(4, 0), part(0, 1), part(4, 1))
+
+
+def late(state, *others):
+    return (state[0], after(state[1], *others), state[2], after(state[3], *others))
+
+
+def sum_core(keep, send):
     got = swap(send, "mp", 1)
-    near = keep[0].astype(FULL) + got[0].astype(FULL)
-    away = (keep[1].astype(FULL) + got[1].astype(FULL)).astype(LOW)
-    near = near + swap(away, "mp", 2).astype(FULL)
-    for bit, half in ((1, 4), (2, 2), (4, 1)):
-        near = near[:half] + swap(near[half:].astype(LOW), "dp", bit).astype(FULL)
-    return near[0]
+    half = keep.shape[2] // 2
+
+    def term(*at):
+        return keep[at].astype(FULL) + got[at].astype(FULL)
+
+    upper, lower = slice(0, half), slice(half, 2 * half)
+    one, two = slice(0, 4), slice(4, 8)
+    every = slice(None)
+    upper_pair = (term(0, every, upper), term(1, every, upper).astype(LOW))
+    lower_pair = (term(every, one, lower), term(every, two, lower).astype(LOW))
+    return upper_pair, lower_pair
+
+
+def sum_plane_one(pairs):
+    (upper, upper_away), (lower, lower_away) = pairs
+    upper_got = swap(upper_away, "mp", 2)
+    lower_got = swap(lower_away, "dp", 1)
+    return upper, upper_got, lower, lower_got
+
+
+def sum_plane_two(upper, upper_got, lower, lower_got):
+    upper_got, lower_got = upper_got.astype(FULL), lower_got.astype(FULL)
+    upper_next = swap((upper[4:] + upper_got[4:]).astype(LOW), "dp", 1)
+    lower_next = swap((lower[1] + lower_got[1]).astype(LOW), "mp", 2)
+    return upper[:4] + upper_got[:4], upper_next, lower[0] + lower_got[0], lower_next
+
+
+def sum_line_one(upper, upper_got, lower, lower_got):
+    here = jnp.concatenate(
+        [upper + upper_got.astype(FULL), lower + lower_got.astype(FULL)], axis=1
+    )
+    return here[:2], swap(here[2:].astype(LOW), "dp", 2)
+
+
+def sum_line_two(here, got):
+    here = here + got.astype(FULL)
+    return here[0], swap(here[1].astype(LOW)[None], "dp", 4)[0]
+
+
+def sum_end(here, got):
+    return here + got.astype(FULL)
 
 
 def adam(weight, moment_one, moment_two, incoming, step_rate, decay_rate):
@@ -727,19 +815,24 @@
 
     first, last = pack_attention(attention_weights.astype(LOW))
     mlp_low = mlp_weights.astype(LOW)
+    units = mlp_low.shape[2]
+    part = units // 2
+    second = jnp.concatenate([last, mlp_low[0, :, :part], mlp_low[1, :, :part]], axis=1)
+    third = jnp.concatenate([mlp_low[0, :, part:], mlp_low[1, :, part:]], axis=1)
     if near:
-        mine = reversed_bits(lax.axis_index("dp")).astype(jnp.int32)[None]
+        mine = lax.axis_index("dp").astype(jnp.int32)[None]
         other = swap(head_params, "mp", 2)
         both = jnp.stack([head_params, other])
         cross = swap(both, "mp", 1)
         tables = jnp.stack([both[0], cross[0], both[1], cross[1]])
         unit_bias = norm_params[8:]
-        qkv_pieces = gather_near(first)
-        out_pieces = gather_near(last)
-        up_pieces = gather_near(mlp_low[0])
-        down_pieces = gather_near(mlp_low[1])
         lanes = [lane_index ^ index for index in range(LANES)]
         unit_bias = jnp.stack([lax.dynamic_index_in_dim(unit_bias, lane, 0, False) for lane in lanes])
+        first_z = z_gather(first)
+        second_z = z_gather(second, first_z)
+        third_z = z_gather(third, second_z)
+        first_state = plane_two(*plane_one(first_z))
+        first_all = plane_core(*first_state)
     else:
         mine = jnp.zeros((1,), jnp.int32)
 
@@ -749,14 +842,15 @@
             full = full.reshape(LANES, CHUNKS, chunk_rows, piece.shape[1])
             order = [reversed_bits(index) for index in range(CHUNKS)]
             full = jnp.stack([full[:, index] for index in order], axis=1)
-            return tuple(full[index] for index in range(LANES))
+            slots = range(CHUNKS)
+            table = tuple(((0, [(group, slot) for slot in slots]),) for group in range(LANES))
+            return [full[index] for index in range(LANES)], table
 
         tables = lax.all_gather(head_params, "mp", axis=0, tiled=False)
-        qkv_pieces = gather_far(first)
-        out_pieces = gather_far(last)
-        up_pieces = gather_far(mlp_low[0])
-        down_pieces = gather_far(mlp_low[1])
         unit_bias = norm_params[8:]
+        first_all = gather_far(first)
+        second_all = gather_far(second)
+        third_all = gather_far(third)
 
     per_lane = image_size.shape[0] // LANES
     image_dims = lax.dynamic_slice_in_dim(image_size, lane_index * per_lane, per_lane, 0)
@@ -779,17 +873,36 @@
     spread = spread_table(tables[:, :, 2 * HD :].reshape(LANES * local_heads, -1))
 
     normed_one, bias = prepare(block_input, norm_params, spread, images)
-    qkv, prob, ctx, full = attend(mine, normed_one, bias, add, scale, mask, qkv_pieces, images)
+    if near:
+        second_state = plane_two(*plane_one(after(second_z, bias)))
+    qkv, prob, ctx, full = attend(mine, normed_one, bias, add, scale, mask, first_all, images)
+    if near:
+        third_state = plane_one(third_z)
+        second_all = plane_core(*late(second_state, ctx))
+        third_all = plane_core(*plane_two(*late(third_state, ctx)))
     att, mid, normed_two, grad_down, cot_sum, wo = middle(
-        mine, ctx, block_input, cotangent, norm_params, out_pieces, images
-    )
-    down, grad_normed, keep1, send1, keep2, send2, unit_sums = feed(
-        mine, normed_two, grad_down, unit_bias, up_pieces, down_pieces, images
-    )
-    output, grad_mid, dqkv, keep_out, send_out, grad_spread, sums, cols = back(
-        mine, down, grad_normed, mid, att, ctx, cotangent, norm_params, wo, qkv, prob, images, chunk_rows
-    )
-    keep_qkv, send_qkv = project(mine, normed_one, dqkv, chunk_rows)
+        mine, ctx, block_input, cotangent, norm_params, second_all, (0, OUT_PACK), images
+    )
+    groups = ((second_all, OUT_PACK, OUT_PACK + part), (third_all, 0, part))
+    down, grad_normed, keep_mlp, send_mlp, unit_sums = feed(
+        mine, normed_two, grad_down, unit_bias, groups, units, images
+    )
+    if near:
+        mlp_pairs = sum_core(keep_mlp, send_mlp)
+        mlp_terms = sum_plane_one(mlp_pairs)
+        down = after(down, mlp_pairs[0][1], mlp_pairs[1][1])
+    output, grad_mid, dqkv, grad_att, grad_spread, sums, cols = back(
+        down, grad_normed, mid, att, cotangent, norm_params, wo, qkv, prob, images
+    )
+    if near:
+        mlp_terms = sum_plane_two(*late(mlp_terms, dqkv))
+        dqkv = after(dqkv, mlp_terms[0], mlp_terms[2])
+    keep_att, send_att = project(mine, normed_one, dqkv, grad_att, ctx)
+    if near:
+        mlp_line = sum_line_one(*late(mlp_terms, send_att))
+        att_pairs = sum_core(keep_att, after(send_att, mlp_line[0]))
+        att_terms = sum_plane_one(att_pairs)
+        dqkv = after(dqkv, att_pairs[0][1], att_pairs[1][1])
     grad_input, first_sums = input_back(dqkv, full, grad_mid, block_input, norm_params, images)
 
     sums = jnp.sum(sums, axis=1)
@@ -828,19 +941,20 @@
         norms = wide(jnp.concatenate([vector_rows, placed], axis=0))
         keep = jnp.concatenate([norms, grad_heads[0], grad_heads[2]], axis=0)
         send = jnp.concatenate([norms, grad_heads[1], grad_heads[3]], axis=0)
-        small = keep + swap(send, "mp", 1)
+        small = keep + swap(after(send, att_terms[1], att_terms[3]), "mp", 1)
         rest = 12 + local_heads
         keep = small[:rest]
         send = jnp.concatenate([small[:12], small[rest:]], axis=0)
         small = keep + swap(send, "mp", 2)
         for bit in (1, 2, 4):
             small = small + swap(small, "dp", bit)
+        att_terms = sum_plane_two(*att_terms)
+        mlp_line = sum_line_two(*mlp_line)
+        att_line = sum_line_two(*sum_line_one(*att_terms))
+        sum_mlp = sum_end(*mlp_line)
+        sum_att = sum_end(*att_line)
         reduced_norms = small[:12, :width]
         reduced_heads = small[12:]
-        grad_up = scatter_near(keep1, send1)
-        grad_dn = scatter_near(keep2, send2)
-        grad_out = scatter_near(keep_out, send_out)
-        grad_qkv = scatter_near(keep_qkv, send_qkv)
     else:
         norms = jnp.concatenate([vector_rows, unit_sums], axis=0)
         reduced_norms = lax.psum(norms, ("dp", "mp"))
@@ -858,13 +972,11 @@
                 mine_only.astype(FULL), "dp", scatter_dimension=0, tiled=True
             )
 
-        grad_up = scatter_far(keep1, send1)
-        grad_dn = scatter_far(keep2, send2)
-        grad_out = scatter_far(keep_out, send_out)
-        grad_qkv = scatter_far(keep_qkv, send_qkv)
-
-    reduced_attention = unpack_attention(grad_qkv, grad_out)
-    reduced_mlp = jnp.stack([grad_up, grad_dn])
+        sum_mlp = scatter_far(keep_mlp, send_mlp)
+        sum_att = scatter_far(keep_att, send_att)
+
+    reduced_attention = unpack_attention(sum_att[:, :PACK], sum_att[:, PACK:])
+    reduced_mlp = jnp.stack([sum_mlp[:, :units], sum_mlp[:, units:]])
     attention_second_new, attention_new = adam(
         attention_weights,
         attention_first,

time: 420 us -> 326 us (0.78)
  waiting for transfers between devices: 194 us -> 89.2 us
  other arithmetic: 20.3 us -> 35.3 us
    ppermute x51, waiting for transfers between devices: 194 us -> 89.2 us  [swap(): lax.ppermute(values, axis, [(index, index ^ bit) for index in range(count)])]
    add x15 -> x13, other arithmetic: 4.15 us -> 14.9 us  [the longest x4 10.7 us: term(): return keep[at].astype(FULL) + got[at].astype(FULL)]
    another operation x15, local copies, waits for them, and re-layouts: 9.92 us -> 4.37 us  [spread_table(): flat = jnp.stack(parts, axis=1).reshape(heads, GRID, SPAN * GRID)]
  transfers between devices with their start and end apart: 51 -> 51, of which waited for: 25 -> 19; matrix products, arithmetic and copies ran while one was open for 9% -> 13% of each run, Pallas kernels for 14% -> 29%
where the time goes in v2:
time: 326 us; the launch traced here: 321 us
  Pallas kernels  128 us (39%)
  waiting for transfers between devices  89.2 us (27%)
  starting transfers between devices  46.4 us (14%)
  other arithmetic  35.3 us (11%)
  local copies, waits for them, and re-layouts  19.9 us (6%)
    ppermute x51, waiting for transfers between devices, swap(): lax.ppermute(values, axis, [(index, index ^ bit) for index in range(count)])  89.2 us
    ppermute x51, starting transfers between devices, swap(): lax.ppermute(values, axis, [(index, index ^ bit) for index in range(count)])  46.4 us
    pallas_call x1, Pallas kernels, feed(): pl.pallas_call(functools.partial(feed_body, blocks, layout), grid=(LANES,...  36.1 us
    pallas_call x1, Pallas kernels, back(): pl.pallas_call(back_body, grid=(images,), in_specs=[block(), block(), blo...  30.5 us
    pallas_call x1, Pallas kernels, attend(): pl.pallas_call(functools.partial(attend_body, table), grid=(images,), in_...  19.9 us
    pallas_call x1, Pallas kernels, project(): pl.pallas_call(project_body, in_specs=[pl.BlockSpec(memory_space=pltpu.SM...  12.4 us
    pallas_call x1, Pallas kernels, input_back(): pl.pallas_call(input_body, grid=(images,), in_specs=[pl.BlockSpec((LANES,...  11.9 us
    add x4, other arithmetic, term(): return keep[at].astype(FULL) + got[at].astype(FULL)  10.7 us
  transfers between devices with their start and end apart: 51, of which 19 were waited for; matrix products, arithmetic and copies ran while one was open for 13% of the time, Pallas kernels for 29%

profile of v2, /device:TPU:0, one launch (start us, length us, event | category | flops | bytes accessed | tf_op | source)
XLA Modules:
  0.0 320.7 jit_solution(10781145720172176882)
XLA Ops:
  0.7 3.0 collective-permute-start
  8.7 4.6 %collective-permute-done.2 = bf16[1,96,640]{2,1,0:T(8,128)(2,1)S(1)} collective-permute-done((bf16[1,96,640]{2,1,0:T(8,128)(2,1)S(1)}, bf16[1,96,640]{2,1,0:T(8,128)(2,1)S(1)}, u32[]{:S(2)}, u32[]{:S(2)}) %collective-permute-start.2) | collective-permute-done | bytes 122912 | tf_op jit(solution)/shard_map/ppermute | solution.py:659
  14.3 5.9 %collective-permute-done.3 = bf16[2,96,640]{2,1,0:T(8,128)(2,1)S(1)} collective-permute-done((bf16[2,96,640]{2,1,0:T(8,128)(2,1)S(1)}, bf16[2,96,640]{2,1,0:T(8,128)(2,1)S(1)}, u32[]{:S(2)}, u32[]{:S(2)}) %collective-permute-start.3) | collective-permute-done | bytes 245792 | tf_op jit(solution)/shard_map/ppermute | solution.py:659
  20.2 3.4 %collective-permute-start.12 = (bf16[1,96,1024]{2,1,0:T(8,128)(2,1)S(1)}, bf16[1,96,1024]{2,1,0:T(8,128)(2,1)S(1)}, u32[]{:S(2)}, u32[]{:S(2)}) collective-permute-start(bf16[1,96,1024]{2,1,0:T(8,128)(2,1)S(1)} %bitcast.135), channel_id=1, source_target_pairs={{0,16},{4,20},{8,24},{12,28},{16,0},{20,4},{24,8},{28,12},{1,17},{... | collective-permute-start | bytes 589832 | tf_op jit(solution)/shard_map/ppermute | solution.py:659
  25.9 6.6 %collective-permute-done.12 = bf16[1,96,1024]{2,1,0:T(8,128)(2,1)S(1)} collective-permute-done((bf16[1,96,1024]{2,1,0:T(8,128)(2,1)S(1)}, bf16[1,96,1024]{2,1,0:T(8,128)(2,1)S(1)}, u32[]{:S(2)}, u32[]{:S(2)}) %collective-permute-start.12) | collective-permute-done | bytes 196640 | tf_op jit(solution)/shard_map/ppermute | solution.py:659
  40.5 6.3 %shard_map.254 = (bf16[832,768]{1,0:T(8,128)(2,1)}, f32[12,208,208]{2,1,0:T(8,128)}) custom-call(f32[784,768]{1,0:T(8,128)} %x_ref.5, f32[12,768]{1,0:T(8,128)} %vec_ref.7, f32[12,14,384]{2,1,0:T(8,128)} %pad.64.spread_ref), custom_call_target="tpu_custom_call" | custom-call | flops 1000000 | bytes 8000000 | tf_op jit(solution)/shard_map/pallas_call | solution.py:145
  52.9 3.4 %collective-permute-start.22 = (bf16[1,96,768]{2,1,0:T(8,128)(2,1)S(1)}, bf16[1,96,768]{2,1,0:T(8,128)(2,1)S(1)}, u32[]{:S(2)}, u32[]{:S(2)}) collective-permute-start(bf16[1,96,768]{2,1,0:T(8,128)(2,1)S(1)} %bitcast.138), channel_id=1, source_target_pairs={{0,16},{4,20},{8,24},{12,28},{16,0},{20,4},{24,8},{28,12},{1,17},{... | collective-permute-start | bytes 442376 | tf_op jit(solution)/shard_map/ppermute | solution.py:659
  58.7 3.6 %collective-permute-done.22 = bf16[1,96,768]{2,1,0:T(8,128)(2,1)S(1)} collective-permute-done((bf16[1,96,768]{2,1,0:T(8,128)(2,1)S(1)}, bf16[1,96,768]{2,1,0:T(8,128)(2,1)S(1)}, u32[]{:S(2)}, u32[]{:S(2)}) %collective-permute-start.22) | collective-permute-done | bytes 147488 | tf_op jit(solution)/shard_map/ppermute | solution.py:659
  63.2 6.1 %collective-permute-done.16 = bf16[4,48,1024]{2,1,0:T(8,128)(2,1)S(1)} collective-permute-done((bf16[4,48,1024]{2,1,0:T(8,128)(2,1)S(1)}, bf16[4,48,1024]{2,1,0:T(8,128)(2,1)S(1)}, u32[]{:S(2)}, u32[]{:S(2)}) %collective-permute-start.16) | collective-permute-done | bytes 393248 | tf_op jit(solution)/shard_map/ppermute | solution.py:659
  77.3 19.9 %shard_map.255 = (bf16[4,832,640]{2,1,0:T(8,128)(2,1)}, bf16[4,12,208,208]{3,2,1,0:T(8,128)(2,1)}, bf16[832,1024]{1,0:T(8,128)(2,1)}, bf16[4,768,640]{2,1,0:T(8,128)(2,1)}) custom-call(s32[1]{0:T(128)} %bitcast.me_ref, bf16[832,768]{1,0:T(8,128)(2,1)} %get-tuple-element.58.n_ref, f32[12,208,208]{2,1,0:T(8,128)} %get-tuple-element.59.bias_ref, ...), custom_call_target="tpu_custom_call" | custom-call | flops 15000000512 | bytes 20000000 | tf_op jit(solution)/shard_map/pallas_call | solution.py:217
  102.8 12.7 %collective-permute-done.25.refs_9_ = bf16[8,48,768]{2,1,0:T(8,128)(2,1)} collective-permute-done((bf16[8,48,768]{2,1,0:T(8,128)(2,1)S(1)}, bf16[8,48,768]{2,1,0:T(8,128)(2,1)}, u32[]{:S(2)}, u32[]{:S(2)}) %collective-permute-start.25) | collective-permute-done | bytes 589856 | tf_op jit(solution)/shard_map/ppermute | solution.py:659
  116.4 10.5 %shard_map.256 = (f32[832,768]{1,0:T(8,128)}, f32[832,768]{1,0:T(8,128)}, bf16[832,768]{1,0:T(8,128)(2,1)}, bf16[832,768]{1,0:T(8,128)(2,1)}, f32[8,768]{1,0:T(8,128)}, /*index=5*/bf16[4,768,256]{2,1,0:T(8,128)(2,1)}) custom-call(s32[1]{0:T(128)} %bitcast.me_ref, bf16[832,1024]{1,0:T(8,128)(2,1)} %get-tuple-element.60.ctx_ref, f32[784,768]{1,0:T(8,128)} %x_ref.5, ...), custom_call_target="tpu_custom_call" | custom-call | flops 8000000000 | bytes 15000000 | tf_op jit(solution)/shard_map/pallas_call | solution.py:281
  128.0 36.1 %shard_map.257 = (f32[832,768]{1,0:T(8,128)}, f32[832,768]{1,0:T(8,128)}, bf16[2,8,96,1536]{3,2,1,0:T(8,128)(2,1)}, bf16[2,8,96,1536]{3,2,1,0:T(8,128)(2,1)}, f32[4,8,768]{2,1,0:T(8,128)}) custom-call(s32[1]{0:T(128)} %bitcast.me_ref, bf16[832,768]{1,0:T(8,128)(2,1)} %get-tuple-element.65.n_ref, bf16[832,768]{1,0:T(8,128)(2,1)} %get-tuple-element.66.gd_ref, ...), custom_call_target="tpu_custom_call" | custom-call | flops 35000000512 | bytes 40000000 | tf_op jit(solution)/shard_map/pallas_call | solution.py:404
  164.2 8.0 %collective-permute-done.32 = bf16[2,8,96,1536]{3,2,1,0:T(8,128)(2,1)S(1)} collective-permute-done((bf16[2,8,96,1536]{3,2,1,0:T(8,128)(2,1)}, bf16[2,8,96,1536]{3,2,1,0:T(8,128)(2,1)S(1)}, u32[]{:S(2)}, u32[]{:S(2)}) %collective-permute-start.32) | collective-permute-done | bytes 4718624 | tf_op jit(solution)/shard_map/ppermute | solution.py:659
  172.2 4.4 %convert_add_fusion = (f32[2,4,48,1536]{3,2,1,0:T(8,128)}, bf16[2,4,48,1536]{3,2,1,0:T(8,128)(2,1)}) fusion(bf16[2,8,96,1536]{3,2,1,0:T(8,128)(2,1)S(1)} %collective-permute-done.32, bf16[2,8,96,1536]{3,2,1,0:T(8,128)(2,1)} %get-tuple-element.71), kind=kLoop, calls=%fused_computation.2 | loop fusion | flops 4128768 | bytes 8257536 | tf_op jit(solution)/shard_map/add | solution.py:707
  181.1 30.5 %shard_map.258 = (f32[784,768]{1,0:T(8,128)}, f32[832,768]{1,0:T(8,128)}, bf16[4,832,640]{2,1,0:T(8,128)(2,1)}, bf16[832,768]{1,0:T(8,128)(2,1)}, f32[12,14,384]...) custom-call(f32[832,768]{1,0:T(8,128)} %get-tuple-element.73.down_ref, f32[832,768]{1,0:T(8,128)} %get-tuple-element.74.gn_ref, ...), custom_call_target="tpu_custom_call" | custom-call | flops 30000001024 | bytes 40000000 | tf_op jit(solution)/shard_map/pallas_call | solution.py:544
  218.9 12.4 %shard_map.259 = (bf16[2,8,96,896]{3,2,1,0:T(8,128)(2,1)}, bf16[2,8,96,896]{3,2,1,0:T(8,128)(2,1)}) custom-call(s32[1]{0:T(128)} %bitcast.me_ref, bf16[832,768]{1,0:T(8,128)(2,1)} %get-tuple-element.58.n_ref, bf16[4,832,640]{2,1,0:T(8,128)(2,1)} %get-tuple-element.91.dqkv_ref, bf16[832,768]{1,0:T(8,128)(2,1)} %get-tuple-element.85.ga_ref, ...), custom_call_target="tpu_custom_call" | custom-call | flops 8000000000 | bytes 10000000 | tf_op jit(solution)/shard_map/pallas_call | solution.py:609
  233.9 13.3 %collective-permute-done.44 = bf16[2,96,1536]{2,1,0:T(8,128)(2,1)S(1)} collective-permute-done((bf16[2,96,1536]{2,1,0:T(8,128)(2,1)S(1)}, bf16[2,96,1536]{2,1,0:T(8,128)(2,1)S(1)}, u32[]{:S(2)}, u32[]{:S(2)}) %collective-permute-start.44) | collective-permute-done | bytes 589856 | tf_op jit(solution)/shard_map/ppermute | solution.py:659
  263.8 3.4 %collective-permute-start.45 = (bf16[1,96,1536]{2,1,0:T(8,128)(2,1)}, bf16[1,96,1536]{2,1,0:T(8,128)(2,1)}, u32[]{:S(2)}, u32[]{:S(2)}) collective-permute-start(bf16[1,96,1536]{2,1,0:T(8,128)(2,1)} %slice.758), channel_id=1, source_target_pairs={{0,16},{4,20},{8,24},{12,28},{16,0},{20,4},{24,8},{28,12},{1,17},{... | collective-permute-start | bytes 884744 | tf_op jit(solution)/shard_map/ppermute | solution.py:659
  267.2 11.9 %shard_map.260 = (f32[784,768]{1,0:T(8,128)}, f32[2,8,768]{2,1,0:T(8,128)}) custom-call(bf16[4,832,640]{2,1,0:T(8,128)(2,1)} %get-tuple-element.91.dqkv_ref, bf16[4,768,640]{2,1,0:T(8,128)(2,1)} %get-tuple-element.92.full_ref, f32[832,768]{1,0:T(8,128)} %get-tuple-element.93.gm_ref, f32[784,768]{1,0:T(8,128)} %x_ref.5, f32[12,768]{1,0:T(8,128)} %vec_ref.7), custom_call_target="tpu_custom_call" | custom-call | flops 4000000000 | bytes 15000000 | tf_op jit(solution)/shard_map/pallas_call | solution.py:639
  289.3 6.5 %collective-permute-done.48 = f32[15,857]{1,0:T(8,128)S(1)} collective-permute-done((f32[15,857]{1,0:T(8,128)S(1)}, f32[15,857]{1,0:T(8,128)S(1)}, u32[]{:S(2)}, u32[]{:S(2)}) %collective-permute-start.48) | collective-permute-done | bytes 51452 | tf_op jit(solution)/shard_map/ppermute | solution.py:659
  296.2 3.9 %collective-permute-done.49 = f32[15,857]{1,0:T(8,128)S(1)} collective-permute-done((f32[15,857]{1,0:T(8,128)S(1)}, f32[15,857]{1,0:T(8,128)S(1)}, u32[]{:S(2)}, u32[]{:S(2)}) %collective-permute-start.49) | collective-permute-done | bytes 51452 | tf_op jit(solution)/shard_map/ppermute | solution.py:659
  306.5 4.2 %collective-permute-done.42 = bf16[2,96,896]{2,1,0:T(8,128)(2,1)S(1)} collective-permute-done((bf16[2,96,896]{2,1,0:T(8,128)(2,1)S(1)}, bf16[2,96,896]{2,1,0:T(8,128)(2,1)S(1)}, u32[]{:S(2)}, u32[]{:S(2)}) %collective-permute-start.42) | collective-permute-done | bytes 344096 | tf_op jit(solution)/shard_map/ppermute | solution.py:659
  312.9 5.9 %collective-permute-done.43 = bf16[1,96,896]{2,1,0:T(8,128)(2,1)S(1)} collective-permute-done((bf16[1,96,896]{2,1,0:T(8,128)(2,1)S(1)}, bf16[1,96,896]{2,1,0:T(8,128)(2,1)S(1)}, u32[]{:S(2)}, u32[]{:S(2)}) %collective-permute-start.43) | collective-permute-done | bytes 172064 | tf_op jit(solution)/shard_map/ppermute | solution.py:659
  (312 shorter events, 91.9 us)
Async XLA Ops:
  23.7 24.8 %collective-permute-start.6 = (bf16[4,48,640]{2,1,0:T(8,128)(2,1)S(1)}, bf16[4,48,640]{2,1,0:T(8,128)(2,1)}, u32[]{:S(2)}, u32[]{:S(2)}) collective-permute-start(bf16[4,48,640]{2,1,0:T(8,128)(2,1)S(1)} %get-tuple-element.148), channel_id=1, source_target_pairs={{0,2},{1,3},{2,0},{3,1},{4,6},{5,7},{6,4},{7,5},{8,10},{9,11},{10,... | collective-permute-start | bytes 737288 | tf_op jit(solution)/shard_map/ppermute | solution.py:659
  24.3 22.5 %collective-permute-start.4 = (bf16[4,48,640]{2,1,0:T(8,128)(2,1)S(1)}, bf16[4,48,640]{2,1,0:T(8,128)(2,1)}, u32[]{:S(2)}, u32[]{:S(2)}) collective-permute-start(bf16[4,48,640]{2,1,0:T(8,128)(2,1)S(1)} %get-tuple-element.149), channel_id=1, source_target_pairs={{0,4},{4,0},{8,12},{12,8},{16,20},{20,16},{24,28},{28,24},{1,5},{5... | collective-permute-start | bytes 737288 | tf_op jit(solution)/shard_map/ppermute | solution.py:659
  33.3 18.5 %collective-permute-start.13 = (bf16[2,96,1024]{2,1,0:T(8,128)(2,1)}, bf16[2,96,1024]{2,1,0:T(8,128)(2,1)}, u32[]{:S(2)}, u32[]{:S(2)}) collective-permute-start(bf16[2,96,1024]{2,1,0:T(8,128)(2,1)} %pad_maximum_fusion.12), channel_id=1, source_target_pairs={{0,8},{4,12},{8,0},{12,4},{16,24},{20,28},{24,16},{28,20},{1,9},{5... | collective-permute-start | bytes 1179656 | tf_op jit(solution)/shard_map/ppermute | solution.py:659
  47.9 21.4 %collective-permute-start.5 = (bf16[8,48,640]{2,1,0:T(8,128)(2,1)S(1)}, bf16[8,48,640]{2,1,0:T(8,128)(2,1)}, u32[]{:S(2)}, u32[]{:S(2)}) collective-permute-start(bf16[8,48,640]{2,1,0:T(8,128)(2,1)S(1)} %pad_maximum_fusion.10.refs_0_), channel_id=1, source_target_pairs={{0,2},{1,3},{2,0},{3,1},{4,6},{5,7},{6,4},{7,5},{8,10},{9,11},{10,... | collective-permute-start | bytes 1474568 | tf_op jit(solution)/shard_map/ppermute | solution.py:659
  50.3 19.6 %collective-permute-start.7 = (bf16[8,48,640]{2,1,0:T(8,128)(2,1)}, bf16[8,48,640]{2,1,0:T(8,128)(2,1)}, u32[]{:S(2)}, u32[]{:S(2)}) collective-permute-start(bf16[8,48,640]{2,1,0:T(8,128)(2,1)} %pad_maximum_fusion.11.refs_2_), channel_id=1, source_target_pairs={{0,4},{4,0},{8,12},{12,8},{16,20},{20,16},{24,28},{28,24},{1,5},{5... | collective-permute-start | bytes 1474568 | tf_op jit(solution)/shard_map/ppermute | solution.py:659
  71.6 29.0 %collective-permute-start.18 = (bf16[8,48,1024]{2,1,0:T(8,128)(2,1)S(1)}, bf16[8,48,1024]{2,1,0:T(8,128)(2,1)}, u32[]{:S(2)}, u32[]{:S(2)}) collective-permute-start(bf16[8,48,1024]{2,1,0:T(8,128)(2,1)S(1)} %pad_maximum_fusion.2.refs_0_), channel_id=1, source_target_pairs={{0,1},{1,0},{2,3},{3,2},{4,5},{5,4},{6,7},{7,6},{8,9},{9,8},{10,11... | collective-permute-start | bytes 2359304 | tf_op jit(solution)/shard_map/ppermute | solution.py:659
  72.3 27.1 %collective-permute-start.15 = (bf16[8,48,1024]{2,1,0:T(8,128)(2,1)S(1)}, bf16[8,48,1024]{2,1,0:T(8,128)(2,1)}, u32[]{:S(2)}, u32[]{:S(2)}) collective-permute-start(bf16[8,48,1024]{2,1,0:T(8,128)(2,1)S(1)} %pad_maximum_fusion.2.refs_0_), channel_id=1, source_target_pairs={{0,2},{1,3},{2,0},{3,1},{4,6},{5,7},{6,4},{7,5},{8,10},{9,11},{10,... | collective-permute-start | bytes 2359304 | tf_op jit(solution)/shard_map/ppermute | solution.py:659
  73.8 25.5 %collective-permute-start.17 = (bf16[8,48,1024]{2,1,0:T(8,128)(2,1)S(1)}, bf16[8,48,1024]{2,1,0:T(8,128)(2,1)}, u32[]{:S(2)}, u32[]{:S(2)}) collective-permute-start(bf16[8,48,1024]{2,1,0:T(8,128)(2,1)S(1)} %pad_maximum_fusion.3.refs_2_), channel_id=1, source_target_pairs={{0,4},{4,0},{8,12},{12,8},{16,20},{20,16},{24,28},{28,24},{1,5},{5... | collective-permute-start | bytes 2359304 | tf_op jit(solution)/shard_map/ppermute | solution.py:659
  75.4 22.8 %collective-permute-start.26 = (bf16[4,48,768]{2,1,0:T(8,128)(2,1)S(1)}, bf16[4,48,768]{2,1,0:T(8,128)(2,1)S(1)}, u32[]{:S(2)}, u32[]{:S(2)}) collective-permute-start(bf16[4,48,768]{2,1,0:T(8,128)(2,1)S(1)} %get-tuple-element.146), channel_id=1, source_target_pairs={{0,2},{1,3},{2,0},{3,1},{4,6},{5,7},{6,4},{7,5},{8,10},{9,11},{10,... | collective-permute-start | bytes 884744 | tf_op jit(solution)/shard_map/ppermute | solution.py:659
  75.9 23.4 %collective-permute-start.24 = (bf16[4,48,768]{2,1,0:T(8,128)(2,1)S(1)}, bf16[4,48,768]{2,1,0:T(8,128)(2,1)S(1)}, u32[]{:S(2)}, u32[]{:S(2)}) collective-permute-start(bf16[4,48,768]{2,1,0:T(8,128)(2,1)S(1)} %get-tuple-element.147), channel_id=1, source_target_pairs={{0,4},{4,0},{8,12},{12,8},{16,20},{20,16},{24,28},{28,24},{1,5},{5... | collective-permute-start | bytes 884744 | tf_op jit(solution)/shard_map/ppermute | solution.py:659
  99.3 16.7 %collective-permute-start.19 = (bf16[8,48,1024]{2,1,0:T(8,128)(2,1)}, bf16[8,48,1024]{2,1,0:T(8,128)(2,1)}, u32[]{:S(2)}, u32[]{:S(2)}) collective-permute-start(bf16[8,48,1024]{2,1,0:T(8,128)(2,1)} %collective-permute-done.15.refs_1_), channel_id=1, source_target_pairs={{0,1},{1,0},{2,3},{3,2},{4,5},{5,4},{6,7},{7,6},{8,9},{9,8},{10,11... | collective-permute-start | bytes 2359304 | tf_op jit(solution)/shard_map/ppermute | solution.py:659
  99.4 17.0 %collective-permute-start.21 = (bf16[8,48,1024]{2,1,0:T(8,128)(2,1)}, bf16[8,48,1024]{2,1,0:T(8,128)(2,1)}, u32[]{:S(2)}, u32[]{:S(2)}) collective-permute-start(bf16[8,48,1024]{2,1,0:T(8,128)(2,1)} %collective-permute-done.17.refs_3_), channel_id=1, source_target_pairs={{0,1},{1,0},{2,3},{3,2},{4,5},{5,4},{6,7},{7,6},{8,9},{9,8},{10,11... | collective-permute-start | bytes 2359304 | tf_op jit(solution)/shard_map/ppermute | solution.py:659
  100.0 15.5 %collective-permute-start.25 = (bf16[8,48,768]{2,1,0:T(8,128)(2,1)S(1)}, bf16[8,48,768]{2,1,0:T(8,128)(2,1)}, u32[]{:S(2)}, u32[]{:S(2)}) collective-permute-start(bf16[8,48,768]{2,1,0:T(8,128)(2,1)S(1)} %pad_maximum_fusion.6.refs_8_), channel_id=1, source_target_pairs={{0,2},{1,3},{2,0},{3,1},{4,6},{5,7},{6,4},{7,5},{8,10},{9,11},{10,... | collective-permute-start | bytes 1769480 | tf_op jit(solution)/shard_map/ppermute | solution.py:659
  100.6 15.3 %collective-permute-start.27 = (bf16[8,48,768]{2,1,0:T(8,128)(2,1)S(1)}, bf16[8,48,768]{2,1,0:T(8,128)(2,1)S(1)}, u32[]{:S(2)}, u32[]{:S(2)}) collective-permute-start(bf16[8,48,768]{2,1,0:T(8,128)(2,1)S(1)} %pad_maximum_fusion.7.refs_10_), channel_id=1, source_target_pairs={{0,4},{4,0},{8,12},{12,8},{16,20},{20,16},{24,28},{28,24},{1,5},{5... | collective-permute-start | bytes 1769480 | tf_op jit(solution)/shard_map/ppermute | solution.py:659
  102.8 24.1 %collective-permute-start.28 = (bf16[8,48,768]{2,1,0:T(8,128)(2,1)S(1)}, bf16[8,48,768]{2,1,0:T(8,128)(2,1)S(1)}, u32[]{:S(2)}, u32[]{:S(2)}) collective-permute-start(bf16[8,48,768]{2,1,0:T(8,128)(2,1)S(1)} %pad_maximum_fusion.6.refs_8_), channel_id=1, source_target_pairs={{0,1},{1,0},{2,3},{3,2},{4,5},{5,4},{6,7},{7,6},{8,9},{9,8},{10,11... | collective-permute-start | bytes 1769480 | tf_op jit(solution)/shard_map/ppermute | solution.py:659
  176.6 35.0 %collective-permute-start.34 = (bf16[2,4,48,1536]{3,2,1,0:T(8,128)(2,1)}, bf16[2,4,48,1536]{3,2,1,0:T(8,128)(2,1)S(1)}, u32[]{:S(2)}, u32[]{:S(2)}) collective-permute-start(bf16[2,4,48,1536]{3,2,1,0:T(8,128)(2,1)} %get-tuple-element.117), channel_id=1, source_target_pairs={{0,4},{4,0},{8,12},{12,8},{16,20},{20,16},{24,28},{28,24},{1,5},{5... | collective-permute-start | bytes 3538952 | tf_op jit(solution)/shard_map/ppermute | solution.py:659
  179.8 35.4 %collective-permute-start.33 = (bf16[8,48,1536]{2,1,0:T(8,128)(2,1)}, bf16[8,48,1536]{2,1,0:T(8,128)(2,1)}, u32[]{:S(2)}, u32[]{:S(2)}) collective-permute-start(bf16[8,48,1536]{2,1,0:T(8,128)(2,1)} %get-tuple-element.119), channel_id=1, source_target_pairs={{0,2},{1,3},{2,0},{3,1},{4,6},{5,7},{6,4},{7,5},{8,10},{9,11},{10,... | collective-permute-start | bytes 3538952 | tf_op jit(solution)/shard_map/ppermute | solution.py:659
  214.4 16.8 %collective-permute-start.36 = (bf16[4,48,1536]{2,1,0:T(8,128)(2,1)}, bf16[4,48,1536]{2,1,0:T(8,128)(2,1)}, u32[]{:S(2)}, u32[]{:S(2)}) collective-permute-start(bf16[4,48,1536]{2,1,0:T(8,128)(2,1)} %get-tuple-element.126), channel_id=1, source_target_pairs={{0,2},{1,3},{2,0},{3,1},{4,6},{5,7},{6,4},{7,5},{8,10},{9,11},{10,... | collective-permute-start | bytes 1769480 | tf_op jit(solution)/shard_map/ppermute | solution.py:659
  218.4 14.7 %collective-permute-start.35 = (bf16[4,48,1536]{2,1,0:T(8,128)(2,1)}, bf16[4,48,1536]{2,1,0:T(8,128)(2,1)S(1)}, u32[]{:S(2)}, u32[]{:S(2)}) collective-permute-start(bf16[4,48,1536]{2,1,0:T(8,128)(2,1)} %get-tuple-element.124), channel_id=1, source_target_pairs={{0,4},{4,0},{8,12},{12,8},{16,20},{20,16},{24,28},{28,24},{1,5},{5... | collective-permute-start | bytes 1769480 | tf_op jit(solution)/shard_map/ppermute | solution.py:659
  233.4 13.9 %collective-permute-start.44 = (bf16[2,96,1536]{2,1,0:T(8,128)(2,1)S(1)}, bf16[2,96,1536]{2,1,0:T(8,128)(2,1)S(1)}, u32[]{:S(2)}, u32[]{:S(2)}) collective-permute-start(bf16[2,96,1536]{2,1,0:T(8,128)(2,1)S(1)} %fusion.2), channel_id=1, source_target_pairs={{0,8},{4,12},{8,0},{12,4},{16,24},{20,28},{24,16},{28,20},{1,9},{5... | collective-permute-start | bytes 1769480 | tf_op jit(solution)/shard_map/ppermute | solution.py:659
  256.1 24.7 %collective-permute-start.40 = (bf16[2,4,48,896]{3,2,1,0:T(8,128)(2,1)S(1)}, bf16[2,4,48,896]{3,2,1,0:T(8,128)(2,1)}, u32[]{:S(2)}, u32[]{:S(2)}) collective-permute-start(bf16[2,4,48,896]{3,2,1,0:T(8,128)(2,1)S(1)} %get-tuple-element.121), channel_id=1, source_target_pairs={{0,4},{4,0},{8,12},{12,8},{16,20},{20,16},{24,28},{28,24},{1,5},{5... | collective-permute-start | bytes 2064392 | tf_op jit(solution)/shard_map/ppermute | solution.py:659
  260.2 20.6 %collective-permute-start.38 = (bf16[8,48,896]{2,1,0:T(8,128)(2,1)}, bf16[8,48,896]{2,1,0:T(8,128)(2,1)}, u32[]{:S(2)}, u32[]{:S(2)}) collective-permute-start(bf16[8,48,896]{2,1,0:T(8,128)(2,1)} %get-tuple-element.123), channel_id=1, source_target_pairs={{0,2},{1,3},{2,0},{3,1},{4,6},{5,7},{6,4},{7,5},{8,10},{9,11},{10,... | collective-permute-start | bytes 2064392 | tf_op jit(solution)/shard_map/ppermute | solution.py:659
  263.8 17.1 %collective-permute-start.45 = (bf16[1,96,1536]{2,1,0:T(8,128)(2,1)}, bf16[1,96,1536]{2,1,0:T(8,128)(2,1)}, u32[]{:S(2)}, u32[]{:S(2)}) collective-permute-start(bf16[1,96,1536]{2,1,0:T(8,128)(2,1)} %slice.758), channel_id=1, source_target_pairs={{0,16},{4,20},{8,24},{12,28},{16,0},{20,4},{24,8},{28,12},{1,17},{... | collective-permute-start | bytes 884744 | tf_op jit(solution)/shard_map/ppermute | solution.py:659
  284.4 16.8 %collective-permute-start.39 = (bf16[4,48,896]{2,1,0:T(8,128)(2,1)S(1)}, bf16[4,48,896]{2,1,0:T(8,128)(2,1)S(1)}, u32[]{:S(2)}, u32[]{:S(2)}) collective-permute-start(bf16[4,48,896]{2,1,0:T(8,128)(2,1)S(1)} %fusion.13), channel_id=1, source_target_pairs={{0,4},{4,0},{8,12},{12,8},{16,20},{20,16},{24,28},{28,24},{1,5},{5... | collective-permute-start | bytes 1032200 | tf_op jit(solution)/shard_map/ppermute | solution.py:659
  (75 other events, 612.2 us)

commit v3 on v2

v3 whole, which is shorter than its diff:
```python
import functools

import jax
import jax.numpy as jnp
import numpy as np
from jax import lax
from jax.experimental import pallas as pl
from jax.experimental.pallas import tpu as pltpu
from jax.sharding import PartitionSpec as P

HD = 64
GRID = 14
SPAN = 2 * GRID - 1
STEP = 10
PATCHES = 196
PADDED = 208
PACK = 640
OUT_PACK = 256
CHUNKS = 8
LANES = 4
HEADS_LANE = 3
TWO = 2
TABLE = 768
SPREAD = 384

EPSILON = 1e-06
NEGATIVE = -1e30
BETA_ONE = 0.9
BETA_TWO = 0.999
ADAM_EPSILON = 1e-08
RATE_MATRIX = 0.05
RATE_VECTOR = 0.4
DECAY_MATRIX = 0.05

LOW = jnp.bfloat16
FULL = jnp.float32
INV_SQRT2 = 0.7071067811865476
INV_SQRT2PI = 0.3989422804014327
VMEM_LIMIT = 60 << 20


def dot(former, latter, former_dim=1, latter_dim=0):
    return lax.dot_general(
        former,
        latter,
        (((former_dim,), (latter_dim,)), ((), ())),
        preferred_element_type=FULL,
    )


def normalise(values):
    row_mean = jnp.mean(values, axis=-1, keepdims=True)
    centre = values - row_mean
    variance = jnp.mean(centre * centre, axis=-1, keepdims=True)
    inverse = lax.rsqrt(variance + EPSILON)
    return centre * inverse, inverse


def norm_back(incoming, norm_gain, scaled, inverse):
    weighted = incoming * norm_gain
    centred = weighted - jnp.mean(weighted, axis=-1, keepdims=True)
    return inverse * (centred - scaled * jnp.mean(weighted * scaled, axis=-1, keepdims=True))


def fold(values):
    rows, cols = values.shape
    return jnp.sum(values.reshape(rows // 8, 8, cols), axis=0)


def reversed_bits(index):
    return (index & 1) * 4 + (index & 2) + (index & 4) // 4


def whole(shape):
    zeros = (0,) * len(shape)
    return pl.BlockSpec(tuple(shape), lambda *_: zeros)


def params():
    return pltpu.CompilerParams(vmem_limit_bytes=VMEM_LIMIT)


def cost(flops, moved):
    return pl.CostEstimate(flops=int(flops), bytes_accessed=int(moved), transcendentals=0)


def fetch(group, table, refs, columns, target, sem, place):
    for rows, part in table[group]:
        for slot, (source, lead) in enumerate(part):
            height = refs[source].shape[1]
            chunk = target.shape[0] // CHUNKS
            start = (reversed_bits(slot) ^ place) * chunk + rows
            pltpu.make_async_copy(
                refs[source].at[lead, :, columns[0] : columns[1]],
                target.at[pl.ds(pl.multiple_of(start, 16), height), :],
                sem,
            ).start()


def fetched(target, sem):
    pltpu.make_async_copy(target, target, sem).wait()


def anywhere():
    return pl.BlockSpec(memory_space=pl.ANY)


def load_images(pad, source, step):
    count = pad.shape[0] // PADDED
    for first in range(0, source.shape[0] // PATCHES, count):

        @pl.when(step == first // count)
        def _(first=first):
            for index in range(count):
                at = (first + index) * PATCHES
                pad[index * PADDED : index * PADDED + PATCHES, :] = source[at : at + PATCHES, :]

    return pad[...]


def store_images(target, pad, value, step):
    count = pad.shape[0] // PADDED
    pad[...] = value
    for first in range(0, target.shape[0] // PATCHES, count):

        @pl.when(step == first // count)
        def _(first=first):
            for index in range(count):
                at = (first + index) * PATCHES
                target[at : at + PATCHES, :] = pad[index * PADDED : index * PADDED + PATCHES, :]


def first_norm_body(images, x_ref, cot_ref, vec_ref, normed_ref, gd_ref, pad_s):
    pad_s[...] = jnp.zeros_like(pad_s)
    for image in range(images):
        rows = slice(image * PATCHES, (image + 1) * PATCHES)
        target = slice(image * PADDED, (image + 1) * PADDED)
        scaled, _ = normalise(x_ref[rows, :])
        pad_s[0:PATCHES, :] = scaled * vec_ref[0:1, :] + vec_ref[1:2, :]
        normed_ref[target, :] = pad_s[...].astype(LOW)
        pad_s[0:PATCHES, :] = cot_ref[rows, :] * vec_ref[7:8, :]
        gd_ref[target, :] = pad_s[...].astype(LOW)


def first_norm(x, cot, vectors, images):
    width = x.shape[1]
    return pl.pallas_call(
        functools.partial(first_norm_body, images),
        out_shape=[jax.ShapeDtypeStruct((images * PADDED, width), LOW)] * 2,
        scratch_shapes=[pltpu.VMEM((PADDED, width), FULL)],
        compiler_params=params(),
        cost_estimate=cost(3e9, 4e6),
    )(x, cot, vectors)


def thin_matrix():
    matrix = np.zeros((TABLE, SPREAD), np.float32)
    for row in range(SPAN):
        for col in range(GRID):
            matrix[row * SPAN + col, row * GRID + col] = 1.0
    return matrix


def exact_dot(values, onehot, latter_dim=0):
    high = values.astype(LOW)
    rest = values - high.astype(FULL)
    mid = rest.astype(LOW)
    low = (rest - mid.astype(FULL)).astype(LOW)
    return (
        dot(high, onehot, 1, latter_dim)
        + dot(mid, onehot, 1, latter_dim)
        + dot(low, onehot, 1, latter_dim)
    )


def turn(values, shift):
    return pltpu.roll(values, shift % values.shape[1], 1)


def bias_body(t0, t1, t2, t3, thin_ref, bias_ref, add_ref, table_s, turned_s, spread_s):
    table_s[...] = jnp.zeros_like(table_s)
    for group, table in enumerate((t0, t1, t2, t3)):
        heads = slice(group * HEADS_LANE, (group + 1) * HEADS_LANE)
        table_s[heads, 0 : SPAN * SPAN] = table[:, 2 * HD :]
        rows = [table[head : head + 1, :HD] for head in range(HEADS_LANE)]
        more = [table[head : head + 1, HD : 2 * HD] for head in range(HEADS_LANE)]
        add_ref[group] = jnp.concatenate(
            rows + [more[2], more[0], more[1], jnp.zeros((1, PACK - 384), FULL)], axis=1
        )
    table = table_s[...]
    for col in range(GRID):
        turned_s[16 * col : 16 * (col + 1), :] = turn(table, col - (GRID - 1))
    spread = exact_dot(turned_s[...], thin_ref[...])
    for col in range(GRID):
        spread_s[:, col, :] = spread[16 * col : 16 * (col + 1)]

    def head(index, carry):
        bias_ref[index] = jnp.zeros(bias_ref.shape[1:], FULL)
        for row in range(GRID):
            start = GRID * (GRID - 1 - row)
            bias_ref[index, row * GRID : (row + 1) * GRID, 0:PATCHES] = spread_s[
                index, :, start : start + PATCHES
            ]
        return carry

    lax.fori_loop(0, bias_ref.shape[0], head, 0)


def spread_bias(tables, thin):
    heads = LANES * HEADS_LANE
    return pl.pallas_call(
        bias_body,
        out_shape=[
            jax.ShapeDtypeStruct((heads, PADDED, PADDED), FULL),
            jax.ShapeDtypeStruct((LANES, 1, PACK), FULL),
        ],
        scratch_shapes=[
            pltpu.VMEM((16, TABLE), FULL),
            pltpu.VMEM((16 * GRID, TABLE), FULL),
            pltpu.VMEM((16, GRID, SPREAD), FULL),
        ],
        compiler_params=params(),
        cost_estimate=cost(3e9, 4e6),
    )(*tables, thin)


Q_TILE = (0, 0, 1)
K_TILE = (3, 3, 4)
V_TILE = (2, 2, 1)
QK_ODD = (False, True, False)
V_ODD = (False, True, True)


def grid_places():
    position = np.arange(PADDED)
    row = np.where(position < PATCHES, position // GRID, 4 * GRID)
    places = np.stack([row, position % GRID]).astype(np.int32)
    return np.broadcast_to(places[:, :, None], (2, PADDED, 128)).copy()


def halves():
    lane = lax.broadcasted_iota(jnp.int32, (PADDED, 128), 1)
    return lane


def half_of(value, lane, odd):
    keep = lane >= HD if odd else lane < HD
    return jnp.where(keep, value, jnp.zeros_like(value))


def attend_body(table, images, me_ref, size_ref, grid_ref, n_ref, bias_ref, add_ref, *refs):
    pieces = refs[:-5]
    qkv_ref, prob_ref, ctx_ref, weight_s, sems = refs[-5:]
    step = pl.program_id(0)

    @pl.when(step == 0)
    def _():
        for group in range(LANES):
            fetch(group, table, pieces, (0, PACK), weight_s.at[group], sems.at[group], me_ref[0])

    fetched(weight_s.at[step], sems.at[step])
    scale = jnp.where(
        lax.broadcasted_iota(jnp.int32, (1, PACK), 1) < HEADS_LANE * HD, HD**-0.5, 1.0
    )
    acc = dot(n_ref[...], weight_s[step])
    qkv_ref[0] = ((acc + add_ref[0]) * scale).astype(LOW)

    lane = halves()
    masks = []
    for image in range(images):
        index = me_ref[2] * images + image
        inside = (grid_ref[0] < size_ref[index, 0]) & (grid_ref[1] < size_ref[index, 1])
        masks.append(jnp.where(inside, 0.0, NEGATIVE).astype(LOW))
    zero = jnp.zeros_like(masks[0])
    one = jnp.ones_like(masks[0])

    def tile(image, index):
        return qkv_ref[0, image * PADDED : (image + 1) * PADDED, 128 * index : 128 * (index + 1)]

    def score(image, head):
        odd = QK_ODD[head]
        mark = 0 if odd else HD
        keep = lane >= HD if odd else lane < HD
        key = jnp.where(
            keep, tile(image, K_TILE[head]), jnp.where(lane == mark, masks[image], zero)
        )
        query = jnp.where(lane == mark, one, tile(image, Q_TILE[head]))
        return dot(key, query, 1, 1) + bias_ref[head]

    def soften(scores, image, head):
        top = jnp.max(scores, axis=0, keepdims=True)
        exponent = jnp.exp(scores - top)
        total = jnp.sum(exponent, axis=0, keepdims=True)
        prob = (exponent * (1.0 / total)).astype(LOW)
        prob_ref[image, head] = prob
        return prob

    def gather(prob, image, head):
        return dot(prob, half_of(tile(image, V_TILE[head]), lane, V_ODD[head]), 0, 0)

    work = [(image, head) for image in range(images) for head in range(HEADS_LANE)]
    scores, probs, outs = {}, {}, {}
    for turn_index in range(len(work) + 2):
        if turn_index < len(work):
            scores[turn_index] = score(*work[turn_index])
        if 0 <= turn_index - 1 < len(work):
            probs[turn_index - 1] = soften(scores.pop(turn_index - 1), *work[turn_index - 1])
        done = turn_index - 2
        if done >= 0:
            image, head = work[done]
            outs[head] = gather(probs.pop(done), image, head)
            if head == HEADS_LANE - 1:
                rows = slice(image * PADDED, (image + 1) * PADDED)
                ctx_ref[rows, :128] = (outs[0] + outs[1]).astype(LOW)
                ctx_ref[rows, 128:] = outs[2].astype(LOW)


def attend(mine, sizes, normed, bias, add, gathered, images):
    rows, width = normed.shape
    heads = bias.shape[0]
    pieces, table = gathered
    return pl.pallas_call(
        functools.partial(attend_body, table, images),
        grid=(LANES,),
        in_specs=[
            pl.BlockSpec(memory_space=pltpu.SMEM),
            pl.BlockSpec(memory_space=pltpu.SMEM),
            whole((2, PADDED, 128)),
            whole(normed.shape),
            pl.BlockSpec((HEADS_LANE, PADDED, PADDED), lambda g: (g, 0, 0)),
            pl.BlockSpec((1, 1, PACK), lambda g: (g, 0, 0)),
        ]
        + [anywhere()] * len(pieces),
        out_specs=[
            pl.BlockSpec((1, rows, PACK), lambda g: (g, 0, 0)),
            pl.BlockSpec((images, HEADS_LANE, PADDED, PADDED), lambda g: (0, g, 0, 0)),
            pl.BlockSpec((rows, OUT_PACK), lambda g: (0, g)),
        ],
        out_shape=[
            jax.ShapeDtypeStruct((LANES, rows, PACK), LOW),
            jax.ShapeDtypeStruct((images, heads, PADDED, PADDED), LOW),
            jax.ShapeDtypeStruct((rows, LANES * OUT_PACK), LOW),
        ],
        scratch_shapes=[
            pltpu.VMEM((LANES, width, PACK), LOW),
            pltpu.SemaphoreType.DMA((LANES,)),
        ],
        compiler_params=params(),
        cost_estimate=cost(1.5e10, 2e7),
    )(mine, sizes, jnp.asarray(grid_places()), normed, bias, add, *pieces)


def middle_body(table, columns, me_ref, ctx_ref, x_ref, vec_ref, *refs):
    pieces = refs[:-6]
    att_ref, mid_ref, n_ref, weight_s, pad_s, sems = refs[-6:]
    step = pl.program_id(0)

    @pl.when(step == 0)
    def _():
        for group in range(LANES):
            fetch(group, table, pieces, columns, weight_s.at[group], sems.at[group], me_ref[0])
        for group in range(LANES):
            fetched(weight_s.at[group], sems.at[group])
        pad_s[...] = jnp.zeros_like(pad_s)

    total = vec_ref[4:5, :]
    for group in range(LANES):
        total = total + dot(
            ctx_ref[:, group * OUT_PACK : (group + 1) * OUT_PACK], weight_s[group], 1, 1
        )
    att_ref[...] = total.astype(LOW)
    mid = load_images(pad_s, x_ref, step) + vec_ref[5:6, :] * total
    mid_ref[...] = mid
    scaled, _ = normalise(mid)
    n_ref[...] = (scaled * vec_ref[2:3, :] + vec_ref[3:4, :]).astype(LOW)


def middle(mine, ctx, x, vectors, gathered, columns, images):
    rows = images * PADDED
    width = x.shape[1]
    pieces, table = gathered
    block = lambda: pl.BlockSpec((TWO * PADDED, width), lambda i: (i, 0))
    return pl.pallas_call(
        functools.partial(middle_body, table, columns),
        grid=(images // TWO,),
        in_specs=[
            pl.BlockSpec(memory_space=pltpu.SMEM),
            pl.BlockSpec((TWO * PADDED, LANES * OUT_PACK), lambda i: (i, 0)),
            whole(x.shape),
            whole(vectors.shape),
        ]
        + [anywhere()] * len(pieces),
        out_specs=[block(), block(), block()],
        out_shape=[
            jax.ShapeDtypeStruct((rows, width), LOW),
            jax.ShapeDtypeStruct((rows, width), FULL),
            jax.ShapeDtypeStruct((rows, width), LOW),
        ],
        scratch_shapes=[
            pltpu.VMEM((LANES, width, OUT_PACK), LOW),
            pltpu.VMEM((TWO * PADDED, width), FULL),
            pltpu.SemaphoreType.DMA((LANES,)),
        ],
        compiler_params=params(),
        cost_estimate=cost(8e9, 1.5e7),
    )(mine, ctx, x, vectors, *pieces)


def gelu_pair(values):
    density = jnp.exp(values * values * -0.5) * INV_SQRT2PI
    below = 0.5 * lax.erf(values * INV_SQRT2) + 0.5
    return values * below, below + values * density


def feed_body(blocks, layout, me_ref, n_ref, gd_ref, ub_ref, *refs):
    count = sum(part[3] for part in layout)
    pieces = refs[:count]
    out_ref, gn_ref, keep_ref, send_ref, gub_ref, nt_s, gdt_s, up_s, down_s, act_s, gh_s, sems = refs[count:]
    step = pl.program_id(0)
    place = me_ref[0]
    rows = n_ref.shape[0]
    units = up_s.shape[3]
    per = rows // blocks

    def begin(group):
        slot = group % 2
        for index, (_, table, first, number, up_at, down_at) in enumerate(layout):
            held = pieces[first : first + number]
            for target, at, kind in ((up_s, up_at, 0), (down_s, down_at, 1)):
                fetch(
                    group,
                    table,
                    held,
                    (at, at + units),
                    target.at[slot, index],
                    sems.at[slot, kind, index],
                    place,
                )

    @pl.when(step == 0)
    def _():
        begin(0)
        nt_s[...] = n_ref[...].T
        gdt_s[...] = gd_ref[...].T
        out_ref[...] = jnp.zeros_like(out_ref)
        gn_ref[...] = jnp.zeros_like(gn_ref)

    for group in range(LANES):

        @pl.when(step == group)
        def _(group=group):
            if group + 1 < LANES:
                begin(group + 1)

    now = step % 2
    parts = len(layout)
    for index in range(parts):
        for kind, target in enumerate((up_s, down_s)):
            fetched(target.at[now, index], sems.at[now, kind, index])
    up_weight = [up_s[now, index] for index in range(parts)]
    down_weight = [down_s[now, index] for index in range(parts)]
    if parts > 1:
        up_weight = [jnp.concatenate(up_weight, axis=1)]
        down_weight = [jnp.concatenate(down_weight, axis=1)]
    up_weight, down_weight = up_weight[0], down_weight[0]
    true_lane = step ^ me_ref[1]
    unit_bias = ub_ref[true_lane]
    unit_sums = jnp.zeros((8, up_weight.shape[1]), FULL)
    for block in range(blocks):
        part = slice(block * per, (block + 1) * per)
        hidden = dot(n_ref[part, :], up_weight) + unit_bias
        active, slope = gelu_pair(hidden)
        active = active.astype(LOW)
        act_s[part, :] = active
        grad = (dot(gd_ref[part, :], down_weight) * slope).astype(LOW)
        gh_s[part, :] = grad
        unit_sums = unit_sums + fold(grad.astype(FULL))
        out_ref[part, :] += dot(active, down_weight, 1, 1)
        gn_ref[part, :] += dot(grad, up_weight, 1, 1)
    gub_ref[true_lane] = jnp.sum(unit_sums, axis=0, keepdims=True)
    grad_up = dot(nt_s[...], gh_s[...]).astype(LOW)
    grad_down = dot(gdt_s[...], act_s[...]).astype(LOW)
    chunk_rows = keep_ref.shape[2]
    wide = grad_up.shape[1]
    for odd, target in enumerate((keep_ref, send_ref)):

        @pl.when(step % 2 == odd)
        def _(target=target):
            for chunk in range(CHUNKS):
                slot = reversed_bits(chunk) ^ reversed_bits(place)
                at = slice(chunk * chunk_rows, (chunk + 1) * chunk_rows)
                target[0, slot, :, :wide] = grad_up[at]
                target[0, slot, :, wide:] = grad_down[at]


def feed(mine, normed, grad_down, unit_bias, groups, units, images):
    rows, width = normed.shape
    blocks = 2 if images <= 4 else 4
    parts = len(groups)
    sub = units // parts
    pieces, layout = [], []
    for (arrays, table), up_at, down_at in groups:
        layout.append((None, table, len(pieces), len(arrays), up_at, down_at))
        pieces.extend(arrays)
    chunk_rows = width // CHUNKS
    grad_block = (1, CHUNKS, chunk_rows, 2 * units)
    grads = jax.ShapeDtypeStruct((2,) + grad_block[1:], LOW)
    return pl.pallas_call(
        functools.partial(feed_body, blocks, layout),
        grid=(LANES,),
        in_specs=[
            pl.BlockSpec(memory_space=pltpu.SMEM),
            whole((rows, width)),
            whole((rows, width)),
            whole((LANES, 1, units)),
        ]
        + [anywhere()] * len(pieces),
        out_specs=[
            whole((rows, width)),
            whole((rows, width)),
            pl.BlockSpec(grad_block, lambda j: (j // 2, 0, 0, 0)),
            pl.BlockSpec(grad_block, lambda j: (jnp.maximum(j - 1, 0) // 2, 0, 0, 0)),
            whole((LANES, 1, units)),
        ],
        out_shape=[jax.ShapeDtypeStruct((rows, width), FULL)] * 2
        + [grads] * 2
        + [jax.ShapeDtypeStruct((LANES, 1, units), FULL)],
        scratch_shapes=[
            pltpu.VMEM((width, rows), LOW),
            pltpu.VMEM((width, rows), LOW),
            pltpu.VMEM((2, parts, width, sub), LOW),
            pltpu.VMEM((2, parts, width, sub), LOW),
            pltpu.VMEM((rows, units), LOW),
            pltpu.VMEM((rows, units), LOW),
            pltpu.SemaphoreType.DMA((2, 2, parts)),
        ],
        compiler_params=params(),
        cost_estimate=cost(3.5e10, 4e7),
    )(mine, normed, grad_down, unit_bias, *pieces)


def second_body(
    me_ref, down_ref, gn_ref, mid_ref, att_ref, ctx_ref, cot_ref, vec_ref, out_ref, gm_ref, ga_ref, keep_ref, send_ref, rows_ref, pad_s, out_s, sums_s, gat_s
):
    step = pl.program_id(0)

    @pl.when(step == 0)
    def _():
        pad_s[...] = jnp.zeros_like(pad_s)
        sums_s[...] = jnp.zeros_like(sums_s)

    cot = load_images(pad_s, cot_ref, step)
    down = down_ref[...] + vec_ref[6:7, :]
    mid = mid_ref[...]
    store_images(out_ref, out_s, mid + vec_ref[7:8, :] * down, step)
    scaled, inverse = normalise(mid)
    grad_normed = gn_ref[...]
    grad_mid = cot + norm_back(grad_normed, vec_ref[2:3, :], scaled, inverse)
    gm_ref[...] = grad_mid
    grad_att = (grad_mid * vec_ref[5:6, :]).astype(LOW)
    ga_ref[...] = grad_att
    gat_s[step] = grad_att.T
    sums_s[0] += fold(grad_normed * scaled)
    sums_s[1] += fold(grad_normed)
    sums_s[2] += fold(grad_mid)
    sums_s[3] += fold(grad_mid * att_ref[...].astype(FULL))
    sums_s[4] += fold(cot)
    sums_s[5] += fold(cot * down)

    @pl.when(step == pl.num_programs(0) - 1)
    def _():
        sums = [jnp.sum(sums_s[index], axis=0, keepdims=True) for index in range(6)]
        sums[2] = sums[2] * vec_ref[5:6, :]
        sums[4] = sums[4] * vec_ref[7:8, :]
        for index in range(6):
            rows_ref[index : index + 1, :] = sums[index]
        images = gat_s.shape[0]
        for group in range(LANES):
            at = slice(group * OUT_PACK, (group + 1) * OUT_PACK)
            grad = dot(gat_s[0], ctx_ref[0:PADDED, at])
            for image in range(1, images):
                grad = grad + dot(
                    gat_s[image], ctx_ref[image * PADDED : (image + 1) * PADDED, at]
                )
            give(me_ref[0], keep_ref, send_ref, group, grad.astype(LOW))


def give(place, keep_ref, send_ref, group, grad):
    rows = keep_ref.shape[2]
    mine = reversed_bits(place)
    target = (keep_ref, send_ref)[group % 2]
    for chunk in range(CHUNKS):
        target[group // 2, reversed_bits(chunk) ^ mine] = grad[chunk * rows : (chunk + 1) * rows]


def second_back(mine, down, grad_normed, mid, att, ctx, cot, vectors, images):
    rows, width = mid.shape
    block = lambda: pl.BlockSpec((PADDED, width), lambda i: (i, 0))
    grads = (2, CHUNKS, width // CHUNKS, OUT_PACK)
    return pl.pallas_call(
        second_body,
        grid=(images,),
        in_specs=[
            pl.BlockSpec(memory_space=pltpu.SMEM),
            block(),
            block(),
            block(),
            block(),
            whole(ctx.shape),
            whole(cot.shape),
            whole(vectors.shape),
        ],
        out_specs=[whole(cot.shape), block(), block(), whole(grads), whole(grads), whole((6, width))],
        out_shape=[
            jax.ShapeDtypeStruct(cot.shape, FULL),
            jax.ShapeDtypeStruct((rows, width), FULL),
            jax.ShapeDtypeStruct((rows, width), LOW),
            jax.ShapeDtypeStruct(grads, LOW),
            jax.ShapeDtypeStruct(grads, LOW),
            jax.ShapeDtypeStruct((6, width), FULL),
        ],
        scratch_shapes=[
            pltpu.VMEM((PADDED, width), FULL),
            pltpu.VMEM((PADDED, width), FULL),
            pltpu.VMEM((6, 8, width), FULL),
            pltpu.VMEM((images, width, PADDED), LOW),
        ],
        compiler_params=params(),
        cost_estimate=cost(1e10, 2e7),
    )(mine, down, grad_normed, mid, att, ctx, cot, vectors)


def back_body(table, columns, images, me_ref, ga_ref, qkv_ref, prob_ref, *refs):
    pieces = refs[:-6]
    dqkv_ref, pair_ref, cols_ref, weight_s, gc_s, sems = refs[-6:]
    step = pl.program_id(0)

    @pl.when(step == 0)
    def _():
        for group in range(LANES):
            fetch(group, table, pieces, columns, weight_s.at[group], sems.at[group], me_ref[0])

    fetched(weight_s.at[step], sems.at[step])
    gc_s[...] = dot(ga_ref[...], weight_s[step]).astype(LOW)
    lane = halves()

    def tile(image, index):
        return qkv_ref[0, image * PADDED : (image + 1) * PADDED, 128 * index : 128 * (index + 1)]

    def upstream(image, head):
        at = 128 if head == 2 else 0
        value = gc_s[image * PADDED : (image + 1) * PADDED, at : at + 128]
        return half_of(value, lane, V_ODD[head])

    def first(image, head):
        return dot(tile(image, V_TILE[head]), upstream(image, head), 1, 1)

    def second(grad_prob, image, head):
        soft = prob_ref[image, head].astype(FULL)
        weighted = soft * grad_prob
        inner = jnp.sum(weighted, axis=0, keepdims=True)
        grad_score = weighted - soft * inner
        if image == 0:
            pair_ref[head] = grad_score
        else:
            pair_ref[head] += grad_score
        return grad_score.astype(LOW)

    def third(low_score, image, head):
        odd = QK_ODD[head]
        return (
            dot(low_score, half_of(tile(image, K_TILE[head]), lane, odd), 0, 0) * HD**-0.5,
            dot(low_score, half_of(tile(image, Q_TILE[head]), lane, odd)),
            dot(prob_ref[image, head], upstream(image, head)),
        )

    work = [(image, head) for image in range(images) for head in range(HEADS_LANE)]
    probs, scores, grads = {}, {}, {}
    sums = [jnp.zeros((8, 128), FULL)] * 3
    for turn_index in range(len(work) + 2):
        if turn_index < len(work):
            probs[turn_index] = first(*work[turn_index])
        if 0 <= turn_index - 1 < len(work):
            scores[turn_index - 1] = second(probs.pop(turn_index - 1), *work[turn_index - 1])
        done = turn_index - 2
        if done < 0:
            continue
        image, head = work[done]
        grads[head] = third(scores.pop(done), image, head)
        if head < HEADS_LANE - 1:
            continue
        packed = (
            grads[0][0] + grads[1][0],
            grads[2][0] + grads[2][2],
            grads[0][2] + grads[1][2],
            grads[0][1] + grads[1][1],
            grads[2][1],
        )
        rows = slice(image * PADDED, (image + 1) * PADDED)
        for index, value in enumerate(packed):
            low_value = value.astype(LOW)
            dqkv_ref[0, rows, 128 * index : 128 * (index + 1)] = low_value
            if index < 3:
                sums[index] = sums[index] + fold(low_value.astype(FULL))
    for index in range(3):
        cols_ref[0, :, 128 * index : 128 * (index + 1)] = sums[index]


def back(mine, grad_att, qkv, prob, gathered, columns, images):
    rows, width = grad_att.shape
    heads = prob.shape[1]
    pieces, table = gathered
    return pl.pallas_call(
        functools.partial(back_body, table, columns, images),
        grid=(LANES,),
        in_specs=[
            pl.BlockSpec(memory_space=pltpu.SMEM),
            whole(grad_att.shape),
            pl.BlockSpec((1, rows, PACK), lambda g: (g, 0, 0)),
            pl.BlockSpec((images, HEADS_LANE, PADDED, PADDED), lambda g: (0, g, 0, 0)),
        ]
        + [anywhere()] * len(pieces),
        out_specs=[
            pl.BlockSpec((1, rows, PACK), lambda g: (g, 0, 0)),
            pl.BlockSpec((HEADS_LANE, PADDED, PADDED), lambda g: (g, 0, 0)),
            pl.BlockSpec((1, 8, 384), lambda g: (g, 0, 0)),
        ],
        out_shape=[
            jax.ShapeDtypeStruct((LANES, rows, PACK), LOW),
            jax.ShapeDtypeStruct((heads, PADDED, PADDED), FULL),
            jax.ShapeDtypeStruct((LANES, 8, 384), FULL),
        ],
        scratch_shapes=[
            pltpu.VMEM((LANES, width, OUT_PACK), LOW),
            pltpu.VMEM((rows, OUT_PACK), LOW),
            pltpu.SemaphoreType.DMA((LANES,)),
        ],
        compiler_params=params(),
        cost_estimate=cost(3e10, 4e7),
    )(mine, grad_att, qkv, prob, *pieces)


def heads_body(pair_ref, cols_ref, thin_ref, heads_ref, spread_s, flat_s):
    heads = pair_ref.shape[0]
    spread_s[...] = jnp.zeros_like(spread_s)

    def head_sum(index, carry):
        for row in range(GRID):
            at = GRID * (GRID - 1 - row)
            spread_s[index, :, at : at + PATCHES] += pair_ref[
                index, row * GRID : (row + 1) * GRID, 0:PATCHES
            ]
        return carry

    lax.fori_loop(0, heads, head_sum, 0)
    for col in range(GRID):
        flat_s[16 * col : 16 * (col + 1), :] = spread_s[:, col, :]
    wide = exact_dot(flat_s[...], thin_ref[...], 1)
    table = jnp.zeros((16, TABLE), FULL)
    for col in range(GRID):
        table = table + turn(wide[16 * col : 16 * (col + 1)], GRID - 1 - col)
    for group in range(LANES):
        cols = jnp.sum(cols_ref[group], axis=0, keepdims=True)
        for head in range(HEADS_LANE):
            at = HD * (4 + head if head < 2 else 3)
            heads_ref[group, head : head + 1, 0:HD] = cols[:, HD * head : HD * (head + 1)]
            heads_ref[group, head : head + 1, HD : 2 * HD] = cols[:, at : at + HD]
        first = group * HEADS_LANE
        heads_ref[group, :, 2 * HD :] = table[first : first + HEADS_LANE, 0 : SPAN * SPAN]


def heads_back(pair, cols, thin):
    heads = pair.shape[0]
    return pl.pallas_call(
        heads_body,
        out_shape=jax.ShapeDtypeStruct((LANES, HEADS_LANE, 2 * HD + SPAN * SPAN), FULL),
        scratch_shapes=[
            pltpu.VMEM((16, GRID, SPREAD), FULL),
            pltpu.VMEM((16 * GRID, SPREAD), FULL),
        ],
        compiler_params=params(),
        cost_estimate=cost(3e9, 4e6),
    )(pair, cols, thin)


def project_body(me_ref, n_ref, dqkv_ref, keep_ref, send_ref, t_s):
    t_s[...] = n_ref[...].T
    for group in range(LANES):
        give(me_ref[0], keep_ref, send_ref, group, dot(t_s[...], dqkv_ref[group]).astype(LOW))


def project(mine, normed, dqkv):
    rows, width = normed.shape
    grads = jax.ShapeDtypeStruct((2, CHUNKS, width // CHUNKS, PACK), LOW)
    return pl.pallas_call(
        project_body,
        in_specs=[pl.BlockSpec(memory_space=pltpu.SMEM)] + [pl.BlockSpec(memory_space=pltpu.VMEM)] * 2,
        out_shape=[grads, grads],
        scratch_shapes=[pltpu.VMEM((width, rows), LOW)],
        compiler_params=params(),
        cost_estimate=cost(8e9, 1e7),
    )(mine, normed, dqkv)


def input_body(table, me_ref, dqkv_ref, gm_ref, x_ref, vec_ref, *refs):
    pieces = refs[:-7]
    out_ref, rows_ref, weight_s, pad_s, out_s, sums_s, sems = refs[-7:]
    step = pl.program_id(0)

    @pl.when(step == 0)
    def _():
        for group in range(LANES):
            fetch(group, table, pieces, (0, PACK), weight_s.at[group], sems.at[group], me_ref[0])
        pad_s[...] = jnp.zeros_like(pad_s)
        sums_s[...] = jnp.zeros_like(sums_s)
        for group in range(LANES):
            fetched(weight_s.at[group], sems.at[group])

    scaled, inverse = normalise(load_images(pad_s, x_ref, step))
    grad = dot(dqkv_ref[0], weight_s[0], 1, 1)
    for group in range(1, LANES):
        grad = grad + dot(dqkv_ref[group], weight_s[group], 1, 1)
    sums_s[0] += fold(grad * scaled)
    sums_s[1] += fold(grad)
    for index in range(2):
        rows_ref[index : index + 1, :] = jnp.sum(sums_s[index], axis=0, keepdims=True)
    result = gm_ref[...] + norm_back(grad, vec_ref[0:1, :], scaled, inverse)
    store_images(out_ref, out_s, result, step)


def input_back(mine, dqkv, grad_mid, x, vectors, gathered, images):
    width = x.shape[1]
    pieces, table = gathered
    return pl.pallas_call(
        functools.partial(input_body, table),
        grid=(images // TWO,),
        in_specs=[
            pl.BlockSpec(memory_space=pltpu.SMEM),
            pl.BlockSpec((LANES, TWO * PADDED, PACK), lambda i: (0, i, 0)),
            pl.BlockSpec((TWO * PADDED, width), lambda i: (i, 0)),
            whole(x.shape),
            whole(vectors.shape),
        ]
        + [anywhere()] * len(pieces),
        out_specs=[whole(x.shape), whole((2, width))],
        out_shape=[jax.ShapeDtypeStruct(x.shape, FULL), jax.ShapeDtypeStruct((2, width), FULL)],
        scratch_shapes=[
            pltpu.VMEM((LANES, width, PACK), LOW),
            pltpu.VMEM((TWO * PADDED, width), FULL),
            pltpu.VMEM((TWO * PADDED, width), FULL),
            pltpu.VMEM((2, 8, width), FULL),
            pltpu.SemaphoreType.DMA((LANES,)),
        ],
        compiler_params=params(),
        cost_estimate=cost(1.5e10, 1.5e7),
    )(mine, dqkv, grad_mid, x, vectors, *pieces)


def swap(values, axis, bit):
    count = lax.axis_size(axis)
    return lax.ppermute(values, axis, [(index, index ^ bit) for index in range(count)])


def after(values, *others):
    return lax.optimization_barrier((values,) + others)[0]


def sync(*values):
    return lax.optimization_barrier(values)


def join(former, latter, axis=0):
    return jnp.concatenate([former, latter], axis=axis)


def split_rows(held):
    half = held.shape[1] // 2
    return held[:, :half], held[:, half:]


def pieces_of(upper, upper_x, lower, lower_y, near_core, far_core):
    arrays = [upper, upper_x, lower, lower_y, near_core[0], far_core[0], near_core[1], far_core[1]]
    half = upper.shape[1]

    def part(first, far):
        top = [(first + far, slot) for slot in range(8)]
        low = [(first + 2 + slot // 4, 4 * far + slot % 4) for slot in range(8)]
        return ((0, top), (half, low))

    return arrays, (part(0, 0), part(4, 0), part(0, 1), part(4, 1))


def total_of(terms):
    total = terms[0].astype(FULL)
    for one in terms[1:]:
        total = total + one.astype(FULL)
    return total


def sum_call(body, grid, views, outs, moved):
    return pl.pallas_call(
        body,
        grid=(grid,),
        in_specs=[pl.BlockSpec(block, index) for _, block, index in views],
        out_specs=[pl.BlockSpec(block, index) for _, _, block, index in outs],
        out_shape=[jax.ShapeDtypeStruct(shape, dtype) for shape, dtype, _, _ in outs],
        compiler_params=params(),
        cost_estimate=cost(1e6, moved),
    )(*[array for array, _, _ in views])


def sum_away(keeps, gots):
    half = keeps[0].shape[2] // 2
    wide = sum(keep.shape[3] for keep in keeps)
    views = []
    for keep, got in zip(keeps, gots):
        block = (1, 2, half, keep.shape[3])
        for array in (keep, got):
            views.append((array, block, lambda j: (1, j, 0, 0)))
            views.append((array, block, lambda j: (j // 2, 2 + j % 2, 1, 0)))

    def body(*refs):
        ins, (upper, lower) = refs[:-2], refs[-2:]
        first = 0
        for index in range(0, len(ins), 4):
            keep_u, keep_l, got_u, got_l = ins[index : index + 4]
            at = slice(first, first + keep_u.shape[3])
            first = at.stop
            upper[:, :, at] = total_of((keep_u[0], got_u[0])).astype(LOW)
            lower[0, :, :, at] = total_of((keep_l[0], got_l[0])).astype(LOW)

    outs = [
        ((8, half, wide), LOW, (2, half, wide), lambda j: (j, 0, 0)),
        ((2, 4, half, wide), LOW, (1, 2, half, wide), lambda j: (j // 2, j % 2, 0, 0)),
    ]
    return sum_call(body, 4, views, outs, 8e6)


def sum_here(keeps, gots, upper_got, lower_got):
    half = keeps[0].shape[2] // 2
    wide = sum(keep.shape[3] for keep in keeps)
    places = (
        lambda j: (0, j, 0, 0),
        lambda j: (0, 4 + j, 0, 0),
        lambda j: (0, j, 1, 0),
        lambda j: (1, j, 1, 0),
    )
    views = [
        (upper_got, (1, half, wide), lambda j: (j, 0, 0)),
        (upper_got, (1, half, wide), lambda j: (4 + j, 0, 0)),
        (lower_got, (1, 1, half, wide), lambda j: (0, j, 0, 0)),
        (lower_got, (1, 1, half, wide), lambda j: (1, j, 0, 0)),
    ]
    for keep, got in zip(keeps, gots):
        for array in (keep, got):
            views.extend((array, (1, 1, half, keep.shape[3]), place) for place in places)

    def body(*refs):
        far, ins, outs = refs[:4], refs[4:-4], refs[-4:]
        first = 0
        for index in range(0, len(ins), 8):
            at = slice(first, first + ins[index].shape[3])
            first = at.stop
            for view in range(4):
                came = far[view][0, :, at] if view < 2 else far[view][0, 0, :, at]
                terms = (ins[index + view][0, 0], ins[index + 4 + view][0, 0], came)
                outs[view][0, :, at] = total_of(terms).astype(outs[view].dtype)

    outs = [
        ((4, half, wide), dtype, (1, half, wide), lambda j: (j, 0, 0))
        for dtype in (FULL, LOW, FULL, LOW)
    ]
    return sum_call(body, 4, views, outs, 1.2e7)


def sum_line(upper, upper_got, lower, lower_got):
    half, wide = upper.shape[1:]
    views = []
    for array in (upper, upper_got, lower, lower_got):
        views.append((array, (1, half, wide), lambda j: (j, 0, 0)))
        views.append((array, (1, half, wide), lambda j: (2 + j, 0, 0)))

    def body(*refs):
        for side in range(2):
            out = refs[8 + side]
            out[0, :half] = total_of((refs[side][0], refs[2 + side][0])).astype(out.dtype)
            out[0, half:] = total_of((refs[4 + side][0], refs[6 + side][0])).astype(out.dtype)

    outs = [
        ((2, 2 * half, wide), dtype, (1, 2 * half, wide), lambda j: (j, 0, 0))
        for dtype in (FULL, LOW)
    ]
    return sum_call(body, 2, views, outs, 6e6)


def adam(weight, moment_one, moment_two, incoming, step_rate, decay_rate):
    first_new = BETA_ONE * moment_one + (1.0 - BETA_ONE) * incoming
    second_new = BETA_TWO * moment_two + (1.0 - BETA_TWO) * incoming * incoming
    update = (
        first_new
        / (1.0 - BETA_ONE**STEP)
        / (jnp.sqrt(second_new / (1.0 - BETA_TWO**STEP)) + ADAM_EPSILON)
    )
    return (second_new, weight * (1.0 - step_rate * decay_rate) - step_rate * update)


def pack_attention(weights):
    query, key, value, out = (weights[index] for index in range(4))
    rows = query.shape[0]
    blank = jnp.zeros((rows, HD), weights.dtype)
    first = jnp.concatenate([query, value[:, 128:], value[:, :128], key, blank], axis=1)
    last = jnp.concatenate([out[:, :128], blank, out[:, 128:]], axis=1)
    return first, last


def unpack_attention(first, last):
    query = first[:, :192]
    value = jnp.concatenate([first[:, 256:384], first[:, 192:256]], axis=1)
    key = first[:, 384:576]
    out = jnp.concatenate([last[:, :128], last[:, 192:]], axis=1)
    return jnp.stack([query, key, value, out])


def shards(
    block_input,
    cotangent,
    image_size,
    attention_weights,
    attention_first,
    attention_second,
    mlp_weights,
    mlp_first,
    mlp_second,
    head_params,
    head_first,
    head_second,
    norm_params,
    norm_first,
    norm_second,
):
    near = lax.axis_size("dp") == CHUNKS
    lane_index = lax.axis_index("mp")
    local_rows, width = block_input.shape
    images = local_rows // PATCHES
    local_heads = head_params.shape[0]
    chunk_rows = width // CHUNKS
    thin = jnp.asarray(thin_matrix(), LOW)

    first, last = pack_attention(attention_weights.astype(LOW))
    mlp_low = mlp_weights.astype(LOW)
    units = mlp_low.shape[2]
    part = units // 2
    unit_bias = norm_params[8:].reshape(LANES, 1, units)
    second = jnp.concatenate([last, mlp_low[0, :, :part], mlp_low[1, :, :part]], axis=1)
    third = jnp.concatenate([mlp_low[0, :, part:], mlp_low[1, :, part:]], axis=1)
    if near:
        mine = jnp.stack([lax.axis_index("dp"), lane_index, lane_index]).astype(jnp.int32)
        core = lambda values: swap(values, "mp", 1)
        x_axis = lambda values: swap(values, "mp", 2)
        y_axis = lambda values: swap(values, "dp", 1)
        z_near = lambda values: swap(values, "dp", 2)
        z_far = lambda values: swap(values, "dp", 4)
        one, two, three = first[None], second[None], third[None]
        got = z_far(one)
        normed_one, grad_down = first_norm(block_input, cotangent, norm_params, images)
        got, normed_one = sync(got, normed_one)
        one = join(one, got)
        got = z_near(one)
        two_got = z_far(after(two, one))
        other = x_axis(after(head_params, one))
        near_table, far_table = core(head_params), core(other)
        upper, lower = split_rows(join(one, got))
        upper, lower = sync(upper, lower)
        upper_got, lower_got = y_axis(upper), x_axis(lower)
        two = join(two, after(two_got, upper, lower))
        two_got = z_near(two)
        bias, add = spread_bias(
            (head_params, after(near_table, two), other, after(far_table, two)), thin
        )
        upper_got, lower_got, bias = sync(upper_got, lower_got, bias)
        upper, lower = sync(join(upper, upper_got), join(lower, lower_got))
        upper_far, lower_far = x_axis(upper), y_axis(lower)
        near_core = sync(core(upper), core(lower))
        two_upper, two_lower = split_rows(join(two, after(two_got, upper, lower)))
        two_upper, two_lower, three = sync(two_upper, two_lower, after(three, *near_core))
        two_upper_got, two_lower_got = y_axis(two_upper), x_axis(two_lower)
        three_got = z_far(three)
        upper_far, lower_far, two_upper_got, two_lower_got, three_got = sync(
            upper_far, lower_far, two_upper_got, two_lower_got, three_got
        )
        far_core = sync(core(upper_far), core(lower_far))
        three = join(three, three_got)
        first_all = pieces_of(upper, upper_far, lower, lower_far, near_core, far_core)
        two_upper, two_lower = join(two_upper, two_upper_got), join(two_lower, two_lower_got)
        two_upper, two_lower, three, normed_one = sync(two_upper, two_lower, three, normed_one)
        two_upper_far, two_lower_far = x_axis(two_upper), y_axis(two_lower)
        three_got = z_near(three)
    else:
        mine = jnp.stack([0 * lane_index, 0 * lane_index, lane_index]).astype(jnp.int32)

        def gather_far(piece):
            full = lax.all_gather(piece, "dp", axis=0, tiled=True)
            full = lax.all_gather(full, "mp", axis=0, tiled=False)
            full = full.reshape(LANES, CHUNKS, chunk_rows, piece.shape[1])
            order = [reversed_bits(index) for index in range(CHUNKS)]
            full = jnp.stack([full[:, index] for index in order], axis=1)
            slots = range(CHUNKS)
            table = tuple(((0, [(group, slot) for slot in slots]),) for group in range(LANES))
            return [full[index] for index in range(LANES)], table

        tables = lax.all_gather(head_params, "mp", axis=0, tiled=False)
        tables = tuple(tables[index] for index in range(LANES))
        normed_one, grad_down = first_norm(block_input, cotangent, norm_params, images)
        bias, add = spread_bias(tables, thin)
        first_all = gather_far(first)
        second_all = gather_far(second)
        third_all = gather_far(third)

    qkv, prob, ctx = attend(mine, image_size, normed_one, bias, add, first_all, images)
    if near:
        ctx, three_got, two_upper_far, two_lower_far = sync(
            ctx, three_got, two_upper_far, two_lower_far
        )
        three_upper, three_lower, two_upper, two_lower = sync(
            *split_rows(join(three, three_got)), two_upper, two_lower
        )
        three_upper_got, three_lower_got = y_axis(three_upper), x_axis(three_lower)
        two_near = sync(core(two_upper), core(two_lower))
        two_far = (core(after(two_upper_far, *two_near)), core(after(two_lower_far, *two_near)))
        two_near, two_far, three_upper_got, three_lower_got = sync(
            two_near, two_far, three_upper_got, three_lower_got
        )
        second_all = pieces_of(two_upper, two_upper_far, two_lower, two_lower_far, two_near, two_far)
        three_upper, three_lower, ctx = sync(
            join(three_upper, three_upper_got), join(three_lower, three_lower_got), ctx
        )
        three_upper_far, three_lower_far = x_axis(three_upper), y_axis(three_lower)
        three_near = (core(three_upper), core(three_lower))
    att, mid, normed_two = middle(
        mine, ctx, block_input, norm_params, second_all, (0, OUT_PACK), images
    )
    if near:
        normed_two, three_upper_far, three_lower_far, three_near = sync(
            normed_two, three_upper_far, three_lower_far, three_near
        )
        three_far = (core(three_upper_far), core(three_lower_far))
        third_all = pieces_of(
            three_upper, three_upper_far, three_lower, three_lower_far, three_near, three_far
        )
    groups = ((second_all, OUT_PACK, OUT_PACK + part), (third_all, 0, part))
    down, grad_normed, keep_mlp, send_mlp, unit_sums = feed(
        mine, normed_two, grad_down, unit_bias, groups, units, images
    )
    if near:
        mlp_core = core(send_mlp)
    output, grad_mid, grad_att, keep_out, send_out, second_rows = second_back(
        mine, down, grad_normed, mid, att, ctx, cotangent, norm_params, images
    )
    if near:
        mlp_core, grad_att, send_out = sync(mlp_core, grad_att, send_out)
        keeps, gots = (keep_mlp, keep_out), (mlp_core, core(send_out))
        upper, lower, grad_att = sync(*sum_away(keeps, gots), grad_att)
        upper_got, lower_got = x_axis(upper), y_axis(lower)
    dqkv, pair, cols = back(
        mine, grad_att, qkv, prob, second_all, (0, OUT_PACK), images
    )
    keep_att, send_att = project(mine, normed_one, dqkv)
    if near:
        keep_att, send_att, upper_got, lower_got = sync(keep_att, send_att, upper_got, lower_got)
        att_core = core(send_att)
        upper, upper_away, lower, lower_away = sum_here(keeps, gots, upper_got, lower_got)
        upper_away, lower_away, att_core, pair = sync(upper_away, lower_away, att_core, pair)
        upper_got, lower_got = y_axis(upper_away), x_axis(lower_away)
        keeps, gots = (keep_att,), (att_core,)
        att_upper, att_lower, pair = sync(*sum_away(keeps, gots), pair)
        att_upper_got, att_lower_got = x_axis(att_upper), y_axis(att_lower)
    grad_heads = heads_back(pair, cols, thin)
    if near:
        upper_got, lower_got, grad_heads = sync(upper_got, lower_got, grad_heads)
        line, line_away = sum_line(upper, upper_got, lower, lower_got)
        line_away, dqkv = sync(line_away, dqkv)
        line_got = z_near(line_away)
        upper_got, lower_got = att_upper_got, att_lower_got
    grad_input, first_rows = input_back(
        mine, dqkv, grad_mid, block_input, norm_params, first_all, images
    )

    norms = jnp.concatenate([first_rows, second_rows, unit_sums.reshape(-1, width)], axis=0)
    if near:
        norms, upper_got, lower_got = sync(norms, upper_got, lower_got)
        upper, upper_away, lower, lower_away = sum_here(keeps, gots, upper_got, lower_got)
        upper_away, lower_away, norms, line_got = sync(upper_away, lower_away, norms, line_got)
        upper_got, lower_got = y_axis(upper_away), x_axis(lower_away)
        heads_width = grad_heads.shape[2]
        count = norms.shape[0]
        norms = jnp.pad(norms, ((0, 0), (0, heads_width - width)))
        packs = [join(norms, grad_heads[index]) for index in range(LANES)]
        small = (packs[0] + core(packs[1])) + (x_axis(packs[2]) + swap(packs[3], "mp", 3))
        small, upper_got, lower_got = sync(small, upper_got, lower_got)
        here, away = sum_line(upper, upper_got, lower, lower_got)
        small, here, away = sync(small, here, away)
        got = z_near(away)
        small_got = y_axis(small)
        line = line + line_got.astype(FULL)
        line_got = z_far(line[1].astype(LOW))
        got, small_got = sync(got, small_got)
        here = here + got.astype(FULL)
        small = small + small_got
        away, small = sync(here[1].astype(LOW), small)
        got = z_far(away)
        small = (small + z_near(small)) + (z_far(small) + swap(small, "dp", 6))
        sum_mlp = line[0] + line_got.astype(FULL)
        sum_att = here[0] + got.astype(FULL)
        sum_mlp, sum_out = sum_mlp[:, : 2 * units], sum_mlp[:, 2 * units :]
        reduced_norms = small[:count, :width]
        reduced_heads = small[count:]
    else:
        reduced_norms = lax.psum(norms, ("dp", "mp"))
        reduced_heads = lax.psum_scatter(
            lax.psum(grad_heads, "dp"), "mp", scatter_dimension=0, tiled=False
        )

        def scatter_far(keep, send):
            terms = jnp.stack([keep[0], send[0], keep[1], send[1]])
            order = [reversed_bits(index) for index in range(CHUNKS)]
            terms = jnp.stack([terms[:, index] for index in order], axis=1)
            terms = terms.reshape(LANES, width, terms.shape[-1])
            mine_only = lax.psum_scatter(terms, "mp", scatter_dimension=0, tiled=False)
            return lax.psum_scatter(
                mine_only.astype(FULL), "dp", scatter_dimension=0, tiled=True
            )

        sum_mlp = scatter_far(keep_mlp, send_mlp)
        sum_out = scatter_far(keep_out, send_out)
        sum_att = scatter_far(keep_att, send_att)

    reduced_attention = unpack_attention(sum_att, sum_out)
    reduced_mlp = jnp.stack([sum_mlp[:, :units], sum_mlp[:, units:]])
    attention_second_new, attention_new = adam(
        attention_weights,
        attention_first,
        attention_second,
        reduced_attention,
        RATE_MATRIX,
        DECAY_MATRIX,
    )
    mlp_second_new, mlp_new = adam(
        mlp_weights, mlp_first, mlp_second, reduced_mlp, RATE_MATRIX, DECAY_MATRIX
    )
    head_second_new, head_new = adam(
        head_params, head_first, head_second, reduced_heads, RATE_VECTOR, 0.0
    )
    norm_second_new, norm_new = adam(
        norm_params, norm_first, norm_second, reduced_norms, RATE_VECTOR, 0.0
    )
    return (
        output,
        grad_input,
        reduced_attention,
        attention_second_new,
        attention_new,
        reduced_mlp,
        mlp_second_new,
        mlp_new,
        reduced_heads,
        head_second_new,
        head_new,
        reduced_norms,
        norm_second_new,
        norm_new,
    )


def solution(mesh):
    rows = P(("dp", "mp"), None)
    matrix = P(None, "dp", "mp")
    head = P("mp", None)
    placed = (rows, rows, P("dp", None)) + (matrix,) * 6 + (head,) * 3 + (P(),) * 3
    given = (rows, rows) + (matrix,) * 6 + (head,) * 3 + (P(),) * 3
    return jax.shard_map(shards, mesh=mesh, in_specs=placed, out_specs=given, check_vma=False)
```

time: 326 us -> 294 us (0.902); the launches traced: 321 us -> 292 us
  other arithmetic: 35.3 us -> 8.34 us
  Pallas kernels: 128 us -> 146 us
  waiting for transfers between devices: 89.2 us -> 74.9 us
  local copies, waits for them, and re-layouts: 19.9 us -> 9.32 us
  starting transfers between devices: 46.4 us -> 52.3 us
    pallas_call x4 -> x13, Pallas kernels: 68.7 us -> 93.8 us  [the longest x6 23.4 us: sum_call(): pl.pallas_call(body, grid=(grid,), in_specs=[pl.BlockSpec(block, index) f...]
    add x18 -> x7, other arithmetic: 15.6 us -> 0.31 us  [the longest x1 0.12 us: shards(): line = line + line_got.astype(FULL)]
    ppermute x51 -> x55, waiting for transfers between devices: 89.2 us -> 74.9 us  [swap(): lax.ppermute(values, axis, [(index, index ^ bit) for index in range(count)])]
    convert_element_type x9 -> x0, other arithmetic: 7.15 us -> none  [the longest x4 4.21 us: sum_plane_two(): upper_got, lower_got = (upper_got.astype(FULL), lower_got.astype(FULL))]
    ppermute x51 -> x55, starting transfers between devices: 46.4 us -> 52.3 us  [swap(): lax.ppermute(values, axis, [(index, index ^ bit) for index in range(count)])]
    unnamed x92 -> x107, local copies, waits for them, and re-layouts: 3.18 us -> 7.99 us
    another operation x17 -> x0, local copies, waits for them, and re-layouts: 4.72 us -> none  [the longest x15 4.37 us: spread_table(): flat = jnp.stack(parts, axis=1).reshape(heads, GRID, SPAN * GRID)]
    pallas_call x1, Pallas kernels: 12.4 us -> 8.78 us  [project(): pl.pallas_call(project_body, in_specs=[pl.BlockSpec(memory_space=pltpu.SM...]
  transfers between devices with their start and end apart: 51 -> 55, of which waited for: 19 -> 30; matrix products, arithmetic and copies ran while one was open for 13% -> 3% of each run, Pallas kernels for 29% -> 36%
where the time goes in v3:
time: 294 us; the launch traced here: 292 us
  Pallas kernels  146 us (50%)
  waiting for transfers between devices  74.9 us (25%)
  starting transfers between devices  52.3 us (18%)
  local copies, waits for them, and re-layouts  9.32 us (3%)
  other arithmetic  8.34 us (3%)
    ppermute x55, waiting for transfers between devices, swap(): lax.ppermute(values, axis, [(index, index ^ bit) for index in range(count)])  74.9 us
    ppermute x55, starting transfers between devices, swap(): lax.ppermute(values, axis, [(index, index ^ bit) for index in range(count)])  52.3 us
    pallas_call x1, Pallas kernels, feed(): pl.pallas_call(functools.partial(feed_body, blocks, layout), grid=(LANES,...  35.9 us
    pallas_call x6, Pallas kernels, sum_call(): pl.pallas_call(body, grid=(grid,), in_specs=[pl.BlockSpec(block, index) f...  23.4 us
    pallas_call x1, Pallas kernels, attend(): pl.pallas_call(functools.partial(attend_body, table, images), grid=(LANES...  15.7 us
    pallas_call x1, Pallas kernels, back(): pl.pallas_call(functools.partial(back_body, table, columns, images), grid...  15 us
    pallas_call x1, Pallas kernels, second_back(): pl.pallas_call(second_body, grid=(images,), in_specs=[pl.BlockSpec(memory...  12.3 us
    pallas_call x1, Pallas kernels, input_back(): pl.pallas_call(functools.partial(input_body, table), grid=(images // TWO,...  11.8 us
  transfers between devices with their start and end apart: 55, of which 30 were waited for; matrix products, arithmetic and copies ran while one was open for 3% of the time, Pallas kernels for 36%

profile of v3, /device:TPU:0, one launch (start us, length us, event | category | flops | bytes accessed | tf_op | source)
XLA Modules:
  0.0 292.4 jit_solution(11187836264936133437)
XLA Ops:
  1.9 4.1 %collective-permute-start = (bf16[1,96,640]{2,1,0:T(8,128)(2,1)S(1)}, bf16[1,96,640]{2,1,0:T(8,128)(2,1)S(1)}, u32[]{:S(2)}, u32[]{:S(2)}) collective-permute-start(bf16[1,96,640]{2,1,0:T(8,128)(2,1)S(1)} %bitcast.60), channel_id=1, source_target_pairs={{0,16},{4,20},{8,24},{12,28},{16,0},{20,4},{24,8},{28,12},{1,17},{... | collective-permute-start | bytes 368648 | tf_op jit(solution)/shard_map/ppermute | solution.py:861
  6.0 5.0 %shard_map.272 = (bf16[832,768]{1,0:T(8,128)(2,1)}, bf16[832,768]{1,0:T(8,128)(2,1)}) custom-call(f32[784,768]{1,0:T(8,128)} %x_ref.5, f32[784,768]{1,0:T(8,128)} %cot_ref.3, f32[12,768]{1,0:T(8,128)} %vec_ref.7), custom_call_target="tpu_custom_call" | custom-call | flops 3000000000 | bytes 4000000 | tf_op jit(solution)/shard_map/pallas_call | solution.py:147
  21.5 4.3 %collective-permute-start.5 = (bf16[4,48,640]{2,1,0:T(8,128)(2,1)S(1)}, bf16[4,48,640]{2,1,0:T(8,128)(2,1)S(1)}, u32[]{:S(2)}, u32[]{:S(2)}) collective-permute-start(bf16[4,48,640]{2,1,0:T(8,128)(2,1)S(1)} %get-tuple-element.159), channel_id=1, source_target_pairs={{0,2},{1,3},{2,0},{3,1},{4,6},{5,7},{6,4},{7,5},{8,10},{9,11},{10,... | collective-permute-start | bytes 737288 | tf_op jit(solution)/shard_map/ppermute | solution.py:861
  28.8 5.4 %shard_map.273 = (f32[12,208,208]{2,1,0:T(8,128)}, f32[4,1,640]{2,1,0:T(1,128)}) custom-call(f32[3,857]{1,0:T(4,128)} %t0.1, f32[3,857]{1,0:T(4,128)} %copy-done.49, f32[3,857]{1,0:T(4,128)} %copy-done.50, f32[3,857]{1,0:T(4,128)} %copy-done.51, bf16[768,384]{1,0:T(8,128)(2,1)} %constant.32.clone.thin_ref), custom_call_target="tpu_custom_call" | custom-call | flops 3000000000 | bytes 4000000 | tf_op jit(solution)/shard_map/pallas_call | solution.py:211
  43.5 5.7 %collective-permute-done.11.refs_1_ = bf16[8,48,640]{2,1,0:T(8,128)(2,1)} collective-permute-done((bf16[8,48,640]{2,1,0:T(8,128)(2,1)S(1)}, bf16[8,48,640]{2,1,0:T(8,128)(2,1)}, u32[]{:S(2)}, u32[]{:S(2)}) %collective-permute-start.11) | collective-permute-done | bytes 491552 | tf_op jit(solution)/shard_map/ppermute | solution.py:861
  49.8 7.1 %collective-permute-done.13 = bf16[4,48,1024]{2,1,0:T(8,128)(2,1)S(1)} collective-permute-done((bf16[4,48,1024]{2,1,0:T(8,128)(2,1)S(1)}, bf16[4,48,1024]{2,1,0:T(8,128)(2,1)S(1)}, u32[]{:S(2)}, u32[]{:S(2)}) %collective-permute-start.13) | collective-permute-done | bytes 393248 | tf_op jit(solution)/shard_map/ppermute | solution.py:861
  64.0 15.7 %shard_map.274 = (bf16[4,832,640]{2,1,0:T(8,128)(2,1)}, bf16[4,12,208,208]{3,2,1,0:T(8,128)(2,1)}, bf16[832,1024]{1,0:T(8,128)(2,1)}) custom-call(s32[3]{0:T(128)} %pad_add_fusion.me_ref, s32[16,2]{1,0:T(8,128)} %copy.31.size_ref, s32[2,208,128]{2,1,0:T(8,128)} %constant.33.clone.grid_ref, bf16[832,768]{1,0:T(8,128)(2,1)} %get-tuple-element.181.n_ref, ...), custom_call_target="tpu_custom_call" | custom-call | flops 15000000512 | bytes 20000000 | tf_op jit(solution)/shard_map/pallas_call | solution.py:322
  87.6 7.0 %collective-permute-done.25 = bf16[4,48,768]{2,1,0:T(8,128)(2,1)S(1)} collective-permute-done((bf16[4,48,768]{2,1,0:T(8,128)(2,1)S(1)}, bf16[4,48,768]{2,1,0:T(8,128)(2,1)S(1)}, u32[]{:S(2)}, u32[]{:S(2)}) %collective-permute-start.25) | collective-permute-done | bytes 294944 | tf_op jit(solution)/shard_map/ppermute | solution.py:861
  97.4 7.4 %shard_map.275 = (bf16[832,768]{1,0:T(8,128)(2,1)}, f32[832,768]{1,0:T(8,128)}, bf16[832,768]{1,0:T(8,128)(2,1)}) custom-call(s32[3]{0:T(128)} %pad_add_fusion.me_ref, bf16[832,1024]{1,0:T(8,128)(2,1)} %get-tuple-element.205.ctx_ref, f32[784,768]{1,0:T(8,128)} %x_ref.5, f32[12,768]{1,0:T(8,128)} %vec_ref.7, bf16[8,48,1024]{2,1,0:T(8,128)(2,1)} %copy-done.14, ...), custom_call_target="tpu_custom_call" | custom-call | flops 8000000000 | bytes 15000000 | tf_op jit(solution)/shard_map/pallas_call | solution.py:383
  104.9 6.9 %collective-permute-done.27.refs_9_ = bf16[8,48,768]{2,1,0:T(8,128)(2,1)S(1)} collective-permute-done((bf16[8,48,768]{2,1,0:T(8,128)(2,1)S(1)}, bf16[8,48,768]{2,1,0:T(8,128)(2,1)S(1)}, u32[]{:S(2)}, u32[]{:S(2)}) %collective-permute-start.27) | collective-permute-done | bytes 589856 | tf_op jit(solution)/shard_map/ppermute | solution.py:861
  116.4 35.9 %shard_map.276 = (f32[832,768]{1,0:T(8,128)}, f32[832,768]{1,0:T(8,128)}, bf16[2,8,96,1536]{3,2,1,0:T(8,128)(2,1)}, bf16[2,8,96,1536]{3,2,1,0:T(8,128)(2,1)}, f32[4,1,768]{2,1,0:T(1,128)}) custom-call(s32[3]{0:T(128)} %pad_add_fusion.me_ref, bf16[832,768]{1,0:T(8,128)(2,1)} %get-tuple-element.213.n_ref, bf16[832,768]{1,0:T(8,128)(2,1)} %get-tuple-element.214.gd_ref, ...), custom_call_target="tpu_custom_call" | custom-call | flops 35000000512 | bytes 40000000 | tf_op jit(solution)/shard_map/pallas_call | solution.py:508
  152.6 12.3 %shard_map.277 = (f32[784,768]{1,0:T(8,128)}, f32[832,768]{1,0:T(8,128)}, bf16[832,768]{1,0:T(8,128)(2,1)}, bf16[2,8,96,256]{3,2,1,0:T(8,128)(2,1)}, bf16[2,8,96,256]{3,2,1,0:T(8,128)(2,1)}, /*index=5*/f32[6,768]{1,0:T(8,128)}) custom-call(s32[3]{0:T(128)} %pad_add_fusion.me_ref, f32[832,768]{1,0:T(8,128)} %get-tuple-element.219.down_ref, ...), custom_call_target="tpu_custom_call" | custom-call | flops 10000000000 | bytes 20000000 | tf_op jit(solution)/shard_map/pallas_call | solution.py:600
  168.3 4.6 %shard_map.278 = (bf16[8,48,1792]{2,1,0:T(8,128)(2,1)}, bf16[2,4,48,1792]{3,2,1,0:T(8,128)(2,1)}) custom-call(bf16[2,8,96,1536]{3,2,1,0:T(8,128)(2,1)} %get-tuple-element.224.refs_0_.refs_1_.refs_4_.refs_5_.refs_6_.refs_7_, bf16[2,8,96,1536]{3,2,1,0:T(8,128)(2,1)} %get-tuple-element.224.refs_0_.refs_1_.refs_4_.refs_5_.refs_6_.refs_7_, ...), custom_call_target="tpu_custom_call" | custom-call | flops 1000000 | bytes 8000000 | tf_op jit(solution)/shard_map/pallas_call | solution.py:901
  175.0 15.0 %shard_map.279 = (bf16[4,832,640]{2,1,0:T(8,128)(2,1)}, f32[12,208,208]{2,1,0:T(8,128)}, f32[4,8,384]{2,1,0:T(8,128)}) custom-call(s32[3]{0:T(128)} %pad_add_fusion.me_ref, bf16[832,768]{1,0:T(8,128)(2,1)} %get-tuple-element.234.ga_ref, bf16[4,832,640]{2,1,0:T(8,128)(2,1)} %get-tuple-element.235.qkv_ref, ...), custom_call_target="tpu_custom_call" | custom-call | flops 30000001024 | bytes 40000000 | tf_op jit(solution)/shard_map/pallas_call | solution.py:713
  190.0 8.8 %shard_map.280 = (bf16[2,8,96,640]{3,2,1,0:T(8,128)(2,1)}, bf16[2,8,96,640]{3,2,1,0:T(8,128)(2,1)}) custom-call(s32[3]{0:T(128)} %pad_add_fusion.me_ref, bf16[832,768]{1,0:T(8,128)(2,1)} %get-tuple-element.181.n_ref, bf16[4,832,640]{2,1,0:T(8,128)(2,1)} %get-tuple-element.262.dqkv_ref), custom_call_target="tpu_custom_call" | custom-call | flops 8000000000 | bytes 10000000 | tf_op jit(solution)/shard_map/pallas_call | solution.py:795
  198.8 6.9 %collective-permute-done.35.refs_0_.refs_1_ = bf16[8,48,1792]{2,1,0:T(8,128)(2,1)S(1)} collective-permute-done((bf16[8,48,1792]{2,1,0:T(8,128)(2,1)}, bf16[8,48,1792]{2,1,0:T(8,128)(2,1)S(1)}, u32[]{:S(2)}, u32[]{:S(2)}) %collective-permute-start.35) | collective-permute-done | bytes 1376288 | tf_op jit(solution)/shard_map/ppermute | solution.py:861
  207.9 5.9 %shard_map.281 = (f32[4,48,1792]{2,1,0:T(8,128)}, bf16[4,48,1792]{2,1,0:T(8,128)(2,1)}, f32[4,48,1792]{2,1,0:T(8,128)}, bf16[4,48,1792]{2,1,0:T(8,128)(2,1)}) custom-call(bf16[8,48,1792]{2,1,0:T(8,128)(2,1)} %copy-done.2, bf16[8,48,1792]{2,1,0:T(8,128)(2,1)} %copy-done.2, bf16[2,4,48,1792]{3,2,1,0:T(8,128)(2,1)} %copy-done.3, ...), custom_call_target="tpu_custom_call" | custom-call | flops 1000000 | bytes 12000000 | tf_op jit(solution)/shard_map/pallas_call | solution.py:901
  215.1 3.6 %shard_map.282 = (bf16[8,48,640]{2,1,0:T(8,128)(2,1)}, bf16[2,4,48,640]{3,2,1,0:T(8,128)(2,1)}) custom-call(bf16[2,8,96,640]{3,2,1,0:T(8,128)(2,1)} %get-tuple-element.251.refs_0_.refs_1_.refs_4_.refs_5_.refs_6_.refs_7_, bf16[2,8,96,640]{3,2,1,0:T(8,128)(2,1)} %get-tuple-element.251.refs_0_.refs_1_.refs_4_.refs_5_.refs_6_.refs_7_, ...), custom_call_target="tpu_custom_call" | custom-call | flops 1000000 | bytes 8000000 | tf_op jit(solution)/shard_map/pallas_call | solution.py:901
  221.6 5.4 %shard_map.283 = f32[4,3,857]{2,1,0:T(4,128)} custom-call(f32[12,208,208]{2,1,0:T(8,128)} %get-tuple-element.256.pair_ref, f32[4,8,384]{2,1,0:T(8,128)} %get-tuple-element.257.cols_ref, bf16[768,384]{1,0:T(8,128)(2,1)} %constant.32.clone.thin_ref), custom_call_target="tpu_custom_call" | custom-call | flops 3000000000 | bytes 4000000 | tf_op jit(solution)/shard_map/pallas_call | solution.py:774
  227.0 5.3 %collective-permute-done.38.refs_2_.refs_3_ = bf16[4,48,1792]{2,1,0:T(8,128)(2,1)S(1)} collective-permute-done((bf16[4,48,1792]{2,1,0:T(8,128)(2,1)}, bf16[4,48,1792]{2,1,0:T(8,128)(2,1)S(1)}, u32[]{:S(2)}, u32[]{:S(2)}) %collective-permute-start.38) | collective-permute-done | bytes 688160 | tf_op jit(solution)/shard_map/ppermute | solution.py:861
  237.4 11.8 %shard_map.285 = (f32[784,768]{1,0:T(8,128)}, f32[2,768]{1,0:T(2,128)}) custom-call(s32[3]{0:T(128)} %pad_add_fusion.me_ref, bf16[4,832,640]{2,1,0:T(8,128)(2,1)} %get-tuple-element.262.dqkv_ref, f32[832,768]{1,0:T(8,128)} %get-tuple-element.263.gm_ref, f32[784,768]{1,0:T(8,128)} %x_ref.5, f32[12,768]{1,0:T(8,128)} %vec_ref.7, ...), custom_call_target="tpu_custom_call" | custom-call | flops 15000000512 | bytes 15000000 | tf_op jit(solution)/shard_map/pallas_call | solution.py:834
  251.5 3.8 %shard_map.286 = (f32[4,48,640]{2,1,0:T(8,128)}, bf16[4,48,640]{2,1,0:T(8,128)(2,1)}, f32[4,48,640]{2,1,0:T(8,128)}, bf16[4,48,640]{2,1,0:T(8,128)(2,1)}) custom-call(bf16[8,48,640]{2,1,0:T(8,128)(2,1)} %copy-done.8, bf16[8,48,640]{2,1,0:T(8,128)(2,1)} %copy-done.8, bf16[2,4,48,640]{3,2,1,0:T(8,128)(2,1)} %copy-done.9, bf16[2,4,48,640]{3,2,1,0:T(8,128)(2,1)} %copy-done.9, ...), custom_call_target="tpu_custom_call" | custom-call | flops 1000000 | bytes 12000000 | tf_op jit(solution)/shard_map/pallas_call | solution.py:901
  263.0 4.7 %collective-permute-done.46.refs_2_.refs_3_ = bf16[4,48,640]{2,1,0:T(8,128)(2,1)S(1)} collective-permute-done((bf16[4,48,640]{2,1,0:T(8,128)(2,1)S(1)}, bf16[4,48,640]{2,1,0:T(8,128)(2,1)S(1)}, u32[]{:S(2)}, u32[]{:S(2)}) %collective-permute-start.46) | collective-permute-done | bytes 245792 | tf_op jit(solution)/shard_map/ppermute | solution.py:861
  276.2 3.7 %collective-permute-done.48 = bf16[2,96,640]{2,1,0:T(8,128)(2,1)S(1)} collective-permute-done((bf16[2,96,640]{2,1,0:T(8,128)(2,1)}, bf16[2,96,640]{2,1,0:T(8,128)(2,1)S(1)}, u32[]{:S(2)}, u32[]{:S(2)}) %collective-permute-start.48) | collective-permute-done | bytes 245792 | tf_op jit(solution)/shard_map/ppermute | solution.py:861
  (263 shorter events, 94.5 us)
Async XLA Ops:
  12.7 14.9 %collective-permute-start.6 = (f32[3,857]{1,0:T(4,128)S(1)}, f32[3,857]{1,0:T(4,128)S(1)}, u32[]{:S(2)}, u32[]{:S(2)}) collective-permute-start(f32[3,857]{1,0:T(4,128)S(1)} %copy-done.30), channel_id=1, source_target_pairs={{0,1},{1,0},{2,3},{3,2},{4,5},{5,4},{6,7},{7,6},{8,9},{9,8},{10,11... | collective-permute-start | bytes 30860 | tf_op jit(solution)/shard_map/ppermute | solution.py:861
  14.5 13.0 %collective-permute-start.1 = (bf16[1,96,1024]{2,1,0:T(8,128)(2,1)S(1)}, bf16[1,96,1024]{2,1,0:T(8,128)(2,1)S(1)}, u32[]{:S(2)}, u32[]{:S(2)}) collective-permute-start(bf16[1,96,1024]{2,1,0:T(8,128)(2,1)S(1)} %bitcast.57), channel_id=1, source_target_pairs={{0,16},{4,20},{8,24},{12,28},{16,0},{20,4},{24,8},{28,12},{1,17},{... | collective-permute-start | bytes 589832 | tf_op jit(solution)/shard_map/ppermute | solution.py:861
  21.4 12.8 %collective-permute-start.4 = (bf16[4,48,640]{2,1,0:T(8,128)(2,1)S(1)}, bf16[4,48,640]{2,1,0:T(8,128)(2,1)S(1)}, u32[]{:S(2)}, u32[]{:S(2)}) collective-permute-start(bf16[4,48,640]{2,1,0:T(8,128)(2,1)S(1)} %get-tuple-element.158), channel_id=1, source_target_pairs={{0,4},{4,0},{8,12},{12,8},{16,20},{20,16},{24,28},{28,24},{1,5},{5... | collective-permute-start | bytes 737288 | tf_op jit(solution)/shard_map/ppermute | solution.py:861
  21.5 12.7 %collective-permute-start.5 = (bf16[4,48,640]{2,1,0:T(8,128)(2,1)S(1)}, bf16[4,48,640]{2,1,0:T(8,128)(2,1)S(1)}, u32[]{:S(2)}, u32[]{:S(2)}) collective-permute-start(bf16[4,48,640]{2,1,0:T(8,128)(2,1)S(1)} %get-tuple-element.159), channel_id=1, source_target_pairs={{0,2},{1,3},{2,0},{3,1},{4,6},{5,7},{6,4},{7,5},{8,10},{9,11},{10,... | collective-permute-start | bytes 737288 | tf_op jit(solution)/shard_map/ppermute | solution.py:861
  27.5 10.8 %collective-permute-start.3 = (bf16[2,96,1024]{2,1,0:T(8,128)(2,1)S(1)}, bf16[2,96,1024]{2,1,0:T(8,128)(2,1)S(1)}, u32[]{:S(2)}, u32[]{:S(2)}) collective-permute-start(bf16[2,96,1024]{2,1,0:T(8,128)(2,1)S(1)} %pad_maximum_fusion.9), channel_id=1, source_target_pairs={{0,8},{4,12},{8,0},{12,4},{16,24},{20,28},{24,16},{28,20},{1,9},{5... | collective-permute-start | bytes 1179656 | tf_op jit(solution)/shard_map/ppermute | solution.py:861
  34.9 14.2 %collective-permute-start.11 = (bf16[8,48,640]{2,1,0:T(8,128)(2,1)S(1)}, bf16[8,48,640]{2,1,0:T(8,128)(2,1)}, u32[]{:S(2)}, u32[]{:S(2)}) collective-permute-start(bf16[8,48,640]{2,1,0:T(8,128)(2,1)S(1)} %get-tuple-element.167.refs_0_), channel_id=1, source_target_pairs={{0,2},{1,3},{2,0},{3,1},{4,6},{5,7},{6,4},{7,5},{8,10},{9,11},{10,... | collective-permute-start | bytes 1474568 | tf_op jit(solution)/shard_map/ppermute | solution.py:861
  35.6 14.2 %collective-permute-start.12 = (bf16[8,48,640]{2,1,0:T(8,128)(2,1)S(1)}, bf16[8,48,640]{2,1,0:T(8,128)(2,1)}, u32[]{:S(2)}, u32[]{:S(2)}) collective-permute-start(bf16[8,48,640]{2,1,0:T(8,128)(2,1)S(1)} %get-tuple-element.168.refs_2_), channel_id=1, source_target_pairs={{0,4},{4,0},{8,12},{12,8},{16,20},{20,16},{24,28},{28,24},{1,5},{5... | collective-permute-start | bytes 1474568 | tf_op jit(solution)/shard_map/ppermute | solution.py:861
  38.5 18.4 %collective-permute-start.13 = (bf16[4,48,1024]{2,1,0:T(8,128)(2,1)S(1)}, bf16[4,48,1024]{2,1,0:T(8,128)(2,1)S(1)}, u32[]{:S(2)}, u32[]{:S(2)}) collective-permute-start(bf16[4,48,1024]{2,1,0:T(8,128)(2,1)S(1)} %get-tuple-element.173), channel_id=1, source_target_pairs={{0,4},{4,0},{8,12},{12,8},{16,20},{20,16},{24,28},{28,24},{1,5},{5... | collective-permute-start | bytes 1179656 | tf_op jit(solution)/shard_map/ppermute | solution.py:861
  40.1 16.8 %collective-permute-start.14 = (bf16[4,48,1024]{2,1,0:T(8,128)(2,1)S(1)}, bf16[4,48,1024]{2,1,0:T(8,128)(2,1)}, u32[]{:S(2)}, u32[]{:S(2)}) collective-permute-start(bf16[4,48,1024]{2,1,0:T(8,128)(2,1)S(1)} %get-tuple-element.174), channel_id=1, source_target_pairs={{0,2},{1,3},{2,0},{3,1},{4,6},{5,7},{6,4},{7,5},{8,10},{9,11},{10,... | collective-permute-start | bytes 1179656 | tf_op jit(solution)/shard_map/ppermute | solution.py:861
  58.9 20.8 %collective-permute-start.18 = (bf16[2,96,768]{2,1,0:T(8,128)(2,1)S(1)}, bf16[2,96,768]{2,1,0:T(8,128)(2,1)S(1)}, u32[]{:S(2)}, u32[]{:S(2)}) collective-permute-start(bf16[2,96,768]{2,1,0:T(8,128)(2,1)S(1)} %pad_maximum_fusion.11), channel_id=1, source_target_pairs={{0,8},{4,12},{8,0},{12,4},{16,24},{20,28},{24,16},{28,20},{1,9},{5... | collective-permute-start | bytes 884744 | tf_op jit(solution)/shard_map/ppermute | solution.py:861
  61.0 19.2 %collective-permute-start.19 = (bf16[8,48,1024]{2,1,0:T(8,128)(2,1)S(1)}, bf16[8,48,1024]{2,1,0:T(8,128)(2,1)S(1)}, u32[]{:S(2)}, u32[]{:S(2)}) collective-permute-start(bf16[8,48,1024]{2,1,0:T(8,128)(2,1)S(1)} %pad_maximum_fusion.1.refs_0_), channel_id=1, source_target_pairs={{0,2},{1,3},{2,0},{3,1},{4,6},{5,7},{6,4},{7,5},{8,10},{9,11},{10,... | collective-permute-start | bytes 2359304 | tf_op jit(solution)/shard_map/ppermute | solution.py:861
  62.5 19.0 %collective-permute-start.20 = (bf16[8,48,1024]{2,1,0:T(8,128)(2,1)S(1)}, bf16[8,48,1024]{2,1,0:T(8,128)(2,1)}, u32[]{:S(2)}, u32[]{:S(2)}) collective-permute-start(bf16[8,48,1024]{2,1,0:T(8,128)(2,1)S(1)} %pad_maximum_fusion.2.refs_2_), channel_id=1, source_target_pairs={{0,4},{4,0},{8,12},{12,8},{16,20},{20,16},{24,28},{28,24},{1,5},{5... | collective-permute-start | bytes 2359304 | tf_op jit(solution)/shard_map/ppermute | solution.py:861
  96.1 15.7 %collective-permute-start.27 = (bf16[8,48,768]{2,1,0:T(8,128)(2,1)S(1)}, bf16[8,48,768]{2,1,0:T(8,128)(2,1)S(1)}, u32[]{:S(2)}, u32[]{:S(2)}) collective-permute-start(bf16[8,48,768]{2,1,0:T(8,128)(2,1)S(1)} %pad_maximum_fusion.3.refs_8_), channel_id=1, source_target_pairs={{0,2},{1,3},{2,0},{3,1},{4,6},{5,7},{6,4},{7,5},{8,10},{9,11},{10,... | collective-permute-start | bytes 1769480 | tf_op jit(solution)/shard_map/ppermute | solution.py:861
  96.7 15.1 %collective-permute-start.30 = (bf16[8,48,768]{2,1,0:T(8,128)(2,1)S(1)}, bf16[8,48,768]{2,1,0:T(8,128)(2,1)S(1)}, u32[]{:S(2)}, u32[]{:S(2)}) collective-permute-start(bf16[8,48,768]{2,1,0:T(8,128)(2,1)S(1)} %pad_maximum_fusion.4.refs_10_), channel_id=1, source_target_pairs={{0,1},{1,0},{2,3},{3,2},{4,5},{5,4},{6,7},{7,6},{8,9},{9,8},{10,11... | collective-permute-start | bytes 1769480 | tf_op jit(solution)/shard_map/ppermute | solution.py:861
  96.9 15.7 %collective-permute-start.28 = (bf16[8,48,768]{2,1,0:T(8,128)(2,1)S(1)}, bf16[8,48,768]{2,1,0:T(8,128)(2,1)}, u32[]{:S(2)}, u32[]{:S(2)}) collective-permute-start(bf16[8,48,768]{2,1,0:T(8,128)(2,1)S(1)} %pad_maximum_fusion.4.refs_10_), channel_id=1, source_target_pairs={{0,4},{4,0},{8,12},{12,8},{16,20},{20,16},{24,28},{28,24},{1,5},{5... | collective-permute-start | bytes 1769480 | tf_op jit(solution)/shard_map/ppermute | solution.py:861
  152.4 12.4 %collective-permute-start.33 = (bf16[2,8,96,1536]{3,2,1,0:T(8,128)(2,1)}, bf16[2,8,96,1536]{3,2,1,0:T(8,128)(2,1)}, u32[]{:S(2)}, u32[]{:S(2)}) collective-permute-start(bf16[2,8,96,1536]{3,2,1,0:T(8,128)(2,1)} %get-tuple-element.225), channel_id=1, source_target_pairs={{0,1},{1,0},{2,3},{3,2},{4,5},{5,4},{6,7},{7,6},{8,9},{9,8},{10,11... | collective-permute-start | bytes 14155784 | tf_op jit(solution)/shard_map/ppermute | solution.py:861
  173.0 32.7 %collective-permute-start.35 = (bf16[8,48,1792]{2,1,0:T(8,128)(2,1)}, bf16[8,48,1792]{2,1,0:T(8,128)(2,1)S(1)}, u32[]{:S(2)}, u32[]{:S(2)}) collective-permute-start(bf16[8,48,1792]{2,1,0:T(8,128)(2,1)} %get-tuple-element.240), channel_id=1, source_target_pairs={{0,2},{1,3},{2,0},{3,1},{4,6},{5,7},{6,4},{7,5},{8,10},{9,11},{10,... | collective-permute-start | bytes 4128776 | tf_op jit(solution)/shard_map/ppermute | solution.py:861
  174.4 32.4 %collective-permute-start.36 = (bf16[2,4,48,1792]{3,2,1,0:T(8,128)(2,1)}, bf16[2,4,48,1792]{3,2,1,0:T(8,128)(2,1)S(1)}, u32[]{:S(2)}, u32[]{:S(2)}) collective-permute-start(bf16[2,4,48,1792]{3,2,1,0:T(8,128)(2,1)} %get-tuple-element.241), channel_id=1, source_target_pairs={{0,4},{4,0},{8,12},{12,8},{16,20},{20,16},{24,28},{28,24},{1,5},{5... | collective-permute-start | bytes 4128776 | tf_op jit(solution)/shard_map/ppermute | solution.py:861
  213.8 18.5 %collective-permute-start.38 = (bf16[4,48,1792]{2,1,0:T(8,128)(2,1)}, bf16[4,48,1792]{2,1,0:T(8,128)(2,1)S(1)}, u32[]{:S(2)}, u32[]{:S(2)}) collective-permute-start(bf16[4,48,1792]{2,1,0:T(8,128)(2,1)} %get-tuple-element.249), channel_id=1, source_target_pairs={{0,4},{4,0},{8,12},{12,8},{16,20},{20,16},{24,28},{28,24},{1,5},{5... | collective-permute-start | bytes 2064392 | tf_op jit(solution)/shard_map/ppermute | solution.py:861
  214.4 18.5 %collective-permute-start.39 = (bf16[4,48,1792]{2,1,0:T(8,128)(2,1)}, bf16[4,48,1792]{2,1,0:T(8,128)(2,1)S(1)}, u32[]{:S(2)}, u32[]{:S(2)}) collective-permute-start(bf16[4,48,1792]{2,1,0:T(8,128)(2,1)} %get-tuple-element.250), channel_id=1, source_target_pairs={{0,2},{1,3},{2,0},{3,1},{4,6},{5,7},{6,4},{7,5},{8,10},{9,11},{10,... | collective-permute-start | bytes 2064392 | tf_op jit(solution)/shard_map/ppermute | solution.py:861
  218.8 31.1 %collective-permute-start.40 = (bf16[8,48,640]{2,1,0:T(8,128)(2,1)}, bf16[8,48,640]{2,1,0:T(8,128)(2,1)S(1)}, u32[]{:S(2)}, u32[]{:S(2)}) collective-permute-start(bf16[8,48,640]{2,1,0:T(8,128)(2,1)} %get-tuple-element.268), channel_id=1, source_target_pairs={{0,2},{1,3},{2,0},{3,1},{4,6},{5,7},{6,4},{7,5},{8,10},{9,11},{10,... | collective-permute-start | bytes 1474568 | tf_op jit(solution)/shard_map/ppermute | solution.py:861
  220.1 29.8 %collective-permute-start.41 = (bf16[2,4,48,640]{3,2,1,0:T(8,128)(2,1)}, bf16[2,4,48,640]{3,2,1,0:T(8,128)(2,1)S(1)}, u32[]{:S(2)}, u32[]{:S(2)}) collective-permute-start(bf16[2,4,48,640]{3,2,1,0:T(8,128)(2,1)} %get-tuple-element.269), channel_id=1, source_target_pairs={{0,4},{4,0},{8,12},{12,8},{16,20},{20,16},{24,28},{28,24},{1,5},{5... | collective-permute-start | bytes 1474568 | tf_op jit(solution)/shard_map/ppermute | solution.py:861
  237.0 18.2 %collective-permute-start.42 = (bf16[2,96,1792]{2,1,0:T(8,128)(2,1)}, bf16[2,96,1792]{2,1,0:T(8,128)(2,1)S(1)}, u32[]{:S(2)}, u32[]{:S(2)}) collective-permute-start(bf16[2,96,1792]{2,1,0:T(8,128)(2,1)} %get-tuple-element.275), channel_id=1, source_target_pairs={{0,8},{4,12},{8,0},{12,4},{16,24},{20,28},{24,16},{28,20},{1,9},{5... | collective-permute-start | bytes 2064392 | tf_op jit(solution)/shard_map/ppermute | solution.py:861
  255.5 18.3 %collective-permute-start.51 = (bf16[96,1792]{1,0:T(8,128)(2,1)S(1)}, bf16[96,1792]{1,0:T(8,128)(2,1)S(1)}, u32[]{:S(2)}, u32[]{:S(2)}) collective-permute-start(bf16[96,1792]{1,0:T(8,128)(2,1)S(1)} %fusion.3), channel_id=1, source_target_pairs={{0,16},{4,20},{8,24},{12,28},{16,0},{20,4},{24,8},{28,12},{1,17},{... | collective-permute-start | bytes 1032200 | tf_op jit(solution)/shard_map/ppermute | solution.py:861
  (84 other events, 619.0 us)

commit v4 on v3

--- a/solution.py
+++ b/solution.py
@@ -495,7 +495,7 @@
 
 def feed(mine, normed, grad_down, unit_bias, groups, units, images):
     rows, width = normed.shape
-    blocks = 2 if images <= 4 else 4
+    blocks = max(1, images // 4)
     parts = len(groups)
     sub = units // parts
     pieces, layout = [], []
@@ -1049,10 +1049,10 @@
     first, last = pack_attention(attention_weights.astype(LOW))
     mlp_low = mlp_weights.astype(LOW)
     units = mlp_low.shape[2]
-    part = units // 2
     unit_bias = norm_params[8:].reshape(LANES, 1, units)
-    second = jnp.concatenate([last, mlp_low[0, :, :part], mlp_low[1, :, :part]], axis=1)
-    third = jnp.concatenate([mlp_low[0, :, part:], mlp_low[1, :, part:]], axis=1)
+    first = jnp.concatenate([first, last], axis=1)
+    second = jnp.concatenate([mlp_low[0], mlp_low[1]], axis=1)
+    out_at = (PACK, PACK + OUT_PACK)
     if near:
         mine = jnp.stack([lax.axis_index("dp"), lane_index, lane_index]).astype(jnp.int32)
         core = lambda values: swap(values, "mp", 1)
@@ -1060,41 +1060,34 @@
         y_axis = lambda values: swap(values, "dp", 1)
         z_near = lambda values: swap(values, "dp", 2)
         z_far = lambda values: swap(values, "dp", 4)
-        one, two, three = first[None], second[None], third[None]
+        one, two = first[None], second[None]
         got = z_far(one)
         normed_one, grad_down = first_norm(block_input, cotangent, norm_params, images)
-        got, normed_one = sync(got, normed_one)
+        got, normed_one, other = sync(got, normed_one, x_axis(after(head_params, first)))
         one = join(one, got)
         got = z_near(one)
         two_got = z_far(after(two, one))
-        other = x_axis(after(head_params, one))
-        near_table, far_table = core(head_params), core(other)
+        got, near_table, far_table = sync(got, core(head_params), core(other))
         upper, lower = split_rows(join(one, got))
         upper, lower = sync(upper, lower)
         upper_got, lower_got = y_axis(upper), x_axis(lower)
+        upper_got, lower_got = sync(upper_got, lower_got)
+        upper, lower = sync(join(upper, upper_got), join(lower, lower_got))
+        upper_far, lower_far = x_axis(upper), y_axis(lower)
         two = join(two, after(two_got, upper, lower))
         two_got = z_near(two)
         bias, add = spread_bias(
             (head_params, after(near_table, two), other, after(far_table, two)), thin
         )
-        upper_got, lower_got, bias = sync(upper_got, lower_got, bias)
-        upper, lower = sync(join(upper, upper_got), join(lower, lower_got))
-        upper_far, lower_far = x_axis(upper), y_axis(lower)
         near_core = sync(core(upper), core(lower))
-        two_upper, two_lower = split_rows(join(two, after(two_got, upper, lower)))
-        two_upper, two_lower, three = sync(two_upper, two_lower, after(three, *near_core))
-        two_upper_got, two_lower_got = y_axis(two_upper), x_axis(two_lower)
-        three_got = z_far(three)
-        upper_far, lower_far, two_upper_got, two_lower_got, three_got = sync(
-            upper_far, lower_far, two_upper_got, two_lower_got, three_got
+        upper_far, lower_far, two_got, bias = sync(
+            upper_far, lower_far, after(two_got, *near_core), bias
         )
         far_core = sync(core(upper_far), core(lower_far))
-        three = join(three, three_got)
         first_all = pieces_of(upper, upper_far, lower, lower_far, near_core, far_core)
-        two_upper, two_lower = join(two_upper, two_upper_got), join(two_lower, two_lower_got)
-        two_upper, two_lower, three, normed_one = sync(two_upper, two_lower, three, normed_one)
-        two_upper_far, two_lower_far = x_axis(two_upper), y_axis(two_lower)
-        three_got = z_near(three)
+        two_upper, two_lower = split_rows(join(two, two_got))
+        two_upper, two_lower, normed_one = sync(two_upper, two_lower, normed_one)
+        two_upper_got, two_lower_got = y_axis(two_upper), x_axis(two_lower)
     else:
         mine = jnp.stack([0 * lane_index, 0 * lane_index, lane_index]).astype(jnp.int32)
 
@@ -1114,40 +1107,30 @@
         bias, add = spread_bias(tables, thin)
         first_all = gather_far(first)
         second_all = gather_far(second)
-        third_all = gather_far(third)
 
     qkv, prob, ctx = attend(mine, image_size, normed_one, bias, add, first_all, images)
     if near:
-        ctx, three_got, two_upper_far, two_lower_far = sync(
-            ctx, three_got, two_upper_far, two_lower_far
+        ctx, two_upper_got, two_lower_got = sync(ctx, two_upper_got, two_lower_got)
+        two_upper, two_lower, ctx = sync(
+            join(two_upper, two_upper_got), join(two_lower, two_lower_got), ctx
         )
-        three_upper, three_lower, two_upper, two_lower = sync(
-            *split_rows(join(three, three_got)), two_upper, two_lower
+        near_two = (core(two_upper), core(two_lower))
+        far_two = (x_axis(two_upper), y_axis(two_lower))
+    att, mid, normed_two = middle(
+        mine, ctx, block_input, norm_params, first_all, out_at, images
+    )
+    if near:
+        normed_two, *far_two = sync(normed_two, *far_two, *near_two)
+        far_two, near_two = far_two[:2], far_two[2:]
+        second_all = pieces_of(
+            two_upper,
+            far_two[0],
+            two_lower,
+            far_two[1],
+            near_two,
+            sync(core(far_two[0]), core(far_two[1])),
         )
-        three_upper_got, three_lower_got = y_axis(three_upper), x_axis(three_lower)
-        two_near = sync(core(two_upper), core(two_lower))
-        two_far = (core(after(two_upper_far, *two_near)), core(after(two_lower_far, *two_near)))
-        two_near, two_far, three_upper_got, three_lower_got = sync(
-            two_near, two_far, three_upper_got, three_lower_got
-        )
-        second_all = pieces_of(two_upper, two_upper_far, two_lower, two_lower_far, two_near, two_far)
-        three_upper, three_lower, ctx = sync(
-            join(three_upper, three_upper_got), join(three_lower, three_lower_got), ctx
-        )
-        three_upper_far, three_lower_far = x_axis(three_upper), y_axis(three_lower)
-        three_near = (core(three_upper), core(three_lower))
-    att, mid, normed_two = middle(
-        mine, ctx, block_input, norm_params, second_all, (0, OUT_PACK), images
-    )
-    if near:
-        normed_two, three_upper_far, three_lower_far, three_near = sync(
-            normed_two, three_upper_far, three_lower_far, three_near
-        )
-        three_far = (core(three_upper_far), core(three_lower_far))
-        third_all = pieces_of(
-            three_upper, three_upper_far, three_lower, three_lower_far, three_near, three_far
-        )
-    groups = ((second_all, OUT_PACK, OUT_PACK + part), (third_all, 0, part))
+    groups = ((second_all, 0, units),)
     down, grad_normed, keep_mlp, send_mlp, unit_sums = feed(
         mine, normed_two, grad_down, unit_bias, groups, units, images
     )
@@ -1162,53 +1145,54 @@
         upper, lower, grad_att = sync(*sum_away(keeps, gots), grad_att)
         upper_got, lower_got = x_axis(upper), y_axis(lower)
     dqkv, pair, cols = back(
-        mine, grad_att, qkv, prob, second_all, (0, OUT_PACK), images
+        mine, grad_att, qkv, prob, first_all, out_at, images
     )
     keep_att, send_att = project(mine, normed_one, dqkv)
+    grad_heads = heads_back(after(pair, keep_att), cols, thin)
     if near:
-        keep_att, send_att, upper_got, lower_got = sync(keep_att, send_att, upper_got, lower_got)
+        keep_att, send_att, upper_got, lower_got, grad_heads = sync(
+            keep_att, send_att, upper_got, lower_got, grad_heads
+        )
         att_core = core(send_att)
         upper, upper_away, lower, lower_away = sum_here(keeps, gots, upper_got, lower_got)
-        upper_away, lower_away, att_core, pair = sync(upper_away, lower_away, att_core, pair)
+        upper_away, lower_away, att_core = sync(upper_away, lower_away, att_core)
         upper_got, lower_got = y_axis(upper_away), x_axis(lower_away)
         keeps, gots = (keep_att,), (att_core,)
-        att_upper, att_lower, pair = sync(*sum_away(keeps, gots), pair)
+        att_upper, att_lower, dqkv = sync(*sum_away(keeps, gots), dqkv)
         att_upper_got, att_lower_got = x_axis(att_upper), y_axis(att_lower)
-    grad_heads = heads_back(pair, cols, thin)
-    if near:
-        upper_got, lower_got, grad_heads = sync(upper_got, lower_got, grad_heads)
-        line, line_away = sum_line(upper, upper_got, lower, lower_got)
-        line_away, dqkv = sync(line_away, dqkv)
-        line_got = z_near(line_away)
-        upper_got, lower_got = att_upper_got, att_lower_got
     grad_input, first_rows = input_back(
         mine, dqkv, grad_mid, block_input, norm_params, first_all, images
     )
-
     norms = jnp.concatenate([first_rows, second_rows, unit_sums.reshape(-1, width)], axis=0)
     if near:
-        norms, upper_got, lower_got = sync(norms, upper_got, lower_got)
+        count = norms.shape[0]
+        rest = count + local_heads
+        norms, *heads = sync(norms, *[grad_heads[index] for index in range(LANES)])
+        norms = jnp.pad(norms, ((0, 0), (0, grad_heads.shape[2] - width)))
+        keep = jnp.concatenate([norms, heads[0], heads[2]], axis=0)
+        small_got = core(jnp.concatenate([norms, heads[1], heads[3]], axis=0))
+        upper_got, lower_got, small_got = sync(upper_got, lower_got, small_got)
+        line, line_away = sum_line(upper, upper_got, lower, lower_got)
+        line_got = z_near(line_away)
+        small = keep + small_got
+        small_got = x_axis(join(small[:count], small[rest:]))
+        upper_got, lower_got, line_away, small_got = sync(
+            att_upper_got, att_lower_got, line_away, small_got
+        )
+        small = small[:rest] + small_got
         upper, upper_away, lower, lower_away = sum_here(keeps, gots, upper_got, lower_got)
-        upper_away, lower_away, norms, line_got = sync(upper_away, lower_away, norms, line_got)
+        upper_away, lower_away, small = sync(upper_away, lower_away, small)
         upper_got, lower_got = y_axis(upper_away), x_axis(lower_away)
-        heads_width = grad_heads.shape[2]
-        count = norms.shape[0]
-        norms = jnp.pad(norms, ((0, 0), (0, heads_width - width)))
-        packs = [join(norms, grad_heads[index]) for index in range(LANES)]
-        small = (packs[0] + core(packs[1])) + (x_axis(packs[2]) + swap(packs[3], "mp", 3))
-        small, upper_got, lower_got = sync(small, upper_got, lower_got)
+        small_got = y_axis(small)
         here, away = sum_line(upper, upper_got, lower, lower_got)
-        small, here, away = sync(small, here, away)
-        got = z_near(away)
-        small_got = y_axis(small)
+        small_got, line_got, away = sync(small_got, line_got, away)
         line = line + line_got.astype(FULL)
-        line_got = z_far(line[1].astype(LOW))
-        got, small_got = sync(got, small_got)
+        small, line_away = sync(small + small_got, line[1].astype(LOW))
+        got, line_got = z_near(away), z_far(line_away)
+        came = (z_near(small), z_far(small), swap(small, "dp", 6))
         here = here + got.astype(FULL)
-        small = small + small_got
-        away, small = sync(here[1].astype(LOW), small)
-        got = z_far(away)
-        small = (small + z_near(small)) + (z_far(small) + swap(small, "dp", 6))
+        got = z_far(here[1].astype(LOW))
+        small = (small + came[0]) + (came[1] + came[2])
         sum_mlp = line[0] + line_got.astype(FULL)
         sum_att = here[0] + got.astype(FULL)
         sum_mlp, sum_out = sum_mlp[:, : 2 * units], sum_mlp[:, 2 * units :]

time: 294 us -> 289 us (0.983)
  starting transfers between devices: 52.3 us -> 42.5 us
  waiting for transfers between devices: 74.9 us -> 81.9 us
    ppermute x55 -> x44, starting transfers between devices: 52.3 us -> 42.5 us  [swap(): lax.ppermute(values, axis, [(index, index ^ bit) for index in range(count)])]
    ppermute x55 -> x44, waiting for transfers between devices: 74.9 us -> 81.9 us  [swap(): lax.ppermute(values, axis, [(index, index ^ bit) for index in range(count)])]
    unnamed x107 -> x90, local copies, waits for them, and re-layouts: 7.99 us -> 7.48 us
  transfers between devices with their start and end apart: 55 -> 44, of which waited for: 30 -> 26; matrix products, arithmetic and copies ran while one was open for 3% -> 2% of each run, Pallas kernels for 36% -> 37%
where the time goes in v4:
time: 289 us; the launch traced here: 288 us
  Pallas kernels  146 us (51%)
  waiting for transfers between devices  81.9 us (28%)
  starting transfers between devices  42.5 us (15%)
  local copies, waits for them, and re-layouts  8.71 us (3%)
  other arithmetic  7.12 us (2%)
    ppermute x44, waiting for transfers between devices, swap(): lax.ppermute(values, axis, [(index, index ^ bit) for index in range(count)])  81.9 us
    ppermute x44, starting transfers between devices, swap(): lax.ppermute(values, axis, [(index, index ^ bit) for index in range(count)])  42.5 us
    pallas_call x1, Pallas kernels, feed(): pl.pallas_call(functools.partial(feed_body, blocks, layout), grid=(LANES,...  35.5 us
    pallas_call x6, Pallas kernels, sum_call(): pl.pallas_call(body, grid=(grid,), in_specs=[pl.BlockSpec(block, index) f...  23.5 us
    pallas_call x1, Pallas kernels, attend(): pl.pallas_call(functools.partial(attend_body, table, images), grid=(LANES...  15.7 us
    pallas_call x1, Pallas kernels, back(): pl.pallas_call(functools.partial(back_body, table, columns, images), grid...  15 us
    pallas_call x1, Pallas kernels, second_back(): pl.pallas_call(second_body, grid=(images,), in_specs=[pl.BlockSpec(memory...  12.2 us
    pallas_call x1, Pallas kernels, input_back(): pl.pallas_call(functools.partial(input_body, table), grid=(images // TWO,...  12 us
  transfers between devices with their start and end apart: 44, of which 26 were waited for; matrix products, arithmetic and copies ran while one was open for 2% of the time, Pallas kernels for 37%

profile of v4, /device:TPU:0, one launch (start us, length us, event | category | flops | bytes accessed | tf_op | source)
XLA Modules:
  0.0 287.6 jit_solution(8724881799585820127)
XLA Ops:
  7.5 5.0 %shard_map.272 = (bf16[832,768]{1,0:T(8,128)(2,1)}, bf16[832,768]{1,0:T(8,128)(2,1)}) custom-call(f32[784,768]{1,0:T(8,128)} %x_ref.5, f32[784,768]{1,0:T(8,128)} %cot_ref.3, f32[12,768]{1,0:T(8,128)} %vec_ref.7), custom_call_target="tpu_custom_call" | custom-call | flops 3000000000 | bytes 4000000 | tf_op jit(solution)/shard_map/pallas_call | solution.py:147
  17.6 6.8 %collective-permute-done.3 = bf16[2,96,896]{2,1,0:T(8,128)(2,1)S(1)} collective-permute-done((bf16[2,96,896]{2,1,0:T(8,128)(2,1)S(1)}, bf16[2,96,896]{2,1,0:T(8,128)(2,1)S(1)}, u32[]{:S(2)}, u32[]{:S(2)}) %collective-permute-start.3) | collective-permute-done | bytes 344096 | tf_op jit(solution)/shard_map/ppermute | solution.py:861
  26.7 3.4 %collective-permute-start.2 = (bf16[1,96,1536]{2,1,0:T(8,128)(2,1)S(1)}, bf16[1,96,1536]{2,1,0:T(8,128)(2,1)S(1)}, u32[]{:S(2)}, u32[]{:S(2)}) collective-permute-start(bf16[1,96,1536]{2,1,0:T(8,128)(2,1)S(1)} %maximum_bitcast_fusion), channel_id=1, source_target_pairs={{0,16},{4,20},{8,24},{12,28},{16,0},{20,4},{24,8},{28,12},{1,17},{... | collective-permute-start | bytes 884744 | tf_op jit(solution)/shard_map/ppermute | solution.py:861
  35.8 6.8 %collective-permute-done.2 = bf16[1,96,1536]{2,1,0:T(8,128)(2,1)S(1)} collective-permute-done((bf16[1,96,1536]{2,1,0:T(8,128)(2,1)S(1)}, bf16[1,96,1536]{2,1,0:T(8,128)(2,1)S(1)}, u32[]{:S(2)}, u32[]{:S(2)}) %collective-permute-start.2) | collective-permute-done | bytes 294944 | tf_op jit(solution)/shard_map/ppermute | solution.py:861
  44.6 5.3 %shard_map.273 = (f32[12,208,208]{2,1,0:T(8,128)}, f32[4,1,640]{2,1,0:T(1,128)}) custom-call(f32[3,857]{1,0:T(4,128)} %t0.1, f32[3,857]{1,0:T(4,128)} %copy-done.42, f32[3,857]{1,0:T(4,128)} %copy-done.41, f32[3,857]{1,0:T(4,128)} %copy-done.43, bf16[768,384]{1,0:T(8,128)(2,1)} %constant.32.clone.thin_ref), custom_call_target="tpu_custom_call" | custom-call | flops 3000000000 | bytes 4000000 | tf_op jit(solution)/shard_map/pallas_call | solution.py:211
  50.0 7.0 %collective-permute-done.10 = bf16[2,96,1536]{2,1,0:T(8,128)(2,1)S(1)} collective-permute-done((bf16[2,96,1536]{2,1,0:T(8,128)(2,1)S(1)}, bf16[2,96,1536]{2,1,0:T(8,128)(2,1)S(1)}, u32[]{:S(2)}, u32[]{:S(2)}) %collective-permute-start.10) | collective-permute-done | bytes 589856 | tf_op jit(solution)/shard_map/ppermute | solution.py:861
  60.7 15.7 %shard_map.274 = (bf16[4,832,640]{2,1,0:T(8,128)(2,1)}, bf16[4,12,208,208]{3,2,1,0:T(8,128)(2,1)}, bf16[832,1024]{1,0:T(8,128)(2,1)}) custom-call(s32[3]{0:T(128)} %pad_add_fusion.me_ref, s32[16,2]{1,0:T(8,128)} %copy.31.size_ref, s32[2,208,128]{2,1,0:T(8,128)} %constant.33.clone.grid_ref, bf16[832,768]{1,0:T(8,128)(2,1)} %get-tuple-element.161.n_ref, ...), custom_call_target="tpu_custom_call" | custom-call | flops 15000000512 | bytes 20000000 | tf_op jit(solution)/shard_map/pallas_call | solution.py:322
  79.0 7.4 %shard_map.275 = (bf16[832,768]{1,0:T(8,128)(2,1)}, f32[832,768]{1,0:T(8,128)}, bf16[832,768]{1,0:T(8,128)(2,1)}) custom-call(s32[3]{0:T(128)} %pad_add_fusion.me_ref, bf16[832,1024]{1,0:T(8,128)(2,1)} %get-tuple-element.173.ctx_ref, f32[784,768]{1,0:T(8,128)} %x_ref.5, f32[12,768]{1,0:T(8,128)} %vec_ref.7, bf16[8,48,896]{2,1,0:T(8,128)(2,1)} %copy-done.16, ...), custom_call_target="tpu_custom_call" | custom-call | flops 8000000000 | bytes 15000000 | tf_op jit(solution)/shard_map/pallas_call | solution.py:383
  86.5 18.7 %collective-permute-done.17.refs_1_ = bf16[8,48,1536]{2,1,0:T(8,128)(2,1)} collective-permute-done((bf16[8,48,1536]{2,1,0:T(8,128)(2,1)S(1)}, bf16[8,48,1536]{2,1,0:T(8,128)(2,1)}, u32[]{:S(2)}, u32[]{:S(2)}) %collective-permute-start.17) | collective-permute-done | bytes 1179680 | tf_op jit(solution)/shard_map/ppermute | solution.py:861
  112.4 35.5 %shard_map.276 = (f32[832,768]{1,0:T(8,128)}, f32[832,768]{1,0:T(8,128)}, bf16[2,8,96,1536]{3,2,1,0:T(8,128)(2,1)}, bf16[2,8,96,1536]{3,2,1,0:T(8,128)(2,1)}, f32[4,1,768]{2,1,0:T(1,128)}) custom-call(s32[3]{0:T(128)} %pad_add_fusion.me_ref, bf16[832,768]{1,0:T(8,128)(2,1)} %get-tuple-element.177.n_ref, bf16[832,768]{1,0:T(8,128)(2,1)} %get-tuple-element.178.gd_ref, ...), custom_call_target="tpu_custom_call" | custom-call | flops 35000000512 | bytes 40000000 | tf_op jit(solution)/shard_map/pallas_call | solution.py:508
  148.1 12.2 %shard_map.277 = (f32[784,768]{1,0:T(8,128)}, f32[832,768]{1,0:T(8,128)}, bf16[832,768]{1,0:T(8,128)(2,1)}, bf16[2,8,96,256]{3,2,1,0:T(8,128)(2,1)}, bf16[2,8,96,256]{3,2,1,0:T(8,128)(2,1)}, /*index=5*/f32[6,768]{1,0:T(8,128)}) custom-call(s32[3]{0:T(128)} %pad_add_fusion.me_ref, f32[832,768]{1,0:T(8,128)} %get-tuple-element.185.down_ref, ...), custom_call_target="tpu_custom_call" | custom-call | flops 10000000000 | bytes 20000000 | tf_op jit(solution)/shard_map/pallas_call | solution.py:600
  163.9 4.7 %shard_map.278 = (bf16[8,48,1792]{2,1,0:T(8,128)(2,1)}, bf16[2,4,48,1792]{3,2,1,0:T(8,128)(2,1)}) custom-call(bf16[2,8,96,1536]{3,2,1,0:T(8,128)(2,1)} %get-tuple-element.190.refs_0_.refs_1_.refs_4_.refs_5_.refs_6_.refs_7_, bf16[2,8,96,1536]{3,2,1,0:T(8,128)(2,1)} %get-tuple-element.190.refs_0_.refs_1_.refs_4_.refs_5_.refs_6_.refs_7_, ...), custom_call_target="tpu_custom_call" | custom-call | flops 1000000 | bytes 8000000 | tf_op jit(solution)/shard_map/pallas_call | solution.py:901
  170.6 15.0 %shard_map.279 = (bf16[4,832,640]{2,1,0:T(8,128)(2,1)}, f32[12,208,208]{2,1,0:T(8,128)}, f32[4,8,384]{2,1,0:T(8,128)}) custom-call(s32[3]{0:T(128)} %pad_add_fusion.me_ref, bf16[832,768]{1,0:T(8,128)(2,1)} %get-tuple-element.200.ga_ref, bf16[4,832,640]{2,1,0:T(8,128)(2,1)} %get-tuple-element.201.qkv_ref, ...), custom_call_target="tpu_custom_call" | custom-call | flops 30000001024 | bytes 40000000 | tf_op jit(solution)/shard_map/pallas_call | solution.py:713
  185.6 8.8 %shard_map.280 = (bf16[2,8,96,640]{3,2,1,0:T(8,128)(2,1)}, bf16[2,8,96,640]{3,2,1,0:T(8,128)(2,1)}) custom-call(s32[3]{0:T(128)} %pad_add_fusion.me_ref, bf16[832,768]{1,0:T(8,128)(2,1)} %get-tuple-element.161.n_ref, bf16[4,832,640]{2,1,0:T(8,128)(2,1)} %get-tuple-element.220.dqkv_ref), custom_call_target="tpu_custom_call" | custom-call | flops 8000000000 | bytes 10000000 | tf_op jit(solution)/shard_map/pallas_call | solution.py:795
  194.4 5.4 %shard_map.281 = f32[4,3,857]{2,1,0:T(4,128)} custom-call(f32[12,208,208]{2,1,0:T(8,128)} %get-tuple-element.209.pair_ref, f32[4,8,384]{2,1,0:T(8,128)} %get-tuple-element.210.cols_ref, bf16[768,384]{1,0:T(8,128)(2,1)} %constant.32.clone.thin_ref), custom_call_target="tpu_custom_call" | custom-call | flops 3000000000 | bytes 4000000 | tf_op jit(solution)/shard_map/pallas_call | solution.py:774
  202.8 5.9 %shard_map.282 = (f32[4,48,1792]{2,1,0:T(8,128)}, bf16[4,48,1792]{2,1,0:T(8,128)(2,1)}, f32[4,48,1792]{2,1,0:T(8,128)}, bf16[4,48,1792]{2,1,0:T(8,128)(2,1)}) custom-call(bf16[8,48,1792]{2,1,0:T(8,128)(2,1)} %copy-done.2, bf16[8,48,1792]{2,1,0:T(8,128)(2,1)} %copy-done.2, bf16[2,4,48,1792]{3,2,1,0:T(8,128)(2,1)} %copy-done.3, ...), custom_call_target="tpu_custom_call" | custom-call | flops 1000000 | bytes 12000000 | tf_op jit(solution)/shard_map/pallas_call | solution.py:901
  210.9 3.6 %shard_map.283 = (bf16[8,48,640]{2,1,0:T(8,128)(2,1)}, bf16[2,4,48,640]{3,2,1,0:T(8,128)(2,1)}) custom-call(bf16[2,8,96,640]{3,2,1,0:T(8,128)(2,1)} %get-tuple-element.211.refs_0_.refs_1_.refs_4_.refs_5_.refs_6_.refs_7_, bf16[2,8,96,640]{3,2,1,0:T(8,128)(2,1)} %get-tuple-element.211.refs_0_.refs_1_.refs_4_.refs_5_.refs_6_.refs_7_, ...), custom_call_target="tpu_custom_call" | custom-call | flops 1000000 | bytes 8000000 | tf_op jit(solution)/shard_map/pallas_call | solution.py:901
  214.6 12.0 %shard_map.284 = (f32[784,768]{1,0:T(8,128)}, f32[2,768]{1,0:T(2,128)}) custom-call(s32[3]{0:T(128)} %pad_add_fusion.me_ref, bf16[4,832,640]{2,1,0:T(8,128)(2,1)} %get-tuple-element.220.dqkv_ref, f32[832,768]{1,0:T(8,128)} %get-tuple-element.221.gm_ref, f32[784,768]{1,0:T(8,128)} %x_ref.5, f32[12,768]{1,0:T(8,128)} %vec_ref.7, ...), custom_call_target="tpu_custom_call" | custom-call | flops 15000000512 | bytes 15000000 | tf_op jit(solution)/shard_map/pallas_call | solution.py:834
  231.9 3.3 %shard_map.285 = (f32[2,96,1792]{2,1,0:T(8,128)}, bf16[2,96,1792]{2,1,0:T(8,128)(2,1)}) custom-call(f32[4,48,1792]{2,1,0:T(8,128)} %get-tuple-element.225.refs_0_.refs_1_, f32[4,48,1792]{2,1,0:T(8,128)} %get-tuple-element.225.refs_0_.refs_1_, bf16[4,48,1792]{2,1,0:T(8,128)(2,1)} %copy-done.4, bf16[4,48,1792]{2,1,0:T(8,128)(2,1)} %copy-done.4, ...), custom_call_target="tpu_custom_call" | custom-call | flops 1000000 | bytes 6000000 | tf_op jit(solution)/shard_map/pallas_call | solution.py:901
  242.3 3.8 %shard_map.286 = (f32[4,48,640]{2,1,0:T(8,128)}, bf16[4,48,640]{2,1,0:T(8,128)(2,1)}, f32[4,48,640]{2,1,0:T(8,128)}, bf16[4,48,640]{2,1,0:T(8,128)(2,1)}) custom-call(bf16[8,48,640]{2,1,0:T(8,128)(2,1)} %copy-done.8, bf16[8,48,640]{2,1,0:T(8,128)(2,1)} %copy-done.8, bf16[2,4,48,640]{3,2,1,0:T(8,128)(2,1)} %copy-done.9, bf16[2,4,48,640]{3,2,1,0:T(8,128)(2,1)} %copy-done.9, ...), custom_call_target="tpu_custom_call" | custom-call | flops 1000000 | bytes 12000000 | tf_op jit(solution)/shard_map/pallas_call | solution.py:901
  249.2 4.4 %collective-permute-done.34.refs_2_.refs_3_ = bf16[4,48,640]{2,1,0:T(8,128)(2,1)S(1)} collective-permute-done((bf16[4,48,640]{2,1,0:T(8,128)(2,1)}, bf16[4,48,640]{2,1,0:T(8,128)(2,1)S(1)}, u32[]{:S(2)}, u32[]{:S(2)}) %collective-permute-start.34) | collective-permute-done | bytes 245792 | tf_op jit(solution)/shard_map/ppermute | solution.py:861
  257.0 4.4 %collective-permute-start.43 = (f32[15,857]{1,0:T(8,128)S(1)}, f32[15,857]{1,0:T(8,128)S(1)}, u32[]{:S(2)}, u32[]{:S(2)}) collective-permute-start(f32[15,857]{1,0:T(8,128)S(1)} %add.85), channel_id=1, source_target_pairs={{0,24},{4,28},{8,16},{12,20},{16,8},{20,12},{24,0},{28,4},{1,25},{... | collective-permute-start | bytes 154268 | tf_op jit(solution)/shard_map/ppermute | solution.py:861
  270.3 5.0 %collective-permute-done.38 = bf16[2,96,640]{2,1,0:T(8,128)(2,1)S(1)} collective-permute-done((bf16[2,96,640]{2,1,0:T(8,128)(2,1)S(1)}, bf16[2,96,640]{2,1,0:T(8,128)(2,1)S(1)}, u32[]{:S(2)}, u32[]{:S(2)}) %collective-permute-start.38) | collective-permute-done | bytes 245792 | tf_op jit(solution)/shard_map/ppermute | solution.py:861
  275.5 8.3 %collective-permute-done.40 = bf16[96,1792]{1,0:T(8,128)(2,1)S(1)} collective-permute-done((bf16[96,1792]{1,0:T(8,128)(2,1)S(1)}, bf16[96,1792]{1,0:T(8,128)(2,1)S(1)}, u32[]{:S(2)}, u32[]{:S(2)}) %collective-permute-start.40) | collective-permute-done | bytes 344096 | tf_op jit(solution)/shard_map/ppermute | solution.py:861
  (222 shorter events, 77.6 us)
Async XLA Ops:
  1.9 10.6 %collective-permute-start.1 = (f32[3,857]{1,0:T(4,128)S(1)}, f32[3,857]{1,0:T(4,128)S(1)}, u32[]{:S(2)}, u32[]{:S(2)}) collective-permute-start(f32[3,857]{1,0:T(4,128)S(1)} %copy-done.28), channel_id=1, source_target_pairs={{0,2},{1,3},{2,0},{3,1},{4,6},{5,7},{6,4},{7,5},{8,10},{9,11},{10,... | collective-permute-start | bytes 30860 | tf_op jit(solution)/shard_map/ppermute | solution.py:861
  4.9 10.4 %collective-permute-start = (bf16[1,96,896]{2,1,0:T(8,128)(2,1)S(1)}, bf16[1,96,896]{2,1,0:T(8,128)(2,1)S(1)}, u32[]{:S(2)}, u32[]{:S(2)}) collective-permute-start(bf16[1,96,896]{2,1,0:T(8,128)(2,1)S(1)} %bitcast.52), channel_id=1, source_target_pairs={{0,16},{4,20},{8,24},{12,28},{16,0},{20,4},{24,8},{28,12},{1,17},{... | collective-permute-start | bytes 516104 | tf_op jit(solution)/shard_map/ppermute | solution.py:861
  26.7 15.9 %collective-permute-start.2 = (bf16[1,96,1536]{2,1,0:T(8,128)(2,1)S(1)}, bf16[1,96,1536]{2,1,0:T(8,128)(2,1)S(1)}, u32[]{:S(2)}, u32[]{:S(2)}) collective-permute-start(bf16[1,96,1536]{2,1,0:T(8,128)(2,1)S(1)} %maximum_bitcast_fusion), channel_id=1, source_target_pairs={{0,16},{4,20},{8,24},{12,28},{16,0},{20,4},{24,8},{28,12},{1,17},{... | collective-permute-start | bytes 884744 | tf_op jit(solution)/shard_map/ppermute | solution.py:861
  34.4 15.6 %collective-permute-start.11 = (bf16[8,48,896]{2,1,0:T(8,128)(2,1)S(1)}, bf16[8,48,896]{2,1,0:T(8,128)(2,1)}, u32[]{:S(2)}, u32[]{:S(2)}) collective-permute-start(bf16[8,48,896]{2,1,0:T(8,128)(2,1)S(1)} %get-tuple-element.147.refs_0_), channel_id=1, source_target_pairs={{0,1},{1,0},{2,3},{3,2},{4,5},{5,4},{6,7},{7,6},{8,9},{9,8},{10,11... | collective-permute-start | bytes 2064392 | tf_op jit(solution)/shard_map/ppermute | solution.py:861
  34.5 22.5 %collective-permute-start.8 = (bf16[8,48,896]{2,1,0:T(8,128)(2,1)S(1)}, bf16[8,48,896]{2,1,0:T(8,128)(2,1)}, u32[]{:S(2)}, u32[]{:S(2)}) collective-permute-start(bf16[8,48,896]{2,1,0:T(8,128)(2,1)S(1)} %get-tuple-element.147.refs_0_), channel_id=1, source_target_pairs={{0,2},{1,3},{2,0},{3,1},{4,6},{5,7},{6,4},{7,5},{8,10},{9,11},{10,... | collective-permute-start | bytes 2064392 | tf_op jit(solution)/shard_map/ppermute | solution.py:861
  35.1 14.9 %collective-permute-start.12 = (bf16[8,48,896]{2,1,0:T(8,128)(2,1)S(1)}, bf16[8,48,896]{2,1,0:T(8,128)(2,1)}, u32[]{:S(2)}, u32[]{:S(2)}) collective-permute-start(bf16[8,48,896]{2,1,0:T(8,128)(2,1)S(1)} %get-tuple-element.148.refs_2_), channel_id=1, source_target_pairs={{0,1},{1,0},{2,3},{3,2},{4,5},{5,4},{6,7},{7,6},{8,9},{9,8},{10,11... | collective-permute-start | bytes 2064392 | tf_op jit(solution)/shard_map/ppermute | solution.py:861
  35.3 21.8 %collective-permute-start.9 = (bf16[8,48,896]{2,1,0:T(8,128)(2,1)S(1)}, bf16[8,48,896]{2,1,0:T(8,128)(2,1)}, u32[]{:S(2)}, u32[]{:S(2)}) collective-permute-start(bf16[8,48,896]{2,1,0:T(8,128)(2,1)S(1)} %get-tuple-element.148.refs_2_), channel_id=1, source_target_pairs={{0,4},{4,0},{8,12},{12,8},{16,20},{20,16},{24,28},{28,24},{1,5},{5... | collective-permute-start | bytes 2064392 | tf_op jit(solution)/shard_map/ppermute | solution.py:861
  42.6 14.4 %collective-permute-start.10 = (bf16[2,96,1536]{2,1,0:T(8,128)(2,1)S(1)}, bf16[2,96,1536]{2,1,0:T(8,128)(2,1)S(1)}, u32[]{:S(2)}, u32[]{:S(2)}) collective-permute-start(bf16[2,96,1536]{2,1,0:T(8,128)(2,1)S(1)} %pad_maximum_fusion.6), channel_id=1, source_target_pairs={{0,8},{4,12},{8,0},{12,4},{16,24},{20,28},{24,16},{28,20},{1,9},{5... | collective-permute-start | bytes 1769480 | tf_op jit(solution)/shard_map/ppermute | solution.py:861
  57.7 18.6 %collective-permute-start.15 = (bf16[4,48,1536]{2,1,0:T(8,128)(2,1)S(1)}, bf16[4,48,1536]{2,1,0:T(8,128)(2,1)S(1)}, u32[]{:S(2)}, u32[]{:S(2)}) collective-permute-start(bf16[4,48,1536]{2,1,0:T(8,128)(2,1)S(1)} %get-tuple-element.160), channel_id=1, source_target_pairs={{0,4},{4,0},{8,12},{12,8},{16,20},{20,16},{24,28},{28,24},{1,5},{5... | collective-permute-start | bytes 1769480 | tf_op jit(solution)/shard_map/ppermute | solution.py:861
  58.3 18.0 %collective-permute-start.16 = (bf16[4,48,1536]{2,1,0:T(8,128)(2,1)S(1)}, bf16[4,48,1536]{2,1,0:T(8,128)(2,1)S(1)}, u32[]{:S(2)}, u32[]{:S(2)}) collective-permute-start(bf16[4,48,1536]{2,1,0:T(8,128)(2,1)S(1)} %get-tuple-element.169), channel_id=1, source_target_pairs={{0,2},{1,3},{2,0},{3,1},{4,6},{5,7},{6,4},{7,5},{8,10},{9,11},{10,... | collective-permute-start | bytes 1769480 | tf_op jit(solution)/shard_map/ppermute | solution.py:861
  76.7 28.5 %collective-permute-start.17 = (bf16[8,48,1536]{2,1,0:T(8,128)(2,1)S(1)}, bf16[8,48,1536]{2,1,0:T(8,128)(2,1)}, u32[]{:S(2)}, u32[]{:S(2)}) collective-permute-start(bf16[8,48,1536]{2,1,0:T(8,128)(2,1)S(1)} %pad_maximum_fusion.1.refs_0_), channel_id=1, source_target_pairs={{0,2},{1,3},{2,0},{3,1},{4,6},{5,7},{6,4},{7,5},{8,10},{9,11},{10,... | collective-permute-start | bytes 3538952 | tf_op jit(solution)/shard_map/ppermute | solution.py:861
  78.2 27.0 %collective-permute-start.20 = (bf16[8,48,1536]{2,1,0:T(8,128)(2,1)S(1)}, bf16[8,48,1536]{2,1,0:T(8,128)(2,1)}, u32[]{:S(2)}, u32[]{:S(2)}) collective-permute-start(bf16[8,48,1536]{2,1,0:T(8,128)(2,1)S(1)} %pad_maximum_fusion.2.refs_2_), channel_id=1, source_target_pairs={{0,1},{1,0},{2,3},{3,2},{4,5},{5,4},{6,7},{7,6},{8,9},{9,8},{10,11... | collective-permute-start | bytes 3538952 | tf_op jit(solution)/shard_map/ppermute | solution.py:861
  78.3 28.4 %collective-permute-start.18 = (bf16[8,48,1536]{2,1,0:T(8,128)(2,1)S(1)}, bf16[8,48,1536]{2,1,0:T(8,128)(2,1)}, u32[]{:S(2)}, u32[]{:S(2)}) collective-permute-start(bf16[8,48,1536]{2,1,0:T(8,128)(2,1)S(1)} %pad_maximum_fusion.2.refs_2_), channel_id=1, source_target_pairs={{0,4},{4,0},{8,12},{12,8},{16,20},{20,16},{24,28},{28,24},{1,5},{5... | collective-permute-start | bytes 3538952 | tf_op jit(solution)/shard_map/ppermute | solution.py:861
  147.9 12.4 %collective-permute-start.23 = (bf16[2,8,96,1536]{3,2,1,0:T(8,128)(2,1)}, bf16[2,8,96,1536]{3,2,1,0:T(8,128)(2,1)}, u32[]{:S(2)}, u32[]{:S(2)}) collective-permute-start(bf16[2,8,96,1536]{3,2,1,0:T(8,128)(2,1)} %get-tuple-element.191), channel_id=1, source_target_pairs={{0,1},{1,0},{2,3},{3,2},{4,5},{5,4},{6,7},{7,6},{8,9},{9,8},{10,11... | collective-permute-start | bytes 14155784 | tf_op jit(solution)/shard_map/ppermute | solution.py:861
  168.5 32.7 %collective-permute-start.25 = (bf16[8,48,1792]{2,1,0:T(8,128)(2,1)}, bf16[8,48,1792]{2,1,0:T(8,128)(2,1)S(1)}, u32[]{:S(2)}, u32[]{:S(2)}) collective-permute-start(bf16[8,48,1792]{2,1,0:T(8,128)(2,1)} %get-tuple-element.206), channel_id=1, source_target_pairs={{0,2},{1,3},{2,0},{3,1},{4,6},{5,7},{6,4},{7,5},{8,10},{9,11},{10,... | collective-permute-start | bytes 4128776 | tf_op jit(solution)/shard_map/ppermute | solution.py:861
  169.1 32.4 %collective-permute-start.26 = (bf16[2,4,48,1792]{3,2,1,0:T(8,128)(2,1)}, bf16[2,4,48,1792]{3,2,1,0:T(8,128)(2,1)S(1)}, u32[]{:S(2)}, u32[]{:S(2)}) collective-permute-start(bf16[2,4,48,1792]{3,2,1,0:T(8,128)(2,1)} %get-tuple-element.207), channel_id=1, source_target_pairs={{0,4},{4,0},{8,12},{12,8},{16,20},{20,16},{24,28},{28,24},{1,5},{5... | collective-permute-start | bytes 4128776 | tf_op jit(solution)/shard_map/ppermute | solution.py:861
  208.8 22.0 %collective-permute-start.30 = (bf16[4,48,1792]{2,1,0:T(8,128)(2,1)}, bf16[4,48,1792]{2,1,0:T(8,128)(2,1)S(1)}, u32[]{:S(2)}, u32[]{:S(2)}) collective-permute-start(bf16[4,48,1792]{2,1,0:T(8,128)(2,1)} %get-tuple-element.226), channel_id=1, source_target_pairs={{0,4},{4,0},{8,12},{12,8},{16,20},{20,16},{24,28},{28,24},{1,5},{5... | collective-permute-start | bytes 2064392 | tf_op jit(solution)/shard_map/ppermute | solution.py:861
  210.2 20.6 %collective-permute-start.31 = (bf16[4,48,1792]{2,1,0:T(8,128)(2,1)}, bf16[4,48,1792]{2,1,0:T(8,128)(2,1)S(1)}, u32[]{:S(2)}, u32[]{:S(2)}) collective-permute-start(bf16[4,48,1792]{2,1,0:T(8,128)(2,1)} %get-tuple-element.227), channel_id=1, source_target_pairs={{0,2},{1,3},{2,0},{3,1},{4,6},{5,7},{6,4},{7,5},{8,10},{9,11},{10,... | collective-permute-start | bytes 2064392 | tf_op jit(solution)/shard_map/ppermute | solution.py:861
  227.4 13.8 %collective-permute-start.28 = (bf16[8,48,640]{2,1,0:T(8,128)(2,1)S(1)}, bf16[8,48,640]{2,1,0:T(8,128)(2,1)S(1)}, u32[]{:S(2)}, u32[]{:S(2)}) collective-permute-start(bf16[8,48,640]{2,1,0:T(8,128)(2,1)S(1)} %copy-done.39), channel_id=1, source_target_pairs={{0,2},{1,3},{2,0},{3,1},{4,6},{5,7},{6,4},{7,5},{8,10},{9,11},{10,... | collective-permute-start | bytes 1474568 | tf_op jit(solution)/shard_map/ppermute | solution.py:861
  228.7 12.8 %collective-permute-start.29 = (bf16[2,4,48,640]{3,2,1,0:T(8,128)(2,1)S(1)}, bf16[2,4,48,640]{3,2,1,0:T(8,128)(2,1)S(1)}, u32[]{:S(2)}, u32[]{:S(2)}) collective-permute-start(bf16[2,4,48,640]{3,2,1,0:T(8,128)(2,1)S(1)} %copy-done.38), channel_id=1, source_target_pairs={{0,4},{4,0},{8,12},{12,8},{16,20},{20,16},{24,28},{28,24},{1,5},{5... | collective-permute-start | bytes 1474568 | tf_op jit(solution)/shard_map/ppermute | solution.py:861
  235.1 21.5 %collective-permute-start.37 = (bf16[2,96,1792]{2,1,0:T(8,128)(2,1)}, bf16[2,96,1792]{2,1,0:T(8,128)(2,1)S(1)}, u32[]{:S(2)}, u32[]{:S(2)}) collective-permute-start(bf16[2,96,1792]{2,1,0:T(8,128)(2,1)} %get-tuple-element.238), channel_id=1, source_target_pairs={{0,8},{4,12},{8,0},{12,4},{16,24},{20,28},{24,16},{28,20},{1,9},{5... | collective-permute-start | bytes 2064392 | tf_op jit(solution)/shard_map/ppermute | solution.py:861
  262.1 13.2 %collective-permute-start.38 = (bf16[2,96,640]{2,1,0:T(8,128)(2,1)S(1)}, bf16[2,96,640]{2,1,0:T(8,128)(2,1)S(1)}, u32[]{:S(2)}, u32[]{:S(2)}) collective-permute-start(bf16[2,96,640]{2,1,0:T(8,128)(2,1)S(1)} %copy-done.40), channel_id=1, source_target_pairs={{0,8},{4,12},{8,0},{12,4},{16,24},{20,28},{24,16},{28,20},{1,9},{5... | collective-permute-start | bytes 737288 | tf_op jit(solution)/shard_map/ppermute | solution.py:861
  263.5 20.4 %collective-permute-start.40 = (bf16[96,1792]{1,0:T(8,128)(2,1)S(1)}, bf16[96,1792]{1,0:T(8,128)(2,1)S(1)}, u32[]{:S(2)}, u32[]{:S(2)}) collective-permute-start(bf16[96,1792]{1,0:T(8,128)(2,1)S(1)} %fusion.3), channel_id=1, source_target_pairs={{0,16},{4,20},{8,24},{12,28},{16,0},{20,4},{24,8},{28,12},{1,17},{... | collective-permute-start | bytes 1032200 | tf_op jit(solution)/shard_map/ppermute | solution.py:861
  275.4 10.0 %collective-permute-start.39 = (bf16[96,640]{1,0:T(8,128)(2,1)S(1)}, bf16[96,640]{1,0:T(8,128)(2,1)S(1)}, u32[]{:S(2)}, u32[]{:S(2)}) collective-permute-start(bf16[96,640]{1,0:T(8,128)(2,1)S(1)} %fusion.5), channel_id=1, source_target_pairs={{0,16},{4,20},{8,24},{12,28},{16,0},{20,4},{24,8},{28,12},{1,17},{... | collective-permute-start | bytes 368648 | tf_op jit(solution)/shard_map/ppermute | solution.py:861
  (65 other events, 472.1 us)

commit v5 on v4

--- a/solution.py
+++ b/solution.py
@@ -941,19 +941,19 @@
     wide = sum(keep.shape[3] for keep in keeps)
     places = (
         lambda j: (0, j, 0, 0),
-        lambda j: (0, 4 + j, 0, 0),
+        lambda j: (0, 2 + j, 0, 0),
         lambda j: (0, j, 1, 0),
         lambda j: (1, j, 1, 0),
     )
     views = [
-        (upper_got, (1, half, wide), lambda j: (j, 0, 0)),
-        (upper_got, (1, half, wide), lambda j: (4 + j, 0, 0)),
-        (lower_got, (1, 1, half, wide), lambda j: (0, j, 0, 0)),
-        (lower_got, (1, 1, half, wide), lambda j: (1, j, 0, 0)),
+        (upper_got, (2, half, wide), lambda j: (j, 0, 0)),
+        (upper_got, (2, half, wide), lambda j: (2 + j, 0, 0)),
+        (lower_got, (1, 2, half, wide), lambda j: (0, j, 0, 0)),
+        (lower_got, (1, 2, half, wide), lambda j: (1, j, 0, 0)),
     ]
     for keep, got in zip(keeps, gots):
         for array in (keep, got):
-            views.extend((array, (1, 1, half, keep.shape[3]), place) for place in places)
+            views.extend((array, (1, 2, half, keep.shape[3]), place) for place in places)
 
     def body(*refs):
         far, ins, outs = refs[:4], refs[4:-4], refs[-4:]
@@ -962,15 +962,15 @@
             at = slice(first, first + ins[index].shape[3])
             first = at.stop
             for view in range(4):
-                came = far[view][0, :, at] if view < 2 else far[view][0, 0, :, at]
-                terms = (ins[index + view][0, 0], ins[index + 4 + view][0, 0], came)
-                outs[view][0, :, at] = total_of(terms).astype(outs[view].dtype)
+                came = far[view][:, :, at] if view < 2 else far[view][0, :, :, at]
+                terms = (ins[index + view][0], ins[index + 4 + view][0], came)
+                outs[view][:, :, at] = total_of(terms).astype(outs[view].dtype)
 
     outs = [
-        ((4, half, wide), dtype, (1, half, wide), lambda j: (j, 0, 0))
+        ((4, half, wide), dtype, (2, half, wide), lambda j: (j, 0, 0))
         for dtype in (FULL, LOW, FULL, LOW)
     ]
-    return sum_call(body, 4, views, outs, 1.2e7)
+    return sum_call(body, 2, views, outs, 1.2e7)
 
 
 def sum_line(upper, upper_got, lower, lower_got):
@@ -1189,6 +1189,7 @@
         line = line + line_got.astype(FULL)
         small, line_away = sync(small + small_got, line[1].astype(LOW))
         got, line_got = z_near(away), z_far(line_away)
+        got, line_got, small = sync(got, line_got, small)
         came = (z_near(small), z_far(small), swap(small, "dp", 6))
         here = here + got.astype(FULL)
         got = z_far(here[1].astype(LOW))

time: 289 us -> 288 us (level)
    unnamed x90 -> x92, local copies, waits for them, and re-layouts: 7.48 us -> 6.55 us
  transfers between devices with their start and end apart: 44 -> 44, of which waited for: 26 -> 25; matrix products, arithmetic and copies ran while one was open for 2% -> 2% of each run, Pallas kernels for 37% -> 36%
where the time goes in v5:
time: 288 us; the launch traced here: 287 us
  Pallas kernels  144 us (50%)
  waiting for transfers between devices  81.8 us (28%)
  starting transfers between devices  44.4 us (15%)
  local copies, waits for them, and re-layouts  7.78 us (3%)
  other arithmetic  7.12 us (2%)
    ppermute x44, waiting for transfers between devices, swap(): lax.ppermute(values, axis, [(index, index ^ bit) for index in range(count)])  81.8 us
    ppermute x44, starting transfers between devices, swap(): lax.ppermute(values, axis, [(index, index ^ bit) for index in range(count)])  44.4 us
    pallas_call x1, Pallas kernels, feed(): pl.pallas_call(functools.partial(feed_body, blocks, layout), grid=(LANES,...  35.5 us
    pallas_call x6, Pallas kernels, sum_call(): pl.pallas_call(body, grid=(grid,), in_specs=[pl.BlockSpec(block, index) f...  22 us
    pallas_call x1, Pallas kernels, attend(): pl.pallas_call(functools.partial(attend_body, table, images), grid=(LANES...  15.7 us
    pallas_call x1, Pallas kernels, back(): pl.pallas_call(functools.partial(back_body, table, columns, images), grid...  15 us
    pallas_call x1, Pallas kernels, second_back(): pl.pallas_call(second_body, grid=(images,), in_specs=[pl.BlockSpec(memory...  12.2 us
    pallas_call x1, Pallas kernels, input_back(): pl.pallas_call(functools.partial(input_body, table), grid=(images // TWO,...  12 us
  transfers between devices with their start and end apart: 44, of which 25 were waited for; matrix products, arithmetic and copies ran while one was open for 2% of the time, Pallas kernels for 36%

profile of v5, /device:TPU:0, one launch (start us, length us, event | category | flops | bytes accessed | tf_op | source)
XLA Modules:
  0.0 286.9 jit_solution(1151274571485233031)
XLA Ops:
  7.5 5.0 %shard_map.272 = (bf16[832,768]{1,0:T(8,128)(2,1)}, bf16[832,768]{1,0:T(8,128)(2,1)}) custom-call(f32[784,768]{1,0:T(8,128)} %x_ref.5, f32[784,768]{1,0:T(8,128)} %cot_ref.3, f32[12,768]{1,0:T(8,128)} %vec_ref.7), custom_call_target="tpu_custom_call" | custom-call | flops 3000000000 | bytes 4000000 | tf_op jit(solution)/shard_map/pallas_call | solution.py:147
  17.6 6.8 %collective-permute-done.3 = bf16[2,96,896]{2,1,0:T(8,128)(2,1)S(1)} collective-permute-done((bf16[2,96,896]{2,1,0:T(8,128)(2,1)S(1)}, bf16[2,96,896]{2,1,0:T(8,128)(2,1)S(1)}, u32[]{:S(2)}, u32[]{:S(2)}) %collective-permute-start.3) | collective-permute-done | bytes 344096 | tf_op jit(solution)/shard_map/ppermute | solution.py:861
  26.7 3.4 %collective-permute-start.2 = (bf16[1,96,1536]{2,1,0:T(8,128)(2,1)S(1)}, bf16[1,96,1536]{2,1,0:T(8,128)(2,1)S(1)}, u32[]{:S(2)}, u32[]{:S(2)}) collective-permute-start(bf16[1,96,1536]{2,1,0:T(8,128)(2,1)S(1)} %maximum_bitcast_fusion), channel_id=1, source_target_pairs={{0,16},{4,20},{8,24},{12,28},{16,0},{20,4},{24,8},{28,12},{1,17},{... | collective-permute-start | bytes 884744 | tf_op jit(solution)/shard_map/ppermute | solution.py:861
  35.8 6.8 %collective-permute-done.2 = bf16[1,96,1536]{2,1,0:T(8,128)(2,1)S(1)} collective-permute-done((bf16[1,96,1536]{2,1,0:T(8,128)(2,1)S(1)}, bf16[1,96,1536]{2,1,0:T(8,128)(2,1)S(1)}, u32[]{:S(2)}, u32[]{:S(2)}) %collective-permute-start.2) | collective-permute-done | bytes 294944 | tf_op jit(solution)/shard_map/ppermute | solution.py:861
  44.6 5.3 %shard_map.273 = (f32[12,208,208]{2,1,0:T(8,128)}, f32[4,1,640]{2,1,0:T(1,128)}) custom-call(f32[3,857]{1,0:T(4,128)} %t0.1, f32[3,857]{1,0:T(4,128)} %copy-done.43, f32[3,857]{1,0:T(4,128)} %copy-done.42, f32[3,857]{1,0:T(4,128)} %copy-done.44, bf16[768,384]{1,0:T(8,128)(2,1)} %constant.32.clone.thin_ref), custom_call_target="tpu_custom_call" | custom-call | flops 3000000000 | bytes 4000000 | tf_op jit(solution)/shard_map/pallas_call | solution.py:211
  50.0 7.0 %collective-permute-done.10 = bf16[2,96,1536]{2,1,0:T(8,128)(2,1)S(1)} collective-permute-done((bf16[2,96,1536]{2,1,0:T(8,128)(2,1)S(1)}, bf16[2,96,1536]{2,1,0:T(8,128)(2,1)S(1)}, u32[]{:S(2)}, u32[]{:S(2)}) %collective-permute-start.10) | collective-permute-done | bytes 589856 | tf_op jit(solution)/shard_map/ppermute | solution.py:861
  60.7 15.7 %shard_map.274 = (bf16[4,832,640]{2,1,0:T(8,128)(2,1)}, bf16[4,12,208,208]{3,2,1,0:T(8,128)(2,1)}, bf16[832,1024]{1,0:T(8,128)(2,1)}) custom-call(s32[3]{0:T(128)} %pad_add_fusion.me_ref, s32[16,2]{1,0:T(8,128)} %copy.31.size_ref, s32[2,208,128]{2,1,0:T(8,128)} %constant.33.clone.grid_ref, bf16[832,768]{1,0:T(8,128)(2,1)} %get-tuple-element.164.n_ref, ...), custom_call_target="tpu_custom_call" | custom-call | flops 15000000512 | bytes 20000000 | tf_op jit(solution)/shard_map/pallas_call | solution.py:322
  79.0 7.4 %shard_map.275 = (bf16[832,768]{1,0:T(8,128)(2,1)}, f32[832,768]{1,0:T(8,128)}, bf16[832,768]{1,0:T(8,128)(2,1)}) custom-call(s32[3]{0:T(128)} %pad_add_fusion.me_ref, bf16[832,1024]{1,0:T(8,128)(2,1)} %get-tuple-element.176.ctx_ref, f32[784,768]{1,0:T(8,128)} %x_ref.5, f32[12,768]{1,0:T(8,128)} %vec_ref.7, bf16[8,48,896]{2,1,0:T(8,128)(2,1)} %copy-done.17, ...), custom_call_target="tpu_custom_call" | custom-call | flops 8000000000 | bytes 15000000 | tf_op jit(solution)/shard_map/pallas_call | solution.py:383
  86.5 18.7 %collective-permute-done.17.refs_1_ = bf16[8,48,1536]{2,1,0:T(8,128)(2,1)} collective-permute-done((bf16[8,48,1536]{2,1,0:T(8,128)(2,1)S(1)}, bf16[8,48,1536]{2,1,0:T(8,128)(2,1)}, u32[]{:S(2)}, u32[]{:S(2)}) %collective-permute-start.17) | collective-permute-done | bytes 1179680 | tf_op jit(solution)/shard_map/ppermute | solution.py:861
  112.4 35.5 %shard_map.276 = (f32[832,768]{1,0:T(8,128)}, f32[832,768]{1,0:T(8,128)}, bf16[2,8,96,1536]{3,2,1,0:T(8,128)(2,1)}, bf16[2,8,96,1536]{3,2,1,0:T(8,128)(2,1)}, f32[4,1,768]{2,1,0:T(1,128)}) custom-call(s32[3]{0:T(128)} %pad_add_fusion.me_ref, bf16[832,768]{1,0:T(8,128)(2,1)} %get-tuple-element.180.n_ref, bf16[832,768]{1,0:T(8,128)(2,1)} %get-tuple-element.181.gd_ref, ...), custom_call_target="tpu_custom_call" | custom-call | flops 35000000512 | bytes 40000000 | tf_op jit(solution)/shard_map/pallas_call | solution.py:508
  148.1 12.2 %shard_map.277 = (f32[784,768]{1,0:T(8,128)}, f32[832,768]{1,0:T(8,128)}, bf16[832,768]{1,0:T(8,128)(2,1)}, bf16[2,8,96,256]{3,2,1,0:T(8,128)(2,1)}, bf16[2,8,96,256]{3,2,1,0:T(8,128)(2,1)}, /*index=5*/f32[6,768]{1,0:T(8,128)}) custom-call(s32[3]{0:T(128)} %pad_add_fusion.me_ref, f32[832,768]{1,0:T(8,128)} %get-tuple-element.188.down_ref, ...), custom_call_target="tpu_custom_call" | custom-call | flops 10000000000 | bytes 20000000 | tf_op jit(solution)/shard_map/pallas_call | solution.py:600
  163.9 4.7 %shard_map.278 = (bf16[8,48,1792]{2,1,0:T(8,128)(2,1)}, bf16[2,4,48,1792]{3,2,1,0:T(8,128)(2,1)}) custom-call(bf16[2,8,96,1536]{3,2,1,0:T(8,128)(2,1)} %get-tuple-element.193.refs_0_.refs_1_.refs_4_.refs_5_.refs_6_.refs_7_, bf16[2,8,96,1536]{3,2,1,0:T(8,128)(2,1)} %get-tuple-element.193.refs_0_.refs_1_.refs_4_.refs_5_.refs_6_.refs_7_, ...), custom_call_target="tpu_custom_call" | custom-call | flops 1000000 | bytes 8000000 | tf_op jit(solution)/shard_map/pallas_call | solution.py:901
  170.7 15.0 %shard_map.279 = (bf16[4,832,640]{2,1,0:T(8,128)(2,1)}, f32[12,208,208]{2,1,0:T(8,128)}, f32[4,8,384]{2,1,0:T(8,128)}) custom-call(s32[3]{0:T(128)} %pad_add_fusion.me_ref, bf16[832,768]{1,0:T(8,128)(2,1)} %get-tuple-element.203.ga_ref, bf16[4,832,640]{2,1,0:T(8,128)(2,1)} %get-tuple-element.204.qkv_ref, ...), custom_call_target="tpu_custom_call" | custom-call | flops 30000001024 | bytes 40000000 | tf_op jit(solution)/shard_map/pallas_call | solution.py:713
  185.6 8.8 %shard_map.280 = (bf16[2,8,96,640]{3,2,1,0:T(8,128)(2,1)}, bf16[2,8,96,640]{3,2,1,0:T(8,128)(2,1)}) custom-call(s32[3]{0:T(128)} %pad_add_fusion.me_ref, bf16[832,768]{1,0:T(8,128)(2,1)} %get-tuple-element.164.n_ref, bf16[4,832,640]{2,1,0:T(8,128)(2,1)} %get-tuple-element.223.dqkv_ref), custom_call_target="tpu_custom_call" | custom-call | flops 8000000000 | bytes 10000000 | tf_op jit(solution)/shard_map/pallas_call | solution.py:795
  194.4 5.4 %shard_map.281 = f32[4,3,857]{2,1,0:T(4,128)} custom-call(f32[12,208,208]{2,1,0:T(8,128)} %get-tuple-element.212.pair_ref, f32[4,8,384]{2,1,0:T(8,128)} %get-tuple-element.213.cols_ref, bf16[768,384]{1,0:T(8,128)(2,1)} %constant.32.clone.thin_ref), custom_call_target="tpu_custom_call" | custom-call | flops 3000000000 | bytes 4000000 | tf_op jit(solution)/shard_map/pallas_call | solution.py:774
  202.8 5.2 %shard_map.282 = (f32[4,48,1792]{2,1,0:T(8,128)}, bf16[4,48,1792]{2,1,0:T(8,128)(2,1)}, f32[4,48,1792]{2,1,0:T(8,128)}, bf16[4,48,1792]{2,1,0:T(8,128)(2,1)}) custom-call(bf16[8,48,1792]{2,1,0:T(8,128)(2,1)} %copy-done.2, bf16[8,48,1792]{2,1,0:T(8,128)(2,1)} %copy-done.2, bf16[2,4,48,1792]{3,2,1,0:T(8,128)(2,1)} %copy-done.3, ...), custom_call_target="tpu_custom_call" | custom-call | flops 1000000 | bytes 12000000 | tf_op jit(solution)/shard_map/pallas_call | solution.py:901
  210.3 3.6 %shard_map.283 = (bf16[8,48,640]{2,1,0:T(8,128)(2,1)}, bf16[2,4,48,640]{3,2,1,0:T(8,128)(2,1)}) custom-call(bf16[2,8,96,640]{3,2,1,0:T(8,128)(2,1)} %get-tuple-element.214.refs_0_.refs_1_.refs_4_.refs_5_.refs_6_.refs_7_, bf16[2,8,96,640]{3,2,1,0:T(8,128)(2,1)} %get-tuple-element.214.refs_0_.refs_1_.refs_4_.refs_5_.refs_6_.refs_7_, ...), custom_call_target="tpu_custom_call" | custom-call | flops 1000000 | bytes 8000000 | tf_op jit(solution)/shard_map/pallas_call | solution.py:901
  213.9 12.0 %shard_map.284 = (f32[784,768]{1,0:T(8,128)}, f32[2,768]{1,0:T(2,128)}) custom-call(s32[3]{0:T(128)} %pad_add_fusion.me_ref, bf16[4,832,640]{2,1,0:T(8,128)(2,1)} %get-tuple-element.223.dqkv_ref, f32[832,768]{1,0:T(8,128)} %get-tuple-element.224.gm_ref, f32[784,768]{1,0:T(8,128)} %x_ref.5, f32[12,768]{1,0:T(8,128)} %vec_ref.7, ...), custom_call_target="tpu_custom_call" | custom-call | flops 15000000512 | bytes 15000000 | tf_op jit(solution)/shard_map/pallas_call | solution.py:834
  231.2 3.3 %shard_map.285 = (f32[2,96,1792]{2,1,0:T(8,128)}, bf16[2,96,1792]{2,1,0:T(8,128)(2,1)}) custom-call(f32[4,48,1792]{2,1,0:T(8,128)} %get-tuple-element.228.refs_0_.refs_1_, f32[4,48,1792]{2,1,0:T(8,128)} %get-tuple-element.228.refs_0_.refs_1_, bf16[4,48,1792]{2,1,0:T(8,128)(2,1)} %copy-done.5, bf16[4,48,1792]{2,1,0:T(8,128)(2,1)} %copy-done.5, ...), custom_call_target="tpu_custom_call" | custom-call | flops 1000000 | bytes 6000000 | tf_op jit(solution)/shard_map/pallas_call | solution.py:901
  247.7 4.4 %collective-permute-done.34.refs_2_.refs_3_ = bf16[4,48,640]{2,1,0:T(8,128)(2,1)S(1)} collective-permute-done((bf16[4,48,640]{2,1,0:T(8,128)(2,1)}, bf16[4,48,640]{2,1,0:T(8,128)(2,1)S(1)}, u32[]{:S(2)}, u32[]{:S(2)}) %collective-permute-start.34) | collective-permute-done | bytes 245792 | tf_op jit(solution)/shard_map/ppermute | solution.py:861
  255.4 3.4 %collective-permute-start.39 = (bf16[96,1792]{1,0:T(8,128)(2,1)S(1)}, bf16[96,1792]{1,0:T(8,128)(2,1)S(1)}, u32[]{:S(2)}, u32[]{:S(2)}) collective-permute-start(bf16[96,1792]{1,0:T(8,128)(2,1)S(1)} %fusion.3), channel_id=1, source_target_pairs={{0,16},{4,20},{8,24},{12,28},{16,0},{20,4},{24,8},{28,12},{1,17},{... | collective-permute-start | bytes 1032200 | tf_op jit(solution)/shard_map/ppermute | solution.py:861
  260.4 9.1 %collective-permute-done.38 = bf16[2,96,640]{2,1,0:T(8,128)(2,1)S(1)} collective-permute-done((bf16[2,96,640]{2,1,0:T(8,128)(2,1)S(1)}, bf16[2,96,640]{2,1,0:T(8,128)(2,1)S(1)}, u32[]{:S(2)}, u32[]{:S(2)}) %collective-permute-start.38) | collective-permute-done | bytes 245792 | tf_op jit(solution)/shard_map/ppermute | solution.py:861
  272.5 3.4 %collective-permute-start.43 = (f32[15,857]{1,0:T(8,128)S(1)}, f32[15,857]{1,0:T(8,128)S(1)}, u32[]{:S(2)}, u32[]{:S(2)}) collective-permute-start(f32[15,857]{1,0:T(8,128)S(1)} %add.82), channel_id=1, source_target_pairs={{0,24},{4,28},{8,16},{12,20},{16,8},{20,12},{24,0},{28,4},{1,25},{... | collective-permute-start | bytes 154268 | tf_op jit(solution)/shard_map/ppermute | solution.py:861
  280.4 3.8 %collective-permute-done.42 = f32[15,857]{1,0:T(8,128)S(1)} collective-permute-done((f32[15,857]{1,0:T(8,128)S(1)}, f32[15,857]{1,0:T(8,128)S(1)}, u32[]{:S(2)}, u32[]{:S(2)}) %collective-permute-start.42) | collective-permute-done | bytes 51452 | tf_op jit(solution)/shard_map/ppermute | solution.py:861
  (225 shorter events, 79.4 us)
Async XLA Ops:
  1.9 10.6 %collective-permute-start.1 = (f32[3,857]{1,0:T(4,128)S(1)}, f32[3,857]{1,0:T(4,128)S(1)}, u32[]{:S(2)}, u32[]{:S(2)}) collective-permute-start(f32[3,857]{1,0:T(4,128)S(1)} %copy-done.29), channel_id=1, source_target_pairs={{0,2},{1,3},{2,0},{3,1},{4,6},{5,7},{6,4},{7,5},{8,10},{9,11},{10,... | collective-permute-start | bytes 30860 | tf_op jit(solution)/shard_map/ppermute | solution.py:861
  4.9 10.4 %collective-permute-start = (bf16[1,96,896]{2,1,0:T(8,128)(2,1)S(1)}, bf16[1,96,896]{2,1,0:T(8,128)(2,1)S(1)}, u32[]{:S(2)}, u32[]{:S(2)}) collective-permute-start(bf16[1,96,896]{2,1,0:T(8,128)(2,1)S(1)} %bitcast.52), channel_id=1, source_target_pairs={{0,16},{4,20},{8,24},{12,28},{16,0},{20,4},{24,8},{28,12},{1,17},{... | collective-permute-start | bytes 516104 | tf_op jit(solution)/shard_map/ppermute | solution.py:861
  26.7 15.9 %collective-permute-start.2 = (bf16[1,96,1536]{2,1,0:T(8,128)(2,1)S(1)}, bf16[1,96,1536]{2,1,0:T(8,128)(2,1)S(1)}, u32[]{:S(2)}, u32[]{:S(2)}) collective-permute-start(bf16[1,96,1536]{2,1,0:T(8,128)(2,1)S(1)} %maximum_bitcast_fusion), channel_id=1, source_target_pairs={{0,16},{4,20},{8,24},{12,28},{16,0},{20,4},{24,8},{28,12},{1,17},{... | collective-permute-start | bytes 884744 | tf_op jit(solution)/shard_map/ppermute | solution.py:861
  34.4 15.6 %collective-permute-start.11 = (bf16[8,48,896]{2,1,0:T(8,128)(2,1)S(1)}, bf16[8,48,896]{2,1,0:T(8,128)(2,1)}, u32[]{:S(2)}, u32[]{:S(2)}) collective-permute-start(bf16[8,48,896]{2,1,0:T(8,128)(2,1)S(1)} %get-tuple-element.150.refs_0_), channel_id=1, source_target_pairs={{0,1},{1,0},{2,3},{3,2},{4,5},{5,4},{6,7},{7,6},{8,9},{9,8},{10,11... | collective-permute-start | bytes 2064392 | tf_op jit(solution)/shard_map/ppermute | solution.py:861
  34.5 22.5 %collective-permute-start.8 = (bf16[8,48,896]{2,1,0:T(8,128)(2,1)S(1)}, bf16[8,48,896]{2,1,0:T(8,128)(2,1)}, u32[]{:S(2)}, u32[]{:S(2)}) collective-permute-start(bf16[8,48,896]{2,1,0:T(8,128)(2,1)S(1)} %get-tuple-element.150.refs_0_), channel_id=1, source_target_pairs={{0,2},{1,3},{2,0},{3,1},{4,6},{5,7},{6,4},{7,5},{8,10},{9,11},{10,... | collective-permute-start | bytes 2064392 | tf_op jit(solution)/shard_map/ppermute | solution.py:861
  35.1 14.9 %collective-permute-start.12 = (bf16[8,48,896]{2,1,0:T(8,128)(2,1)S(1)}, bf16[8,48,896]{2,1,0:T(8,128)(2,1)}, u32[]{:S(2)}, u32[]{:S(2)}) collective-permute-start(bf16[8,48,896]{2,1,0:T(8,128)(2,1)S(1)} %get-tuple-element.151.refs_2_), channel_id=1, source_target_pairs={{0,1},{1,0},{2,3},{3,2},{4,5},{5,4},{6,7},{7,6},{8,9},{9,8},{10,11... | collective-permute-start | bytes 2064392 | tf_op jit(solution)/shard_map/ppermute | solution.py:861
  35.3 21.8 %collective-permute-start.9 = (bf16[8,48,896]{2,1,0:T(8,128)(2,1)S(1)}, bf16[8,48,896]{2,1,0:T(8,128)(2,1)}, u32[]{:S(2)}, u32[]{:S(2)}) collective-permute-start(bf16[8,48,896]{2,1,0:T(8,128)(2,1)S(1)} %get-tuple-element.151.refs_2_), channel_id=1, source_target_pairs={{0,4},{4,0},{8,12},{12,8},{16,20},{20,16},{24,28},{28,24},{1,5},{5... | collective-permute-start | bytes 2064392 | tf_op jit(solution)/shard_map/ppermute | solution.py:861
  42.6 14.4 %collective-permute-start.10 = (bf16[2,96,1536]{2,1,0:T(8,128)(2,1)S(1)}, bf16[2,96,1536]{2,1,0:T(8,128)(2,1)S(1)}, u32[]{:S(2)}, u32[]{:S(2)}) collective-permute-start(bf16[2,96,1536]{2,1,0:T(8,128)(2,1)S(1)} %pad_maximum_fusion.6), channel_id=1, source_target_pairs={{0,8},{4,12},{8,0},{12,4},{16,24},{20,28},{24,16},{28,20},{1,9},{5... | collective-permute-start | bytes 1769480 | tf_op jit(solution)/shard_map/ppermute | solution.py:861
  57.7 18.6 %collective-permute-start.15 = (bf16[4,48,1536]{2,1,0:T(8,128)(2,1)S(1)}, bf16[4,48,1536]{2,1,0:T(8,128)(2,1)S(1)}, u32[]{:S(2)}, u32[]{:S(2)}) collective-permute-start(bf16[4,48,1536]{2,1,0:T(8,128)(2,1)S(1)} %get-tuple-element.163), channel_id=1, source_target_pairs={{0,4},{4,0},{8,12},{12,8},{16,20},{20,16},{24,28},{28,24},{1,5},{5... | collective-permute-start | bytes 1769480 | tf_op jit(solution)/shard_map/ppermute | solution.py:861
  58.3 18.1 %collective-permute-start.16 = (bf16[4,48,1536]{2,1,0:T(8,128)(2,1)S(1)}, bf16[4,48,1536]{2,1,0:T(8,128)(2,1)S(1)}, u32[]{:S(2)}, u32[]{:S(2)}) collective-permute-start(bf16[4,48,1536]{2,1,0:T(8,128)(2,1)S(1)} %get-tuple-element.172), channel_id=1, source_target_pairs={{0,2},{1,3},{2,0},{3,1},{4,6},{5,7},{6,4},{7,5},{8,10},{9,11},{10,... | collective-permute-start | bytes 1769480 | tf_op jit(solution)/shard_map/ppermute | solution.py:861
  76.6 9.8 %collective-permute-start.19 = (bf16[8,48,1536]{2,1,0:T(8,128)(2,1)S(1)}, bf16[8,48,1536]{2,1,0:T(8,128)(2,1)S(1)}, u32[]{:S(2)}, u32[]{:S(2)}) collective-permute-start(bf16[8,48,1536]{2,1,0:T(8,128)(2,1)S(1)} %pad_maximum_fusion.1.refs_0_), channel_id=1, source_target_pairs={{0,1},{1,0},{2,3},{3,2},{4,5},{5,4},{6,7},{7,6},{8,9},{9,8},{10,11... | collective-permute-start | bytes 3538952 | tf_op jit(solution)/shard_map/ppermute | solution.py:861
  76.7 28.5 %collective-permute-start.17 = (bf16[8,48,1536]{2,1,0:T(8,128)(2,1)S(1)}, bf16[8,48,1536]{2,1,0:T(8,128)(2,1)}, u32[]{:S(2)}, u32[]{:S(2)}) collective-permute-start(bf16[8,48,1536]{2,1,0:T(8,128)(2,1)S(1)} %pad_maximum_fusion.1.refs_0_), channel_id=1, source_target_pairs={{0,2},{1,3},{2,0},{3,1},{4,6},{5,7},{6,4},{7,5},{8,10},{9,11},{10,... | collective-permute-start | bytes 3538952 | tf_op jit(solution)/shard_map/ppermute | solution.py:861
  78.2 27.0 %collective-permute-start.20 = (bf16[8,48,1536]{2,1,0:T(8,128)(2,1)S(1)}, bf16[8,48,1536]{2,1,0:T(8,128)(2,1)}, u32[]{:S(2)}, u32[]{:S(2)}) collective-permute-start(bf16[8,48,1536]{2,1,0:T(8,128)(2,1)S(1)} %pad_maximum_fusion.2.refs_2_), channel_id=1, source_target_pairs={{0,1},{1,0},{2,3},{3,2},{4,5},{5,4},{6,7},{7,6},{8,9},{9,8},{10,11... | collective-permute-start | bytes 3538952 | tf_op jit(solution)/shard_map/ppermute | solution.py:861
  78.3 28.4 %collective-permute-start.18 = (bf16[8,48,1536]{2,1,0:T(8,128)(2,1)S(1)}, bf16[8,48,1536]{2,1,0:T(8,128)(2,1)}, u32[]{:S(2)}, u32[]{:S(2)}) collective-permute-start(bf16[8,48,1536]{2,1,0:T(8,128)(2,1)S(1)} %pad_maximum_fusion.2.refs_2_), channel_id=1, source_target_pairs={{0,4},{4,0},{8,12},{12,8},{16,20},{20,16},{24,28},{28,24},{1,5},{5... | collective-permute-start | bytes 3538952 | tf_op jit(solution)/shard_map/ppermute | solution.py:861
  147.9 12.4 %collective-permute-start.23 = (bf16[2,8,96,1536]{3,2,1,0:T(8,128)(2,1)}, bf16[2,8,96,1536]{3,2,1,0:T(8,128)(2,1)}, u32[]{:S(2)}, u32[]{:S(2)}) collective-permute-start(bf16[2,8,96,1536]{3,2,1,0:T(8,128)(2,1)} %get-tuple-element.194), channel_id=1, source_target_pairs={{0,1},{1,0},{2,3},{3,2},{4,5},{5,4},{6,7},{7,6},{8,9},{9,8},{10,11... | collective-permute-start | bytes 14155784 | tf_op jit(solution)/shard_map/ppermute | solution.py:861
  168.5 32.7 %collective-permute-start.25 = (bf16[8,48,1792]{2,1,0:T(8,128)(2,1)}, bf16[8,48,1792]{2,1,0:T(8,128)(2,1)S(1)}, u32[]{:S(2)}, u32[]{:S(2)}) collective-permute-start(bf16[8,48,1792]{2,1,0:T(8,128)(2,1)} %get-tuple-element.209), channel_id=1, source_target_pairs={{0,2},{1,3},{2,0},{3,1},{4,6},{5,7},{6,4},{7,5},{8,10},{9,11},{10,... | collective-permute-start | bytes 4128776 | tf_op jit(solution)/shard_map/ppermute | solution.py:861
  169.1 32.4 %collective-permute-start.26 = (bf16[2,4,48,1792]{3,2,1,0:T(8,128)(2,1)}, bf16[2,4,48,1792]{3,2,1,0:T(8,128)(2,1)S(1)}, u32[]{:S(2)}, u32[]{:S(2)}) collective-permute-start(bf16[2,4,48,1792]{3,2,1,0:T(8,128)(2,1)} %get-tuple-element.210), channel_id=1, source_target_pairs={{0,4},{4,0},{8,12},{12,8},{16,20},{20,16},{24,28},{28,24},{1,5},{5... | collective-permute-start | bytes 4128776 | tf_op jit(solution)/shard_map/ppermute | solution.py:861
  208.1 22.0 %collective-permute-start.30 = (bf16[4,48,1792]{2,1,0:T(8,128)(2,1)}, bf16[4,48,1792]{2,1,0:T(8,128)(2,1)S(1)}, u32[]{:S(2)}, u32[]{:S(2)}) collective-permute-start(bf16[4,48,1792]{2,1,0:T(8,128)(2,1)} %get-tuple-element.229), channel_id=1, source_target_pairs={{0,4},{4,0},{8,12},{12,8},{16,20},{20,16},{24,28},{28,24},{1,5},{5... | collective-permute-start | bytes 2064392 | tf_op jit(solution)/shard_map/ppermute | solution.py:861
  209.5 20.6 %collective-permute-start.31 = (bf16[4,48,1792]{2,1,0:T(8,128)(2,1)}, bf16[4,48,1792]{2,1,0:T(8,128)(2,1)S(1)}, u32[]{:S(2)}, u32[]{:S(2)}) collective-permute-start(bf16[4,48,1792]{2,1,0:T(8,128)(2,1)} %get-tuple-element.230), channel_id=1, source_target_pairs={{0,2},{1,3},{2,0},{3,1},{4,6},{5,7},{6,4},{7,5},{8,10},{9,11},{10,... | collective-permute-start | bytes 2064392 | tf_op jit(solution)/shard_map/ppermute | solution.py:861
  226.7 13.8 %collective-permute-start.28 = (bf16[8,48,640]{2,1,0:T(8,128)(2,1)S(1)}, bf16[8,48,640]{2,1,0:T(8,128)(2,1)S(1)}, u32[]{:S(2)}, u32[]{:S(2)}) collective-permute-start(bf16[8,48,640]{2,1,0:T(8,128)(2,1)S(1)} %copy-done.40), channel_id=1, source_target_pairs={{0,2},{1,3},{2,0},{3,1},{4,6},{5,7},{6,4},{7,5},{8,10},{9,11},{10,... | collective-permute-start | bytes 1474568 | tf_op jit(solution)/shard_map/ppermute | solution.py:861
  228.1 12.8 %collective-permute-start.29 = (bf16[2,4,48,640]{3,2,1,0:T(8,128)(2,1)S(1)}, bf16[2,4,48,640]{3,2,1,0:T(8,128)(2,1)S(1)}, u32[]{:S(2)}, u32[]{:S(2)}) collective-permute-start(bf16[2,4,48,640]{3,2,1,0:T(8,128)(2,1)S(1)} %copy-done.39), channel_id=1, source_target_pairs={{0,4},{4,0},{8,12},{12,8},{16,20},{20,16},{24,28},{28,24},{1,5},{5... | collective-permute-start | bytes 1474568 | tf_op jit(solution)/shard_map/ppermute | solution.py:861
  234.5 20.7 %collective-permute-start.37 = (bf16[2,96,1792]{2,1,0:T(8,128)(2,1)}, bf16[2,96,1792]{2,1,0:T(8,128)(2,1)S(1)}, u32[]{:S(2)}, u32[]{:S(2)}) collective-permute-start(bf16[2,96,1792]{2,1,0:T(8,128)(2,1)} %get-tuple-element.241), channel_id=1, source_target_pairs={{0,8},{4,12},{8,0},{12,4},{16,24},{20,28},{24,16},{28,20},{1,9},{5... | collective-permute-start | bytes 2064392 | tf_op jit(solution)/shard_map/ppermute | solution.py:861
  255.4 16.9 %collective-permute-start.39 = (bf16[96,1792]{1,0:T(8,128)(2,1)S(1)}, bf16[96,1792]{1,0:T(8,128)(2,1)S(1)}, u32[]{:S(2)}, u32[]{:S(2)}) collective-permute-start(bf16[96,1792]{1,0:T(8,128)(2,1)S(1)} %fusion.3), channel_id=1, source_target_pairs={{0,16},{4,20},{8,24},{12,28},{16,0},{20,4},{24,8},{28,12},{1,17},{... | collective-permute-start | bytes 1032200 | tf_op jit(solution)/shard_map/ppermute | solution.py:861
  258.9 10.6 %collective-permute-start.38 = (bf16[2,96,640]{2,1,0:T(8,128)(2,1)S(1)}, bf16[2,96,640]{2,1,0:T(8,128)(2,1)S(1)}, u32[]{:S(2)}, u32[]{:S(2)}) collective-permute-start(bf16[2,96,640]{2,1,0:T(8,128)(2,1)S(1)} %copy-done.41), channel_id=1, source_target_pairs={{0,8},{4,12},{8,0},{12,4},{16,24},{20,28},{24,16},{28,20},{1,9},{5... | collective-permute-start | bytes 737288 | tf_op jit(solution)/shard_map/ppermute | solution.py:861
  (67 other events, 444.6 us)

commit v6 on v5

--- a/solution.py
+++ b/solution.py
@@ -914,10 +914,10 @@
     wide = sum(keep.shape[3] for keep in keeps)
     views = []
     for keep, got in zip(keeps, gots):
-        block = (1, 2, half, keep.shape[3])
+        block = (1, 4, half, keep.shape[3])
         for array in (keep, got):
             views.append((array, block, lambda j: (1, j, 0, 0)))
-            views.append((array, block, lambda j: (j // 2, 2 + j % 2, 1, 0)))
+            views.append((array, block, lambda j: (j, 1, 1, 0)))
 
     def body(*refs):
         ins, (upper, lower) = refs[:-2], refs[-2:]
@@ -930,10 +930,10 @@
             lower[0, :, :, at] = total_of((keep_l[0], got_l[0])).astype(LOW)
 
     outs = [
-        ((8, half, wide), LOW, (2, half, wide), lambda j: (j, 0, 0)),
-        ((2, 4, half, wide), LOW, (1, 2, half, wide), lambda j: (j // 2, j % 2, 0, 0)),
+        ((8, half, wide), LOW, (4, half, wide), lambda j: (j, 0, 0)),
+        ((2, 4, half, wide), LOW, (1, 4, half, wide), lambda j: (j, 0, 0, 0)),
     ]
-    return sum_call(body, 4, views, outs, 8e6)
+    return sum_call(body, 2, views, outs, 8e6)
 
 
 def sum_here(keeps, gots, upper_got, lower_got):
@@ -1193,12 +1193,9 @@
         came = (z_near(small), z_far(small), swap(small, "dp", 6))
         here = here + got.astype(FULL)
         got = z_far(here[1].astype(LOW))
-        small = (small + came[0]) + (came[1] + came[2])
         sum_mlp = line[0] + line_got.astype(FULL)
         sum_att = here[0] + got.astype(FULL)
         sum_mlp, sum_out = sum_mlp[:, : 2 * units], sum_mlp[:, 2 * units :]
-        reduced_norms = small[:count, :width]
-        reduced_heads = small[count:]
     else:
         reduced_norms = lax.psum(norms, ("dp", "mp"))
         reduced_heads = lax.psum_scatter(
@@ -1229,6 +1226,11 @@
         RATE_MATRIX,
         DECAY_MATRIX,
     )
+    if near:
+        came = [after(one, attention_new) for one in came]
+        small = (small + came[0]) + (came[1] + came[2])
+        reduced_norms = small[:count, :width]
+        reduced_heads = small[count:]
     mlp_second_new, mlp_new = adam(
         mlp_weights, mlp_first, mlp_second, reduced_mlp, RATE_MATRIX, DECAY_MATRIX
     )

time: 288 us -> 287 us (level)
    unnamed x92 -> x90, local copies, waits for them, and re-layouts: 6.55 us -> 6.55 us
where the time goes in v6:
time: 287 us; the launch traced here: 286 us
  Pallas kernels  142 us (49%)
  waiting for transfers between devices  82.9 us (29%)
  starting transfers between devices  44.5 us (16%)
  local copies, waits for them, and re-layouts  7.78 us (3%)
  other arithmetic  7.13 us (2%)
    ppermute x44, waiting for transfers between devices, swap(): lax.ppermute(values, axis, [(index, index ^ bit) for index in range(count)])  82.9 us
    ppermute x44, starting transfers between devices, swap(): lax.ppermute(values, axis, [(index, index ^ bit) for index in range(count)])  44.5 us
    pallas_call x1, Pallas kernels, feed(): pl.pallas_call(functools.partial(feed_body, blocks, layout), grid=(LANES,...  35.5 us
    pallas_call x6, Pallas kernels, sum_call(): pl.pallas_call(body, grid=(grid,), in_specs=[pl.BlockSpec(block, index) f...  20.1 us
    pallas_call x1, Pallas kernels, attend(): pl.pallas_call(functools.partial(attend_body, table, images), grid=(LANES...  15.7 us
    pallas_call x1, Pallas kernels, back(): pl.pallas_call(functools.partial(back_body, table, columns, images), grid...  15 us
    pallas_call x1, Pallas kernels, second_back(): pl.pallas_call(second_body, grid=(images,), in_specs=[pl.BlockSpec(memory...  12.2 us
    pallas_call x1, Pallas kernels, input_back(): pl.pallas_call(functools.partial(input_body, table), grid=(images // TWO,...  12 us
  transfers between devices with their start and end apart: 44, of which 25 were waited for; matrix products, arithmetic and copies ran while one was open for 2% of the time, Pallas kernels for 36%

profile of v6, /device:TPU:0, one launch (start us, length us, event | category | flops | bytes accessed | tf_op | source)
XLA Modules:
  0.0 286.2 jit_solution(9764141218806332978)
XLA Ops:
  1.9 3.0 %collective-permute-start.1 = (f32[3,857]{1,0:T(4,128)S(1)}, f32[3,857]{1,0:T(4,128)S(1)}, u32[]{:S(2)}, u32[]{:S(2)}) collective-permute-start(f32[3,857]{1,0:T(4,128)S(1)} %copy-done.28), channel_id=1, source_target_pairs={{0,2},{1,3},{2,0},{3,1},{4,6},{5,7},{6,4},{7,5},{8,10},{9,11},{10,... | collective-permute-start | bytes 30860 | tf_op jit(solution)/shard_map/ppermute | solution.py:861
  7.5 5.0 %shard_map.272 = (bf16[832,768]{1,0:T(8,128)(2,1)}, bf16[832,768]{1,0:T(8,128)(2,1)}) custom-call(f32[784,768]{1,0:T(8,128)} %x_ref.5, f32[784,768]{1,0:T(8,128)} %cot_ref.3, f32[12,768]{1,0:T(8,128)} %vec_ref.7), custom_call_target="tpu_custom_call" | custom-call | flops 3000000000 | bytes 4000000 | tf_op jit(solution)/shard_map/pallas_call | solution.py:147
  17.6 6.8 %collective-permute-done.3 = bf16[2,96,896]{2,1,0:T(8,128)(2,1)S(1)} collective-permute-done((bf16[2,96,896]{2,1,0:T(8,128)(2,1)S(1)}, bf16[2,96,896]{2,1,0:T(8,128)(2,1)S(1)}, u32[]{:S(2)}, u32[]{:S(2)}) %collective-permute-start.3) | collective-permute-done | bytes 344096 | tf_op jit(solution)/shard_map/ppermute | solution.py:861
  26.7 3.4 %collective-permute-start.2 = (bf16[1,96,1536]{2,1,0:T(8,128)(2,1)S(1)}, bf16[1,96,1536]{2,1,0:T(8,128)(2,1)S(1)}, u32[]{:S(2)}, u32[]{:S(2)}) collective-permute-start(bf16[1,96,1536]{2,1,0:T(8,128)(2,1)S(1)} %maximum_bitcast_fusion), channel_id=1, source_target_pairs={{0,16},{4,20},{8,24},{12,28},{16,0},{20,4},{24,8},{28,12},{1,17},{... | collective-permute-start | bytes 884744 | tf_op jit(solution)/shard_map/ppermute | solution.py:861
  35.8 6.8 %collective-permute-done.2 = bf16[1,96,1536]{2,1,0:T(8,128)(2,1)S(1)} collective-permute-done((bf16[1,96,1536]{2,1,0:T(8,128)(2,1)S(1)}, bf16[1,96,1536]{2,1,0:T(8,128)(2,1)S(1)}, u32[]{:S(2)}, u32[]{:S(2)}) %collective-permute-start.2) | collective-permute-done | bytes 294944 | tf_op jit(solution)/shard_map/ppermute | solution.py:861
  44.6 5.3 %shard_map.273 = (f32[12,208,208]{2,1,0:T(8,128)}, f32[4,1,640]{2,1,0:T(1,128)}) custom-call(f32[3,857]{1,0:T(4,128)} %t0.1, f32[3,857]{1,0:T(4,128)} %copy-done.42, f32[3,857]{1,0:T(4,128)} %copy-done.41, f32[3,857]{1,0:T(4,128)} %copy-done.43, bf16[768,384]{1,0:T(8,128)(2,1)} %constant.32.clone.thin_ref), custom_call_target="tpu_custom_call" | custom-call | flops 3000000000 | bytes 4000000 | tf_op jit(solution)/shard_map/pallas_call | solution.py:211
  50.0 7.0 %collective-permute-done.10 = bf16[2,96,1536]{2,1,0:T(8,128)(2,1)S(1)} collective-permute-done((bf16[2,96,1536]{2,1,0:T(8,128)(2,1)S(1)}, bf16[2,96,1536]{2,1,0:T(8,128)(2,1)S(1)}, u32[]{:S(2)}, u32[]{:S(2)}) %collective-permute-start.10) | collective-permute-done | bytes 589856 | tf_op jit(solution)/shard_map/ppermute | solution.py:861
  60.7 15.7 %shard_map.274 = (bf16[4,832,640]{2,1,0:T(8,128)(2,1)}, bf16[4,12,208,208]{3,2,1,0:T(8,128)(2,1)}, bf16[832,1024]{1,0:T(8,128)(2,1)}) custom-call(s32[3]{0:T(128)} %pad_add_fusion.me_ref, s32[16,2]{1,0:T(8,128)} %copy.31.size_ref, s32[2,208,128]{2,1,0:T(8,128)} %constant.33.clone.grid_ref, bf16[832,768]{1,0:T(8,128)(2,1)} %get-tuple-element.167.n_ref, ...), custom_call_target="tpu_custom_call" | custom-call | flops 15000000512 | bytes 20000000 | tf_op jit(solution)/shard_map/pallas_call | solution.py:322
  79.0 7.4 %shard_map.275 = (bf16[832,768]{1,0:T(8,128)(2,1)}, f32[832,768]{1,0:T(8,128)}, bf16[832,768]{1,0:T(8,128)(2,1)}) custom-call(s32[3]{0:T(128)} %pad_add_fusion.me_ref, bf16[832,1024]{1,0:T(8,128)(2,1)} %get-tuple-element.179.ctx_ref, f32[784,768]{1,0:T(8,128)} %x_ref.5, f32[12,768]{1,0:T(8,128)} %vec_ref.7, bf16[8,48,896]{2,1,0:T(8,128)(2,1)} %copy-done.16, ...), custom_call_target="tpu_custom_call" | custom-call | flops 8000000000 | bytes 15000000 | tf_op jit(solution)/shard_map/pallas_call | solution.py:383
  86.5 18.7 %collective-permute-done.17.refs_1_ = bf16[8,48,1536]{2,1,0:T(8,128)(2,1)} collective-permute-done((bf16[8,48,1536]{2,1,0:T(8,128)(2,1)S(1)}, bf16[8,48,1536]{2,1,0:T(8,128)(2,1)}, u32[]{:S(2)}, u32[]{:S(2)}) %collective-permute-start.17) | collective-permute-done | bytes 1179680 | tf_op jit(solution)/shard_map/ppermute | solution.py:861
  112.4 35.5 %shard_map.276 = (f32[832,768]{1,0:T(8,128)}, f32[832,768]{1,0:T(8,128)}, bf16[2,8,96,1536]{3,2,1,0:T(8,128)(2,1)}, bf16[2,8,96,1536]{3,2,1,0:T(8,128)(2,1)}, f32[4,1,768]{2,1,0:T(1,128)}) custom-call(s32[3]{0:T(128)} %pad_add_fusion.me_ref, bf16[832,768]{1,0:T(8,128)(2,1)} %get-tuple-element.183.n_ref, bf16[832,768]{1,0:T(8,128)(2,1)} %get-tuple-element.184.gd_ref, ...), custom_call_target="tpu_custom_call" | custom-call | flops 35000000512 | bytes 40000000 | tf_op jit(solution)/shard_map/pallas_call | solution.py:508
  148.1 12.2 %shard_map.277 = (f32[784,768]{1,0:T(8,128)}, f32[832,768]{1,0:T(8,128)}, bf16[832,768]{1,0:T(8,128)(2,1)}, bf16[2,8,96,256]{3,2,1,0:T(8,128)(2,1)}, bf16[2,8,96,256]{3,2,1,0:T(8,128)(2,1)}, /*index=5*/f32[6,768]{1,0:T(8,128)}) custom-call(s32[3]{0:T(128)} %pad_add_fusion.me_ref, f32[832,768]{1,0:T(8,128)} %get-tuple-element.191.down_ref, ...), custom_call_target="tpu_custom_call" | custom-call | flops 10000000000 | bytes 20000000 | tf_op jit(solution)/shard_map/pallas_call | solution.py:600
  163.9 3.9 %shard_map.278 = (bf16[8,48,1792]{2,1,0:T(8,128)(2,1)}, bf16[2,4,48,1792]{3,2,1,0:T(8,128)(2,1)}) custom-call(bf16[2,8,96,1536]{3,2,1,0:T(8,128)(2,1)} %get-tuple-element.196.refs_0_.refs_1_.refs_4_.refs_5_.refs_6_.refs_7_, bf16[2,8,96,1536]{3,2,1,0:T(8,128)(2,1)} %get-tuple-element.196.refs_0_.refs_1_.refs_4_.refs_5_.refs_6_.refs_7_, ...), custom_call_target="tpu_custom_call" | custom-call | flops 1000000 | bytes 8000000 | tf_op jit(solution)/shard_map/pallas_call | solution.py:901
  169.9 15.0 %shard_map.279 = (bf16[4,832,640]{2,1,0:T(8,128)(2,1)}, f32[12,208,208]{2,1,0:T(8,128)}, f32[4,8,384]{2,1,0:T(8,128)}) custom-call(s32[3]{0:T(128)} %pad_add_fusion.me_ref, bf16[832,768]{1,0:T(8,128)(2,1)} %get-tuple-element.206.ga_ref, bf16[4,832,640]{2,1,0:T(8,128)(2,1)} %get-tuple-element.207.qkv_ref, ...), custom_call_target="tpu_custom_call" | custom-call | flops 30000001024 | bytes 40000000 | tf_op jit(solution)/shard_map/pallas_call | solution.py:713
  184.9 8.8 %shard_map.280 = (bf16[2,8,96,640]{3,2,1,0:T(8,128)(2,1)}, bf16[2,8,96,640]{3,2,1,0:T(8,128)(2,1)}) custom-call(s32[3]{0:T(128)} %pad_add_fusion.me_ref, bf16[832,768]{1,0:T(8,128)(2,1)} %get-tuple-element.167.n_ref, bf16[4,832,640]{2,1,0:T(8,128)(2,1)} %get-tuple-element.226.dqkv_ref), custom_call_target="tpu_custom_call" | custom-call | flops 8000000000 | bytes 10000000 | tf_op jit(solution)/shard_map/pallas_call | solution.py:795
  193.7 5.4 %shard_map.281 = f32[4,3,857]{2,1,0:T(4,128)} custom-call(f32[12,208,208]{2,1,0:T(8,128)} %get-tuple-element.215.pair_ref, f32[4,8,384]{2,1,0:T(8,128)} %get-tuple-element.216.cols_ref, bf16[768,384]{1,0:T(8,128)(2,1)} %constant.32.clone.thin_ref), custom_call_target="tpu_custom_call" | custom-call | flops 3000000000 | bytes 4000000 | tf_op jit(solution)/shard_map/pallas_call | solution.py:774
  202.1 5.2 %shard_map.282 = (f32[4,48,1792]{2,1,0:T(8,128)}, bf16[4,48,1792]{2,1,0:T(8,128)(2,1)}, f32[4,48,1792]{2,1,0:T(8,128)}, bf16[4,48,1792]{2,1,0:T(8,128)(2,1)}) custom-call(bf16[8,48,1792]{2,1,0:T(8,128)(2,1)} %copy-done.2, bf16[8,48,1792]{2,1,0:T(8,128)(2,1)} %copy-done.2, bf16[2,4,48,1792]{3,2,1,0:T(8,128)(2,1)} %copy-done.3, ...), custom_call_target="tpu_custom_call" | custom-call | flops 1000000 | bytes 12000000 | tf_op jit(solution)/shard_map/pallas_call | solution.py:901
  212.0 12.0 %shard_map.284 = (f32[784,768]{1,0:T(8,128)}, f32[2,768]{1,0:T(2,128)}) custom-call(s32[3]{0:T(128)} %pad_add_fusion.me_ref, bf16[4,832,640]{2,1,0:T(8,128)(2,1)} %get-tuple-element.226.dqkv_ref, f32[832,768]{1,0:T(8,128)} %get-tuple-element.227.gm_ref, f32[784,768]{1,0:T(8,128)} %x_ref.5, f32[12,768]{1,0:T(8,128)} %vec_ref.7, ...), custom_call_target="tpu_custom_call" | custom-call | flops 15000000512 | bytes 15000000 | tf_op jit(solution)/shard_map/pallas_call | solution.py:834
  229.3 3.3 %shard_map.285 = (f32[2,96,1792]{2,1,0:T(8,128)}, bf16[2,96,1792]{2,1,0:T(8,128)(2,1)}) custom-call(f32[4,48,1792]{2,1,0:T(8,128)} %get-tuple-element.231.refs_0_.refs_1_, f32[4,48,1792]{2,1,0:T(8,128)} %get-tuple-element.231.refs_0_.refs_1_, bf16[4,48,1792]{2,1,0:T(8,128)(2,1)} %copy-done.4, bf16[4,48,1792]{2,1,0:T(8,128)(2,1)} %copy-done.4, ...), custom_call_target="tpu_custom_call" | custom-call | flops 1000000 | bytes 6000000 | tf_op jit(solution)/shard_map/pallas_call | solution.py:901
  245.8 4.4 %collective-permute-done.34.refs_2_.refs_3_ = bf16[4,48,640]{2,1,0:T(8,128)(2,1)S(1)} collective-permute-done((bf16[4,48,640]{2,1,0:T(8,128)(2,1)}, bf16[4,48,640]{2,1,0:T(8,128)(2,1)S(1)}, u32[]{:S(2)}, u32[]{:S(2)}) %collective-permute-start.34) | collective-permute-done | bytes 245792 | tf_op jit(solution)/shard_map/ppermute | solution.py:861
  253.4 3.5 %collective-permute-start.39 = (bf16[96,1792]{1,0:T(8,128)(2,1)S(1)}, bf16[96,1792]{1,0:T(8,128)(2,1)S(1)}, u32[]{:S(2)}, u32[]{:S(2)}) collective-permute-start(bf16[96,1792]{1,0:T(8,128)(2,1)S(1)} %fusion.3), channel_id=1, source_target_pairs={{0,16},{4,20},{8,24},{12,28},{16,0},{20,4},{24,8},{28,12},{1,17},{... | collective-permute-start | bytes 1032200 | tf_op jit(solution)/shard_map/ppermute | solution.py:861
  258.4 9.0 %collective-permute-done.38 = bf16[2,96,640]{2,1,0:T(8,128)(2,1)S(1)} collective-permute-done((bf16[2,96,640]{2,1,0:T(8,128)(2,1)S(1)}, bf16[2,96,640]{2,1,0:T(8,128)(2,1)S(1)}, u32[]{:S(2)}, u32[]{:S(2)}) %collective-permute-start.38) | collective-permute-done | bytes 245792 | tf_op jit(solution)/shard_map/ppermute | solution.py:861
  270.3 3.4 %collective-permute-start.43 = (f32[15,857]{1,0:T(8,128)S(1)}, f32[15,857]{1,0:T(8,128)S(1)}, u32[]{:S(2)}, u32[]{:S(2)}) collective-permute-start(f32[15,857]{1,0:T(8,128)S(1)} %add.82), channel_id=1, source_target_pairs={{0,24},{4,28},{8,16},{12,20},{16,8},{20,12},{24,0},{28,4},{1,25},{... | collective-permute-start | bytes 154268 | tf_op jit(solution)/shard_map/ppermute | solution.py:861
  278.4 5.1 %collective-permute-done.40 = bf16[96,640]{1,0:T(8,128)(2,1)S(1)} collective-permute-done((bf16[96,640]{1,0:T(8,128)(2,1)S(1)}, bf16[96,640]{1,0:T(8,128)(2,1)S(1)}, u32[]{:S(2)}, u32[]{:S(2)}) %collective-permute-start.40) | collective-permute-done | bytes 122912 | tf_op jit(solution)/shard_map/ppermute | solution.py:861
  (222 shorter events, 78.8 us)
Async XLA Ops:
  1.9 10.6 %collective-permute-start.1 = (f32[3,857]{1,0:T(4,128)S(1)}, f32[3,857]{1,0:T(4,128)S(1)}, u32[]{:S(2)}, u32[]{:S(2)}) collective-permute-start(f32[3,857]{1,0:T(4,128)S(1)} %copy-done.28), channel_id=1, source_target_pairs={{0,2},{1,3},{2,0},{3,1},{4,6},{5,7},{6,4},{7,5},{8,10},{9,11},{10,... | collective-permute-start | bytes 30860 | tf_op jit(solution)/shard_map/ppermute | solution.py:861
  26.7 15.9 %collective-permute-start.2 = (bf16[1,96,1536]{2,1,0:T(8,128)(2,1)S(1)}, bf16[1,96,1536]{2,1,0:T(8,128)(2,1)S(1)}, u32[]{:S(2)}, u32[]{:S(2)}) collective-permute-start(bf16[1,96,1536]{2,1,0:T(8,128)(2,1)S(1)} %maximum_bitcast_fusion), channel_id=1, source_target_pairs={{0,16},{4,20},{8,24},{12,28},{16,0},{20,4},{24,8},{28,12},{1,17},{... | collective-permute-start | bytes 884744 | tf_op jit(solution)/shard_map/ppermute | solution.py:861
  34.4 15.6 %collective-permute-start.11 = (bf16[8,48,896]{2,1,0:T(8,128)(2,1)S(1)}, bf16[8,48,896]{2,1,0:T(8,128)(2,1)}, u32[]{:S(2)}, u32[]{:S(2)}) collective-permute-start(bf16[8,48,896]{2,1,0:T(8,128)(2,1)S(1)} %get-tuple-element.153.refs_0_), channel_id=1, source_target_pairs={{0,1},{1,0},{2,3},{3,2},{4,5},{5,4},{6,7},{7,6},{8,9},{9,8},{10,11... | collective-permute-start | bytes 2064392 | tf_op jit(solution)/shard_map/ppermute | solution.py:861
  34.5 22.5 %collective-permute-start.8 = (bf16[8,48,896]{2,1,0:T(8,128)(2,1)S(1)}, bf16[8,48,896]{2,1,0:T(8,128)(2,1)}, u32[]{:S(2)}, u32[]{:S(2)}) collective-permute-start(bf16[8,48,896]{2,1,0:T(8,128)(2,1)S(1)} %get-tuple-element.153.refs_0_), channel_id=1, source_target_pairs={{0,2},{1,3},{2,0},{3,1},{4,6},{5,7},{6,4},{7,5},{8,10},{9,11},{10,... | collective-permute-start | bytes 2064392 | tf_op jit(solution)/shard_map/ppermute | solution.py:861
  35.1 14.9 %collective-permute-start.12 = (bf16[8,48,896]{2,1,0:T(8,128)(2,1)S(1)}, bf16[8,48,896]{2,1,0:T(8,128)(2,1)}, u32[]{:S(2)}, u32[]{:S(2)}) collective-permute-start(bf16[8,48,896]{2,1,0:T(8,128)(2,1)S(1)} %get-tuple-element.154.refs_2_), channel_id=1, source_target_pairs={{0,1},{1,0},{2,3},{3,2},{4,5},{5,4},{6,7},{7,6},{8,9},{9,8},{10,11... | collective-permute-start | bytes 2064392 | tf_op jit(solution)/shard_map/ppermute | solution.py:861
  35.3 21.8 %collective-permute-start.9 = (bf16[8,48,896]{2,1,0:T(8,128)(2,1)S(1)}, bf16[8,48,896]{2,1,0:T(8,128)(2,1)}, u32[]{:S(2)}, u32[]{:S(2)}) collective-permute-start(bf16[8,48,896]{2,1,0:T(8,128)(2,1)S(1)} %get-tuple-element.154.refs_2_), channel_id=1, source_target_pairs={{0,4},{4,0},{8,12},{12,8},{16,20},{20,16},{24,28},{28,24},{1,5},{5... | collective-permute-start | bytes 2064392 | tf_op jit(solution)/shard_map/ppermute | solution.py:861
  42.6 14.4 %collective-permute-start.10 = (bf16[2,96,1536]{2,1,0:T(8,128)(2,1)S(1)}, bf16[2,96,1536]{2,1,0:T(8,128)(2,1)S(1)}, u32[]{:S(2)}, u32[]{:S(2)}) collective-permute-start(bf16[2,96,1536]{2,1,0:T(8,128)(2,1)S(1)} %pad_maximum_fusion.6), channel_id=1, source_target_pairs={{0,8},{4,12},{8,0},{12,4},{16,24},{20,28},{24,16},{28,20},{1,9},{5... | collective-permute-start | bytes 1769480 | tf_op jit(solution)/shard_map/ppermute | solution.py:861
  57.7 18.6 %collective-permute-start.15 = (bf16[4,48,1536]{2,1,0:T(8,128)(2,1)S(1)}, bf16[4,48,1536]{2,1,0:T(8,128)(2,1)S(1)}, u32[]{:S(2)}, u32[]{:S(2)}) collective-permute-start(bf16[4,48,1536]{2,1,0:T(8,128)(2,1)S(1)} %get-tuple-element.166), channel_id=1, source_target_pairs={{0,4},{4,0},{8,12},{12,8},{16,20},{20,16},{24,28},{28,24},{1,5},{5... | collective-permute-start | bytes 1769480 | tf_op jit(solution)/shard_map/ppermute | solution.py:861
  58.3 18.0 %collective-permute-start.16 = (bf16[4,48,1536]{2,1,0:T(8,128)(2,1)S(1)}, bf16[4,48,1536]{2,1,0:T(8,128)(2,1)S(1)}, u32[]{:S(2)}, u32[]{:S(2)}) collective-permute-start(bf16[4,48,1536]{2,1,0:T(8,128)(2,1)S(1)} %get-tuple-element.175), channel_id=1, source_target_pairs={{0,2},{1,3},{2,0},{3,1},{4,6},{5,7},{6,4},{7,5},{8,10},{9,11},{10,... | collective-permute-start | bytes 1769480 | tf_op jit(solution)/shard_map/ppermute | solution.py:861
  76.7 28.5 %collective-permute-start.17 = (bf16[8,48,1536]{2,1,0:T(8,128)(2,1)S(1)}, bf16[8,48,1536]{2,1,0:T(8,128)(2,1)}, u32[]{:S(2)}, u32[]{:S(2)}) collective-permute-start(bf16[8,48,1536]{2,1,0:T(8,128)(2,1)S(1)} %pad_maximum_fusion.1.refs_0_), channel_id=1, source_target_pairs={{0,2},{1,3},{2,0},{3,1},{4,6},{5,7},{6,4},{7,5},{8,10},{9,11},{10,... | collective-permute-start | bytes 3538952 | tf_op jit(solution)/shard_map/ppermute | solution.py:861
  78.2 27.0 %collective-permute-start.20 = (bf16[8,48,1536]{2,1,0:T(8,128)(2,1)S(1)}, bf16[8,48,1536]{2,1,0:T(8,128)(2,1)}, u32[]{:S(2)}, u32[]{:S(2)}) collective-permute-start(bf16[8,48,1536]{2,1,0:T(8,128)(2,1)S(1)} %pad_maximum_fusion.2.refs_2_), channel_id=1, source_target_pairs={{0,1},{1,0},{2,3},{3,2},{4,5},{5,4},{6,7},{7,6},{8,9},{9,8},{10,11... | collective-permute-start | bytes 3538952 | tf_op jit(solution)/shard_map/ppermute | solution.py:861
  78.3 28.4 %collective-permute-start.18 = (bf16[8,48,1536]{2,1,0:T(8,128)(2,1)S(1)}, bf16[8,48,1536]{2,1,0:T(8,128)(2,1)}, u32[]{:S(2)}, u32[]{:S(2)}) collective-permute-start(bf16[8,48,1536]{2,1,0:T(8,128)(2,1)S(1)} %pad_maximum_fusion.2.refs_2_), channel_id=1, source_target_pairs={{0,4},{4,0},{8,12},{12,8},{16,20},{20,16},{24,28},{28,24},{1,5},{5... | collective-permute-start | bytes 3538952 | tf_op jit(solution)/shard_map/ppermute | solution.py:861
  147.9 12.4 %collective-permute-start.23 = (bf16[2,8,96,1536]{3,2,1,0:T(8,128)(2,1)}, bf16[2,8,96,1536]{3,2,1,0:T(8,128)(2,1)}, u32[]{:S(2)}, u32[]{:S(2)}) collective-permute-start(bf16[2,8,96,1536]{3,2,1,0:T(8,128)(2,1)} %get-tuple-element.197), channel_id=1, source_target_pairs={{0,1},{1,0},{2,3},{3,2},{4,5},{5,4},{6,7},{7,6},{8,9},{9,8},{10,11... | collective-permute-start | bytes 14155784 | tf_op jit(solution)/shard_map/ppermute | solution.py:861
  167.8 32.7 %collective-permute-start.25 = (bf16[8,48,1792]{2,1,0:T(8,128)(2,1)}, bf16[8,48,1792]{2,1,0:T(8,128)(2,1)S(1)}, u32[]{:S(2)}, u32[]{:S(2)}) collective-permute-start(bf16[8,48,1792]{2,1,0:T(8,128)(2,1)} %get-tuple-element.212), channel_id=1, source_target_pairs={{0,2},{1,3},{2,0},{3,1},{4,6},{5,7},{6,4},{7,5},{8,10},{9,11},{10,... | collective-permute-start | bytes 4128776 | tf_op jit(solution)/shard_map/ppermute | solution.py:861
  168.4 32.4 %collective-permute-start.26 = (bf16[2,4,48,1792]{3,2,1,0:T(8,128)(2,1)}, bf16[2,4,48,1792]{3,2,1,0:T(8,128)(2,1)S(1)}, u32[]{:S(2)}, u32[]{:S(2)}) collective-permute-start(bf16[2,4,48,1792]{3,2,1,0:T(8,128)(2,1)} %get-tuple-element.213), channel_id=1, source_target_pairs={{0,4},{4,0},{8,12},{12,8},{16,20},{20,16},{24,28},{28,24},{1,5},{5... | collective-permute-start | bytes 4128776 | tf_op jit(solution)/shard_map/ppermute | solution.py:861
  207.3 20.8 %collective-permute-start.30 = (bf16[4,48,1792]{2,1,0:T(8,128)(2,1)}, bf16[4,48,1792]{2,1,0:T(8,128)(2,1)S(1)}, u32[]{:S(2)}, u32[]{:S(2)}) collective-permute-start(bf16[4,48,1792]{2,1,0:T(8,128)(2,1)} %get-tuple-element.232), channel_id=1, source_target_pairs={{0,4},{4,0},{8,12},{12,8},{16,20},{20,16},{24,28},{28,24},{1,5},{5... | collective-permute-start | bytes 2064392 | tf_op jit(solution)/shard_map/ppermute | solution.py:861
  208.8 19.4 %collective-permute-start.31 = (bf16[4,48,1792]{2,1,0:T(8,128)(2,1)}, bf16[4,48,1792]{2,1,0:T(8,128)(2,1)S(1)}, u32[]{:S(2)}, u32[]{:S(2)}) collective-permute-start(bf16[4,48,1792]{2,1,0:T(8,128)(2,1)} %get-tuple-element.233), channel_id=1, source_target_pairs={{0,2},{1,3},{2,0},{3,1},{4,6},{5,7},{6,4},{7,5},{8,10},{9,11},{10,... | collective-permute-start | bytes 2064392 | tf_op jit(solution)/shard_map/ppermute | solution.py:861
  224.8 13.7 %collective-permute-start.28 = (bf16[8,48,640]{2,1,0:T(8,128)(2,1)S(1)}, bf16[8,48,640]{2,1,0:T(8,128)(2,1)S(1)}, u32[]{:S(2)}, u32[]{:S(2)}) collective-permute-start(bf16[8,48,640]{2,1,0:T(8,128)(2,1)S(1)} %copy-done.39), channel_id=1, source_target_pairs={{0,2},{1,3},{2,0},{3,1},{4,6},{5,7},{6,4},{7,5},{8,10},{9,11},{10,... | collective-permute-start | bytes 1474568 | tf_op jit(solution)/shard_map/ppermute | solution.py:861
  226.2 12.8 %collective-permute-start.29 = (bf16[2,4,48,640]{3,2,1,0:T(8,128)(2,1)S(1)}, bf16[2,4,48,640]{3,2,1,0:T(8,128)(2,1)S(1)}, u32[]{:S(2)}, u32[]{:S(2)}) collective-permute-start(bf16[2,4,48,640]{3,2,1,0:T(8,128)(2,1)S(1)} %copy-done.38), channel_id=1, source_target_pairs={{0,4},{4,0},{8,12},{12,8},{16,20},{20,16},{24,28},{28,24},{1,5},{5... | collective-permute-start | bytes 1474568 | tf_op jit(solution)/shard_map/ppermute | solution.py:861
  232.6 20.7 %collective-permute-start.37 = (bf16[2,96,1792]{2,1,0:T(8,128)(2,1)}, bf16[2,96,1792]{2,1,0:T(8,128)(2,1)S(1)}, u32[]{:S(2)}, u32[]{:S(2)}) collective-permute-start(bf16[2,96,1792]{2,1,0:T(8,128)(2,1)} %get-tuple-element.244), channel_id=1, source_target_pairs={{0,8},{4,12},{8,0},{12,4},{16,24},{20,28},{24,16},{28,20},{1,9},{5... | collective-permute-start | bytes 2064392 | tf_op jit(solution)/shard_map/ppermute | solution.py:861
  253.4 16.9 %collective-permute-start.39 = (bf16[96,1792]{1,0:T(8,128)(2,1)S(1)}, bf16[96,1792]{1,0:T(8,128)(2,1)S(1)}, u32[]{:S(2)}, u32[]{:S(2)}) collective-permute-start(bf16[96,1792]{1,0:T(8,128)(2,1)S(1)} %fusion.3), channel_id=1, source_target_pairs={{0,16},{4,20},{8,24},{12,28},{16,0},{20,4},{24,8},{28,12},{1,17},{... | collective-permute-start | bytes 1032200 | tf_op jit(solution)/shard_map/ppermute | solution.py:861
  270.3 14.5 %collective-permute-start.43 = (f32[15,857]{1,0:T(8,128)S(1)}, f32[15,857]{1,0:T(8,128)S(1)}, u32[]{:S(2)}, u32[]{:S(2)}) collective-permute-start(f32[15,857]{1,0:T(8,128)S(1)} %add.82), channel_id=1, source_target_pairs={{0,24},{4,28},{8,16},{12,20},{16,8},{20,12},{24,0},{28,4},{1,25},{... | collective-permute-start | bytes 154268 | tf_op jit(solution)/shard_map/ppermute | solution.py:861
  273.7 11.1 %collective-permute-start.42 = (f32[15,857]{1,0:T(8,128)S(1)}, f32[15,857]{1,0:T(8,128)S(1)}, u32[]{:S(2)}, u32[]{:S(2)}) collective-permute-start(f32[15,857]{1,0:T(8,128)S(1)} %add.82), channel_id=1, source_target_pairs={{0,16},{4,20},{8,24},{12,28},{16,0},{20,4},{24,8},{28,12},{1,17},{... | collective-permute-start | bytes 154268 | tf_op jit(solution)/shard_map/ppermute | solution.py:861
  273.7 11.1 %collective-permute-start.41 = (f32[15,857]{1,0:T(8,128)S(1)}, f32[15,857]{1,0:T(8,128)S(1)}, u32[]{:S(2)}, u32[]{:S(2)}) collective-permute-start(f32[15,857]{1,0:T(8,128)S(1)} %add.82), channel_id=1, source_target_pairs={{0,8},{4,12},{8,0},{12,4},{16,24},{20,28},{24,16},{28,20},{1,9},{5... | collective-permute-start | bytes 154268 | tf_op jit(solution)/shard_map/ppermute | solution.py:861
  (65 other events, 406.1 us)
